TPU v7x, 32 devices: a whole 2x2x4 slice. The times are simulated.
32 devices in a mesh: cuts: 16 (over z, y, core), coil: 2 (over x).
Axes of the slice: x: 2, y: 2, z: 4, core: 2. Of those that a mesh axis runs over, the one named last changes fastest.
Arguments:
- volume: bfloat16 [2, 256, 256, 256], P(None, 'cuts', 'coil'), may hold values from -6 to 6
- coil_maps: bfloat16 [16, 2, 256, 256, 256], P('coil', None, 'cuts'), may hold values from -3 to 3
- kspace: bfloat16 [16, 2, 256, 256, 256], P('coil', None, None, 'cuts'), may hold values from -3 to 3
- line_mask: int32 [256, 256], replicated, may hold values 0 or 1
Outputs:
- updated: bfloat16 [2, 256, 256, 256], P(None, 'coil', 'cuts')
All inputs are finite; a program needn't handle non-finite values.
Results may differ from a plain program's by a relative error of at most 0.012.
Values may be sent and summed in bfloat16 or wider, within the bound.
No kernel may reach another device: no remote copies, remote signals or barrier semaphores. Data moves between devices by JAX's collectives and lax.ppermute only.
A program may use at most 384 MiB of HBM per device.

v0:
```python
import math

import jax
import jax.numpy as jnp
from jax import lax
from jax.sharding import PartitionSpec as P


def tables(length):
    counter = jnp.arange(length, dtype=jnp.int32)
    product = counter[:, None] * counter[None, :] % length
    angles = product.astype(jnp.float32) * (2.0 * math.pi / length)
    factor = 1.0 / math.sqrt(length)
    return (
        (jnp.cos(angles) * factor).astype(jnp.bfloat16),
        (jnp.sin(angles) * factor).astype(jnp.bfloat16),
    )


def contract(pattern, values, table):
    return jnp.einsum(pattern, values, table, preferred_element_type=jnp.float32)


def transform(real_part, imag_part, cos_table, sin_table, pattern, inverse):
    real_cos = contract(pattern, real_part, cos_table)
    real_sin = contract(pattern, real_part, sin_table)
    imag_cos = contract(pattern, imag_part, cos_table)
    imag_sin = contract(pattern, imag_part, sin_table)
    if inverse:
        return (
            (real_cos - imag_sin).astype(jnp.bfloat16),
            (imag_cos + real_sin).astype(jnp.bfloat16),
        )
    return ((real_cos + imag_sin).astype(jnp.bfloat16), (imag_cos - real_sin).astype(jnp.bfloat16))


def body(volume, coil_maps, kspace, line_mask):
    edge = volume.shape[3]
    cos_table, sin_table = tables(edge)
    sampled = line_mask.astype(jnp.float32)
    h_real, h_imag = transform(
        kspace[:, 0], kspace[:, 1], cos_table, sin_table, "cnyz,nk->ckyz", True
    )
    hybrid = jnp.stack([h_real, h_imag], axis=1)
    arrived = lax.all_to_all(hybrid, "cuts", split_axis=2, concat_axis=3, tiled=True)
    full_slab = lax.all_gather(volume, "coil", axis=2, tiled=True)
    vol_real = full_slab[0].astype(jnp.float32)
    vol_imag = full_slab[1].astype(jnp.float32)
    map_real = coil_maps[:, 0].astype(jnp.float32)
    map_imag = coil_maps[:, 1].astype(jnp.float32)
    coil_real = (map_real * vol_real - map_imag * vol_imag).astype(jnp.bfloat16)
    coil_imag = (map_real * vol_imag + map_imag * vol_real).astype(jnp.bfloat16)
    z_real, z_imag = transform(coil_real, coil_imag, cos_table, sin_table, "cxyn,nk->cxyk", False)
    k_real, k_imag = transform(z_real, z_imag, cos_table, sin_table, "cxnz,nk->cxkz", False)
    res_real = (sampled * (k_real.astype(jnp.float32) - arrived[:, 0].astype(jnp.float32))).astype(
        jnp.bfloat16
    )
    res_imag = (sampled * (k_imag.astype(jnp.float32) - arrived[:, 1].astype(jnp.float32))).astype(
        jnp.bfloat16
    )
    y_real, y_imag = transform(res_real, res_imag, cos_table, sin_table, "cxnz,nk->cxkz", True)
    b_real, b_imag = transform(y_real, y_imag, cos_table, sin_table, "cxyn,nk->cxyk", True)
    back_real = b_real.astype(jnp.float32)
    back_imag = b_imag.astype(jnp.float32)
    grad_real = jnp.sum(map_real * back_real + map_imag * back_imag, axis=0)
    grad_imag = jnp.sum(map_real * back_imag - map_imag * back_real, axis=0)
    leading = (lax.axis_index("coil") == 0).astype(jnp.float32)
    term = leading * jnp.stack([vol_real, vol_imag]) - 0.5 * jnp.stack([grad_real, grad_imag])
    summed = lax.psum_scatter(term, "coil", scatter_dimension=3, tiled=True).astype(jnp.bfloat16)
    return lax.all_to_all(
        lax.all_to_all(summed, "cuts", split_axis=2, concat_axis=1, tiled=True),
        "coil",
        split_axis=1,
        concat_axis=3,
        tiled=True,
    )


def solution(mesh):
    placed = (
        P(None, "cuts", "coil", None),
        P("coil", None, "cuts", None, None),
        P("coil", None, None, "cuts", None),
        P(),
    )
    return jax.shard_map(
        body, mesh=mesh, in_specs=placed, out_specs=P(None, "coil", "cuts", None), check_vma=False
    )
```

profile of v0, /device:TPU:0, one launch (start us, length us, event | category | flops | bytes accessed | tf_op | source)
XLA Modules:
  0.0 1394.0 jit_solution(13713898884665704678)
XLA Ops:
  6.5 22.6 %fusion.163 = (bf16[8,1,256,16,256]{4,3,2,1,0:T(8,128)(2,1)}, bf16[8,1,256,16,256]{4,3,2,1,0:T(8,128)(2,1)}) fusion(bf16[8,2,256,16,256]{4,3,2,1,0:T(8,128)(2,1)} %param.6), kind=kLoop, calls=%fused_computation.173 | loop fusion | bytes 67108864 | tf_op jit(solution)/shard_map/slice | solution.py:42
  50.7 21.5 %fusion.17 = f32[256,8,16,256]{3,0,2,1:T(8,128)} fusion(bf16[8,1,256,16,256]{4,3,2,1,0:T(8,128)(2,1)} %get-tuple-element.8), kind=kOutput, calls=%fused_computation.42 | convolution fusion | flops 4296015872 | bytes 50331648 | tf_op jit(solution)/shard_map/cnyz,nk->ckyz/dot_general | solution.py:21
  72.2 33.4 %fusion.13 = bf16[8,1,256,16,256]{4,2,3,0,1:T(8,128)(2,1)} fusion(f32[256,8,16,256]{3,0,2,1:T(8,128)} %fusion.16, bf16[8,1,256,16,256]{4,3,2,1,0:T(8,128)(2,1)} %get-tuple-element.7), kind=kOutput, calls=%fused_computation.34 | convolution fusion | flops 4312793088 | bytes 67108864 | tf_op jit(solution)/shard_map/cnyz,nk->ckyz/dot_general | solution.py:21
  105.6 33.2 %fusion.12 = bf16[8,1,256,16,256]{4,2,3,0,1:T(8,128)(2,1)} fusion(f32[256,8,16,256]{3,0,2,1:T(8,128)} %fusion.17, bf16[8,1,256,16,256]{4,3,2,1,0:T(8,128)(2,1)} %get-tuple-element.7), kind=kOutput, calls=%fused_computation.33 | convolution fusion | flops 4312793088 | bytes 67108864 | tf_op jit(solution)/shard_map/cnyz,nk->ckyz/dot_general | solution.py:21
  138.8 22.9 %pad_maximum_fusion = bf16[8,2,256,16,256]{4,2,3,0,1:T(8,128)(2,1)} fusion(bf16[8,1,256,16,256]{4,2,3,0,1:T(8,128)(2,1)} %fusion.13, bf16[8,1,256,16,256]{4,2,3,0,1:T(8,128)(2,1)} %fusion.12), kind=kLoop, calls=%fused_computation.16 | loop fusion | flops 16777216 | bytes 67108864 | tf_op jit(solution)/shard_map/stack | solution.py:44
  161.8 22.9 %copy.99 = bf16[8,2,256,16,256]{4,3,0,1,2:T(8,128)(2,1)} copy(bf16[8,2,256,16,256]{4,2,3,0,1:T(8,128)(2,1)} %pad_maximum_fusion) | data formatting | bytes 67108864 | tf_op jit(solution)/shard_map/stack | solution.py:44
  195.7 57.7 %all-gather.2.cloned.1.call-done = bf16[2,16,256,256]{3,1,0,2:T(8,128)(2,1)} async-done(((bf16[2,16,128,256]{3,1,0,2:T(8,128)(2,1)}), bf16[2,16,256,256]{3,1,0,2:T(8,128)(2,1)}) %all-gather.2.cloned.1.call-update) | async-done | bytes 4194320 | tf_op jit(solution)/shard_map/all_gather | solution.py:46
  262.7 29.2 %fusion.51 = f32[8,16,256,256]{3,2,1,0:T(8,128)} fusion(f32[16,256,256]{2,1,0:T(8,128)} %get-tuple-element.16, f32[16,256,256]{2,1,0:T(8,128)} %get-tuple-element.11, bf16[8,2,16,256,256]{4,3,2,1,0:T(8,128)(2,1)} %param.5), kind=kOutput, calls=%fused_computation.69 | convolution fusion | flops 4346347520 | bytes 75497472 | tf_op jit(solution)/shard_map/cxyn,nk->cxyk/dot_general | solution.py:21
  292.0 32.1 %subtract_convert_fusion.4 = bf16[8,16,256,256]{3,2,1,0:T(8,128)(2,1)} fusion(f32[8,16,256,256]{3,2,1,0:T(8,128)} %fusion.51, f32[16,256,256]{2,1,0:T(8,128)} %get-tuple-element.16, f32[16,256,256]{2,1,0:T(8,128)} %get-tuple-element.11, bf16[8,2,16,256,256]{4,3,2,1,0:T(8,128)(2,1)} %param.5), kind=kOutput, calls=%fused_computation.31 | convolution fusion | flops 4363124736 | bytes 92274688 | tf_op jit(solution)/shard_map/cxyn,nk->cxyk/dot_general | solution.py:21
  343.5 29.4 %fusion.53 = f32[8,16,256,256]{3,2,1,0:T(8,128)} fusion(f32[16,256,256]{2,1,0:T(8,128)} %get-tuple-element.16, f32[16,256,256]{2,1,0:T(8,128)} %get-tuple-element.11, bf16[8,2,16,256,256]{4,3,2,1,0:T(8,128)(2,1)} %param.5), kind=kOutput, calls=%fused_computation.70 | convolution fusion | flops 4346347520 | bytes 75497472 | tf_op jit(solution)/shard_map/cxyn,nk->cxyk/dot_general | solution.py:21
  372.8 32.1 %add_convert_fusion.4 = bf16[8,16,256,256]{3,2,1,0:T(8,128)(2,1)} fusion(f32[8,16,256,256]{3,2,1,0:T(8,128)} %fusion.53, f32[16,256,256]{2,1,0:T(8,128)} %get-tuple-element.16, f32[16,256,256]{2,1,0:T(8,128)} %get-tuple-element.11, bf16[8,2,16,256,256]{4,3,2,1,0:T(8,128)(2,1)} %param.5), kind=kOutput, calls=%fused_computation.32 | convolution fusion | flops 4363124736 | bytes 92274688 | tf_op jit(solution)/shard_map/cxyn,nk->cxyk/dot_general | solution.py:21
  424.2 357.0 %all-to-all-done = bf16[8,2,256,16,256]{4,3,0,1,2:T(8,128)(2,1)} async-done(((bf16[8,2,256,16,256]{4,3,0,1,2:T(8,128)(2,1)}), bf16[8,2,256,16,256]{4,3,0,1,2:T(8,128)(2,1)}, u32[]{:S(2)}, u32[]{:S(2)}) %all-to-all-start) | async-done | bytes 33554464 | tf_op jit(solution)/shard_map/all_to_all | solution.py:45
  781.2 23.4 %copy.100 = bf16[8,2,16,16,16,256]{5,4,2,3,0,1:T(8,128)(2,1)} copy(bf16[8,2,16,16,16,256]{5,4,0,1,3,2:T(8,128)(2,1)} %bitcast.26) | data formatting | bytes 67108864 | tf_op jit(solution)/shard_map/all_to_all | solution.py:45
  804.6 28.0 %fusion.9 = bf16[8,16,256,256]{3,2,1,0:T(8,128)(2,1)} fusion(f32[256,8,16,256]{3,0,2,1:T(8,128)} %fusion.43, bf16[8,2,16,256,256]{4,3,2,0,1:T(8,128)(2,1)} %bitcast.139, f32[256,256]{1,0:T(8,128)S(1)} %copy-done, bf16[8,16,256,256]{3,2,1,0:T(8,128)(2,1)} %add_convert_fusion.4), kind=kOutput, calls=%fused_computation.19 | convolution fusion | flops 4354736128 | bytes 84148224 | tf_op jit(solution)/shard_map/cxnz,nk->cxkz/dot_general | solution.py:21
  852.1 27.9 %fusion.11 = bf16[8,16,256,256]{3,2,1,0:T(8,128)(2,1)} fusion(f32[256,8,16,256]{3,0,2,1:T(8,128)} %fusion.55, bf16[8,2,16,256,256]{4,3,2,0,1:T(8,128)(2,1)} %bitcast.140, f32[256,256]{1,0:T(8,128)S(1)} %copy-done, bf16[8,16,256,256]{3,2,1,0:T(8,128)(2,1)} %subtract_convert_fusion.4), kind=kOutput, calls=%fused_computation.22 | convolution fusion | flops 4354736128 | bytes 84148224 | tf_op jit(solution)/shard_map/cxnz,nk->cxkz/dot_general | solution.py:21
  899.4 22.9 %fusion.15 = bf16[8,16,256,256]{3,2,1,0:T(8,128)(2,1)} fusion(f32[256,8,16,256]{3,0,2,1:T(8,128)} %fusion.41, bf16[8,16,256,256]{3,2,1,0:T(8,128)(2,1)} %fusion.11), kind=kOutput, calls=%fused_computation.36 | convolution fusion | flops 4312793088 | bytes 67108864 | tf_op jit(solution)/shard_map/cxnz,nk->cxkz/dot_general | solution.py:21
  922.3 22.3 %fusion.47 = f32[8,16,256,256]{3,2,1,0:T(8,128)} fusion(bf16[8,16,256,256]{3,2,1,0:T(8,128)(2,1)} %fusion.15), kind=kOutput, calls=%fused_computation.67 | convolution fusion | flops 4296015872 | bytes 50331648 | tf_op jit(solution)/shard_map/cxyn,nk->cxyk/dot_general | solution.py:21
  944.6 22.7 %fusion.14 = bf16[8,16,256,256]{3,2,1,0:T(8,128)(2,1)} fusion(f32[256,8,16,256]{3,0,2,1:T(8,128)} %fusion.57, bf16[8,16,256,256]{3,2,1,0:T(8,128)(2,1)} %fusion.9), kind=kOutput, calls=%fused_computation.35 | convolution fusion | flops 4312793088 | bytes 67108864 | tf_op jit(solution)/shard_map/cxnz,nk->cxkz/dot_general | solution.py:21
  967.3 22.3 %fusion.49 = f32[8,16,256,256]{3,2,1,0:T(8,128)} fusion(bf16[8,16,256,256]{3,2,1,0:T(8,128)(2,1)} %fusion.14), kind=kOutput, calls=%fused_computation.68 | convolution fusion | flops 4296015872 | bytes 50331648 | tf_op jit(solution)/shard_map/cxyn,nk->cxyk/dot_general | solution.py:21
  989.6 24.4 %add_convert_fusion = bf16[8,16,256,256]{3,2,1,0:T(8,128)(2,1)} fusion(f32[8,16,256,256]{3,2,1,0:T(8,128)} %fusion.47, bf16[8,16,256,256]{3,2,1,0:T(8,128)(2,1)} %fusion.14), kind=kOutput, calls=%fused_computation.23 | convolution fusion | flops 4312793088 | bytes 67108864 | tf_op jit(solution)/shard_map/cxyn,nk->cxyk/dot_general | solution.py:21
  1014.0 38.9 %fusion.5 = (f32[16,256,256]{2,1,0:T(8,128)}, f32[16,256,256]{2,1,0:T(8,128)}) fusion(bf16[8,16,256,256]{3,2,1,0:T(8,128)(2,1)} %add_convert_fusion, bf16[8,2,16,256,256]{4,3,2,1,0:T(8,128)(2,1)} %param.5, f32[8,16,256,256]{3,2,1,0:T(8,128)} %fusion.49, bf16[8,16,256,256]{3,2,1,0:T(8,128)(2,1)} %fusion.15), kind=kOutput, calls=%fused_computation.13 | convolution fusion | flops 4411359232 | bytes 109051904 | tf_op jit(solution)/shard_map/cxyn,nk->cxyk/dot_general | solution.py:21
  1060.7 232.6 %reduce-scatter.2.cloned.1.call-done = f32[2,16,256,128]{3,2,1,0:T(8,128)} async-done(((f32[2,16,256,256]{3,2,1,0:T(8,128)}), f32[2,16,256,128]{3,2,1,0:T(8,128)}) %reduce-scatter.2.cloned.1.call-update) | async-done | bytes 4194320 | tf_op jit(solution)/shard_map/reduce_scatter | solution.py:69
  1297.2 52.7 %all_to_all.54 = bf16[2,16,256,128]{3,1,0,2:T(8,128)(2,1)S(1)} all-to-all(bf16[2,16,256,128]{3,1,0,2:T(8,128)(2,1)S(1)} %copy.107), channel_id=1, replica_groups=mesh['cuts'=16,'coil'=2] {'cuts'}, dimensions={2} | all-to-all | bytes 4194304 | tf_op jit(solution)/shard_map/all_to_all | solution.py:71
  1351.2 28.6 %all_to_all.55 = bf16[2,256,16,128]{3,2,0,1:T(8,128)(2,1)S(1)} all-to-all(bf16[2,256,16,128]{3,2,0,1:T(8,128)(2,1)S(1)} %copy.110), channel_id=1, replica_groups=mesh['cuts'=16,'coil'=2] {'coil'}, dimensions={1} | all-to-all | bytes 4194304 | tf_op jit(solution)/shard_map/all_to_all | solution.py:70
  (29 shorter events, 139.5 us)
Async XLA Ops:
  184.7 7.7 copy-start.2
  184.7 10.2 copy-start.3
  184.7 596.5 %all-to-all-start = ((bf16[8,2,256,16,256]{4,3,0,1,2:T(8,128)(2,1)}), bf16[8,2,256,16,256]{4,3,0,1,2:T(8,128)(2,1)}, u32[]{:S(2)}, u32[]{:S(2)}) async-start(bf16[8,2,256,16,256]{4,3,0,1,2:T(8,128)(2,1)} %copy.99), calls=%async_computation | async-start | bytes 67108864 | tf_op jit(solution)/shard_map/all_to_all | solution.py:45
  192.3 61.1 %all-gather.2.cloned.1.call-start = ((), (), s32[]{:S(2)}) async-start(), calls=%async_computation.4 | async-start | bytes 6291456 | tf_op jit(solution)/shard_map/all_gather | solution.py:46
  194.9 1098.5 %reduce-scatter.2.cloned.1.call-start = ((), (), s32[]{:S(2)}) async-start(), calls=%async_computation.5 | async-start | bytes 12582912 | tf_op jit(solution)/shard_map/reduce_scatter | solution.py:69
  781.2 23.4 %copy-start = (f32[256,256]{1,0:T(8,128)S(1)}, f32[256,256]{1,0:T(8,128)}, u32[]{:S(2)}) copy-start(f32[256,256]{1,0:T(8,128)} %convert_element_type.205) | copy-start | bytes 786436
  1014.0 38.9 %copy-start.1 = (f32[1,16,256,256]{3,2,1,0:T(8,128)S(1)}, f32[1,16,256,256]{3,2,1,0:T(8,128)}, u32[]{:S(2)}) copy-start(f32[1,16,256,256]{3,2,1,0:T(8,128)} %get-tuple-element.12) | copy-start | bytes 12582916
Sparse Core Ops, SparseCore 0:
  195.0 58.3 all-gather.1
  1060.9 232.4 reduce-scatter.1
where the time goes:
time: 1400 us; the launch traced here: 1390 us
  waiting for transfers between devices  647 us (46%)
  matrix products  520 us (37%)
  local copies, waits for them, and re-layouts  83.7 us (6%)
  blocking collectives  81.3 us (6%)
  other arithmetic  40.8 us (3%)
    dot_general x20, matrix products, contract(): jnp.einsum(pattern, values, table, preferred_element_type=jnp.float32)  520 us
    all_to_all x1, waiting for transfers between devices, body(): lax.all_to_all(hybrid, 'cuts', split_axis=2, concat_axis=3, tiled=True)  357 us
    reduce_scatter x1, waiting for transfers between devices, body(): lax.psum_scatter(term, 'coil', scatter_dimension=3, tiled=True)  233 us
    all_gather x1, waiting for transfers between devices, body(): full_slab = lax.all_gather(volume, 'coil', axis=2, tiled=True)  57.7 us
    all_to_all x1, blocking collectives, body(): lax.all_to_all(summed, 'cuts', split_axis=2, concat_axis=1, tiled=True)  52.7 us
    all_to_all x1, blocking collectives, body(): lax.all_to_all(lax.all_to_all(summed, 'cuts', split_axis=2, concat_axis=1...  28.6 us
  transfers between devices with their start and end apart: 3, of which 3 were waited for; matrix products, arithmetic and copies ran while one was open for 12% of the time, Pallas kernels for 0%

commit v1 on v0

v1 whole, which is shorter than its diff:
```python
import functools
import math

import jax
import jax.numpy as jnp
from jax import lax
from jax.experimental import pallas as pl
from jax.experimental.pallas import tpu as pltpu
from jax.sharding import PartitionSpec as P

F32 = jnp.float32
BF16 = jnp.bfloat16
VMEM = 56 * 1024 * 1024


def tables(length):
    counter = jnp.arange(length, dtype=jnp.int32)
    product = counter[:, None] * counter[None, :] % length
    angles = product.astype(jnp.float32) * (2.0 * math.pi / length)
    factor = 1.0 / math.sqrt(length)
    return (
        (jnp.cos(angles) * factor).astype(jnp.bfloat16),
        (jnp.sin(angles) * factor).astype(jnp.bfloat16),
    )


def dot(a, b):
    return lax.dot_general(a, b, (((1,), (0,)), ((), ())), preferred_element_type=F32)


def cost(flops, bytes_accessed):
    return pl.CostEstimate(flops=int(flops), bytes_accessed=int(bytes_accessed), transcendentals=0)


def layout(line_mask, parts):
    edge = line_mask.shape[1]
    slab = line_mask.shape[0] // parts
    slots = edge // 2 * (slab + 1)
    half = edge // 2
    low = [max(half * k - (edge if k % 2 == 0 else half), 0) for k in range(slab)]
    high = [min(half * k + (edge if k % 2 == 0 else 3 * half), slots) for k in range(slab)]
    start_of_window = [min(at, slots - 2 * edge) for at in low]
    low, high, start_of_window = (jnp.array(v, jnp.int32) for v in (low, high, start_of_window))
    sampled = line_mask != 0
    upper = jnp.triu(jnp.ones((edge, edge), BF16), 1)
    rank = jnp.dot(sampled.astype(BF16), upper, preferred_element_type=F32).astype(jnp.int32)
    count = jnp.sum(sampled.astype(jnp.int32), axis=1).reshape(parts, slab)
    before = jnp.cumsum(count, axis=1) - count
    shift = lax.cummax(low[None, :] - before, axis=1)
    start = before + shift
    fits = jnp.all(start + count <= high[None, :])
    place = jnp.where(sampled, start.reshape(-1, 1) + rank, -1)
    window = jnp.tile(start_of_window, parts)[:, None]
    relative = jnp.where(sampled, place - window, -1)
    return fits, place, relative, slots


def compact_kernel(tiles, slots, k_ref, s_ref, t_ref, out_ref):
    slab, _, edge = k_ref.shape[1:]
    rows = out_ref.shape[2]
    parts = out_ref.shape[0]

    def tile(at, width):
        picked = None
        for j in range(4):
            k = jnp.clip(2 * at - 1 + j, 0, slab - 1)
            term = dot(k_ref[0, k], s_ref[at, j][:, :width])
            picked = term if picked is None else picked + term
        moved = dot(t_ref[...], picked.astype(BF16)).astype(BF16)
        return moved.reshape(parts, rows, width)

    @pl.loop(0, tiles)
    def _(at):
        out_ref[:, 0, :, pl.ds(pl.multiple_of(at * edge, edge), edge)] = tile(at, edge)

    rest = slots - tiles * edge
    if rest:
        out_ref[:, 0, :, tiles * edge :] = tile(tiles, rest)


def compact(data, select, table, parts, slots):
    coils, slab, both, edge = data.shape
    tiles = slots // edge
    rows = both // parts
    return pl.pallas_call(
        functools.partial(compact_kernel, tiles, slots),
        grid=(coils,),
        in_specs=[
            pl.BlockSpec((1, slab, both, edge), lambda c: (c, 0, 0, 0)),
            pl.BlockSpec(select.shape, lambda c: (0, 0, 0, 0)),
            pl.BlockSpec(table.shape, lambda c: (0, 0)),
        ],
        out_specs=pl.BlockSpec((parts, 1, rows, slots), lambda c: (0, c, 0, 0)),
        out_shape=jax.ShapeDtypeStruct((parts, coils, rows, slots), BF16),
        compiler_params=pltpu.CompilerParams(vmem_limit_bytes=VMEM),
        cost_estimate=cost(
            coils * 2 * slots * both * (4 * edge + both), 2 * coils * (data.size // coils + both * slots)
        ),
    )(data, select, table)


def expand_kernel(windows, rel_ref, in_ref, out_ref):
    edge = rel_ref.shape[1]
    rows = out_ref.shape[1]
    place = lax.broadcasted_iota(jnp.int32, (2 * edge, edge), 0)
    for k, at in enumerate(windows):
        chosen = jnp.where(place == rel_ref[k : k + 1, :], 1.0, 0.0).astype(BF16)
        source = in_ref[0, :, :, at : at + 2 * edge].reshape(rows, 2 * edge)
        out_ref[k] = dot(source, chosen).astype(BF16)


def expand(arrived, relative, windows):
    parts, coils, rows, slots = arrived.shape
    edge = relative.shape[1]
    slab = relative.shape[0] // parts
    return pl.pallas_call(
        functools.partial(expand_kernel, windows),
        grid=(parts,),
        in_specs=[
            pl.BlockSpec((slab, edge), lambda d: (d, 0)),
            pl.BlockSpec((1, coils, rows, slots), lambda d: (d, 0, 0, 0)),
        ],
        out_specs=pl.BlockSpec((slab, coils * rows, edge), lambda d: (d, 0, 0)),
        out_shape=jax.ShapeDtypeStruct((parts * slab, coils * rows, edge), BF16),
        compiler_params=pltpu.CompilerParams(vmem_limit_bytes=VMEM),
        cost_estimate=cost(
            parts * slab * coils * rows * edge * edge * 4, 2 * (arrived.size + parts * slab * coils * rows * edge)
        ),
    )(relative, arrived)


def forward_kernel(maps_ref, vol_ref, right_ref, left_ref, out_ref):
    edge = vol_ref.shape[3]
    for i in range(vol_ref.shape[1]):
        map_real, map_imag = maps_ref[0, 0, i].astype(F32), maps_ref[0, 1, i].astype(F32)
        vol_real, vol_imag = vol_ref[0, i].astype(F32), vol_ref[1, i].astype(F32)
        real = (map_real * vol_real - map_imag * vol_imag).astype(BF16)
        imag = (map_real * vol_imag + map_imag * vol_real).astype(BF16)
        along = dot(jnp.concatenate([real, imag], axis=1), right_ref[...]).astype(BF16)
        stacked = jnp.concatenate([along[:, :edge], along[:, edge:]], axis=0)
        out_ref[0, i] = dot(left_ref[...], stacked).astype(BF16)


def forward(maps, volume, right, left, group):
    coils, _, deep, edge, _ = maps.shape
    return pl.pallas_call(
        forward_kernel,
        grid=(deep // group, coils),
        in_specs=[
            pl.BlockSpec((1, 2, group, edge, edge), lambda x, c: (c, 0, x, 0, 0)),
            pl.BlockSpec((2, group, edge, edge), lambda x, c: (0, x, 0, 0)),
            pl.BlockSpec(right.shape, lambda x, c: (0, 0)),
            pl.BlockSpec(left.shape, lambda x, c: (0, 0)),
        ],
        out_specs=pl.BlockSpec((1, group, 2 * edge, edge), lambda x, c: (c, x, 0, 0)),
        out_shape=jax.ShapeDtypeStruct((coils, deep, 2 * edge, edge), BF16),
        compiler_params=pltpu.CompilerParams(vmem_limit_bytes=VMEM),
        cost_estimate=cost(coils * deep * edge**3 * 16, 4 * maps.size),
    )(maps, volume, right, left)


def backward_kernel(first, *refs):
    if first:
        maps_ref, k_ref, h_ref, mask_ref, left_ref, right_ref, out_ref = refs
    else:
        maps_ref, k_ref, h_ref, mask_ref, left_ref, right_ref, sum_ref, out_ref = refs
    edge = mask_ref.shape[1]
    sampled = mask_ref[...].astype(F32)
    sampled = jnp.concatenate([sampled, sampled], axis=0)

    @pl.when(pl.program_id(1) == 0)
    def _():
        out_ref[...] = jnp.zeros_like(out_ref) if first else sum_ref[...]

    for i in range(k_ref.shape[1]):
        hybrid = h_ref[0, :, i].reshape(2 * edge, edge)
        residual = (sampled * (k_ref[0, i].astype(F32) - hybrid.astype(F32))).astype(BF16)
        back = dot(left_ref[...], residual).astype(BF16)
        back = jnp.concatenate([back[:edge], back[edge:]], axis=1)
        back = dot(back, right_ref[...]).astype(BF16).astype(F32)
        real, imag = back[:, :edge], back[:, edge:]
        map_real, map_imag = maps_ref[0, 0, i].astype(F32), maps_ref[0, 1, i].astype(F32)
        out_ref[0, i] += map_real * real + map_imag * imag
        out_ref[1, i] += map_real * imag - map_imag * real


def backward(maps, coil_kspace, hybrid, line_mask, left, right, total, first_coil, group):
    coils, _, deep, edge, _ = hybrid.shape
    spec_sum = pl.BlockSpec((2, group, edge, edge), lambda x, c: (0, x, 0, 0))
    first = total is None
    return pl.pallas_call(
        functools.partial(backward_kernel, first),
        grid=(deep // group, coils),
        in_specs=[
            pl.BlockSpec((1, 2, group, edge, edge), lambda x, c: (first_coil + c, 0, x, 0, 0)),
            pl.BlockSpec((1, group, 2 * edge, edge), lambda x, c: (first_coil + c, x, 0, 0)),
            pl.BlockSpec((1, 2, group, edge, edge), lambda x, c: (c, 0, x, 0, 0)),
            pl.BlockSpec(line_mask.shape, lambda x, c: (0, 0)),
            pl.BlockSpec(left.shape, lambda x, c: (0, 0)),
            pl.BlockSpec(right.shape, lambda x, c: (0, 0)),
        ]
        + ([] if first else [spec_sum]),
        out_specs=spec_sum,
        out_shape=jax.ShapeDtypeStruct((2, deep, edge, edge), F32),
        compiler_params=pltpu.CompilerParams(vmem_limit_bytes=VMEM),
        cost_estimate=cost(coils * deep * edge**3 * 16, 6 * hybrid.size + 16 * deep * edge**2),
    )(maps, coil_kspace, hybrid, line_mask, left, right, *([] if first else [total]))


def body(coil_groups, volume, coil_maps, kspace, line_mask):
    coils, _, deep, edge, _ = coil_maps.shape
    slab = kspace.shape[3]
    parts = edge // slab
    me = lax.axis_index("cuts")
    cos_table, sin_table = tables(edge)
    turn = jnp.block([[cos_table, sin_table], [-sin_table, cos_table]])
    turn_back = jnp.block([[cos_table, -sin_table], [sin_table, cos_table]])
    by_destination = turn_back.reshape(2, parts, deep, 2 * edge).transpose(1, 0, 2, 3).reshape(2 * edge, 2 * edge)
    fits, place, relative, slots = layout(line_mask, parts)
    half = edge // 2
    windows = tuple(
        min(max(half * k - (edge if k % 2 == 0 else half), 0), slots - 2 * edge) for k in range(slab)
    )
    full_slab = lax.all_gather(volume, "coil", axis=2, tiled=True)
    chunks = min(4, coils)
    each = coils // chunks
    group = min(4, deep)

    def send_sampled(full_slab):
        mine = lax.dynamic_slice_in_dim(place, me * slab, slab, 0)
        tiles = -(-slots // edge)
        member = jnp.clip(2 * jnp.arange(tiles)[:, None] - 1 + jnp.arange(4)[None, :], -1, slab)
        padded = jnp.pad(mine, ((1, 1), (0, 0)), constant_values=-1)
        offset = padded[member + 1] - edge * jnp.arange(tiles)[:, None, None]
        select = (offset[..., None] == jnp.arange(edge)).astype(BF16)
        out = []
        for i in range(chunks):
            part = lax.slice_in_dim(kspace, i * each, (i + 1) * each, axis=0)
            data = part.transpose(0, 3, 1, 2, 4).reshape(each, slab, 2 * edge, edge)
            sent = compact(data, select, by_destination, parts, slots)
            out.append(lax.all_to_all(sent, "cuts", split_axis=0, concat_axis=0, tiled=True))
        coil_kspace = forward(coil_maps, full_slab, turn_back, turn, group)
        total = None
        for i in range(chunks):
            hybrid = expand(out[i], relative, windows)
            hybrid = hybrid.reshape(edge, each, 2, deep, edge).transpose(1, 2, 3, 0, 4)
            total = backward(
                coil_maps, coil_kspace, hybrid, line_mask, turn_back, turn, total, i * each, group
            )
        return total

    def send_all(full_slab):
        out = []
        for i in range(chunks):
            part = lax.slice_in_dim(kspace, i * each, (i + 1) * each, axis=0)
            data = part.transpose(0, 3, 1, 2, 4).reshape(each, slab, 2 * edge, edge)
            moved = jnp.einsum("xn,ckny->xcky", by_destination, data, preferred_element_type=F32).astype(BF16)
            moved = moved.reshape(parts, 2, deep, each, slab, edge)
            out.append(lax.all_to_all(moved, "cuts", split_axis=0, concat_axis=0, tiled=True))
        coil_kspace = forward(coil_maps, full_slab, turn_back, turn, group)
        total = None
        for i in range(chunks):
            hybrid = out[i].transpose(3, 1, 2, 0, 4, 5).reshape(each, 2, deep, edge, edge)
            total = backward(
                coil_maps, coil_kspace, hybrid, line_mask, turn_back, turn, total, i * each, group
            )
        return total

    total = lax.cond(fits, send_sampled, send_all, full_slab)
    return finish(coil_groups, full_slab, total)


def finish(coil_groups, full_slab, total):
    _, deep, edge, _ = total.shape
    mine = lax.axis_index("coil")
    share = deep // coil_groups
    summed = lax.dynamic_slice_in_dim(total, mine * share, share, 1)
    for step in range(1, coil_groups):
        other = lax.rem(mine + step, coil_groups)
        away = lax.dynamic_slice_in_dim(total, other * share, share, 1).astype(BF16)
        ring = [(i, (i + step) % coil_groups) for i in range(coil_groups)]
        summed = summed + lax.ppermute(away, "coil", ring).astype(F32)
    base = lax.dynamic_slice_in_dim(full_slab, mine * share, share, 1).astype(F32)
    updated = (base - 0.5 * summed).astype(BF16)
    updated = lax.all_to_all(updated, "cuts", split_axis=2, concat_axis=1, tiled=True)
    parts = edge // deep
    slab = updated.shape[2]
    updated = updated.reshape(2, coil_groups, parts // coil_groups, share, slab, edge)
    updated = lax.all_to_all(updated, "coil", split_axis=1, concat_axis=1, tiled=True)
    updated = updated.transpose(0, 2, 1, 3, 4, 5)
    return updated.reshape(2, edge // coil_groups, slab, edge)


def solution(mesh):
    placed = (
        P(None, "cuts", "coil", None),
        P("coil", None, "cuts", None, None),
        P("coil", None, None, "cuts", None),
        P(),
    )
    return jax.shard_map(
        functools.partial(body, mesh.shape["coil"]),
        mesh=mesh,
        in_specs=placed,
        out_specs=P(None, "coil", "cuts", None),
        check_vma=False,
    )
```

time: 1400 us -> 893 us (0.64)
  matrix products: 520 us -> 0.19 us
  waiting for transfers between devices: 647 us -> 286 us
  Pallas kernels: 0 us -> 296 us
  starting transfers between devices: 7.67 us -> 68.9 us
  local copies, waits for them, and re-layouts: 83.7 us -> 119 us
  other arithmetic: 40.8 us -> 13.6 us
    dot_general x20 -> x1, matrix products: 520 us -> 0.19 us  [layout(): jnp.dot(sampled.astype(BF16), upper, preferred_element_type=F32)]
    pallas_call x0 -> x13, Pallas kernels: none -> 296 us  [the longest x4 83.4 us: compact(): pl.pallas_call(functools.partial(compact_kernel, tiles, slots), grid=(coi...]
    reduce_scatter x1 -> x0, waiting for transfers between devices: 233 us -> none  [body(): lax.psum_scatter(term, 'coil', scatter_dimension=3, tiled=True)]
    all_to_all x1 -> x4, waiting for transfers between devices: 357 us -> 184 us  [send_sampled(): lax.all_to_all(sent, 'cuts', split_axis=0, concat_axis=0, tiled=True)]
    all_to_all x1 -> x4, starting transfers between devices: 7.58 us -> 68.3 us  [send_sampled(): lax.all_to_all(sent, 'cuts', split_axis=0, concat_axis=0, tiled=True)]
    ppermute x0 -> x1, waiting for transfers between devices: none -> 47.6 us  [finish(): summed = summed + lax.ppermute(away, 'coil', ring).astype(F32)]
    pallas_call x0 -> x4, local copies, waits for them, and re-layouts: none -> 45.6 us  [expand(): pl.pallas_call(functools.partial(expand_kernel, windows), grid=(parts,),...]
    all_to_all x5 -> x1, local copies, waits for them, and re-layouts: 31.8 us -> 1.55 us  [finish(): lax.all_to_all(updated, 'coil', split_axis=1, concat_axis=1, tiled=True)]
  transfers between devices with their start and end apart: 3 -> 6, of which waited for: 3 -> 5; matrix products, arithmetic and copies ran while one was open for 12% -> 5% of each run, Pallas kernels for 0% -> 20%
where the time goes in v1:
time: 893 us; the launch traced here: 885 us
  Pallas kernels  296 us (33%)
  waiting for transfers between devices  286 us (32%)
  local copies, waits for them, and re-layouts  119 us (13%)
  blocking collectives  81.5 us (9%)
  starting transfers between devices  68.9 us (8%)
  between operations  14.7 us (2%)
  other arithmetic  13.6 us (2%)
    all_to_all x4, waiting for transfers between devices, send_sampled(): lax.all_to_all(sent, 'cuts', split_axis=0, concat_axis=0, tiled=True)  184 us
    pallas_call x4, Pallas kernels, compact(): pl.pallas_call(functools.partial(compact_kernel, tiles, slots), grid=(coi...  83.4 us
    pallas_call x4, Pallas kernels, backward(): pl.pallas_call(functools.partial(backward_kernel, first), grid=(deep // g...  82.7 us
    pallas_call x4, Pallas kernels, expand(): pl.pallas_call(functools.partial(expand_kernel, windows), grid=(parts,),...  71.5 us
    all_to_all x4, starting transfers between devices, send_sampled(): lax.all_to_all(sent, 'cuts', split_axis=0, concat_axis=0, tiled=True)  68.3 us
    pallas_call x1, Pallas kernels, forward(): pl.pallas_call(forward_kernel, grid=(deep // group, coils), in_specs=[pl....  58 us
    all_gather x1, waiting for transfers between devices, body(): full_slab = lax.all_gather(volume, 'coil', axis=2, tiled=True)  54.2 us
    all_to_all x1, blocking collectives, finish(): lax.all_to_all(updated, 'cuts', split_axis=2, concat_axis=1, tiled=True)  52.9 us
  transfers between devices with their start and end apart: 6, of which 5 were waited for; matrix products, arithmetic and copies ran while one was open for 5% of the time, Pallas kernels for 20%

profile of v1, /device:TPU:0, one launch (start us, length us, event | category | flops | bytes accessed | tf_op | source)
XLA Modules:
  0.0 885.3 jit_solution(7588542958166878318)
XLA Ops:
  16.1 54.2 %all-gather.2.cloned.1.call-done = bf16[2,16,256,256]{3,1,0,2:T(8,128)(2,1)} async-done(((bf16[2,16,128,256]{3,1,0,2:T(8,128)(2,1)}), bf16[2,16,256,256]{3,1,0,2:T(8,128)(2,1)}) %all-gather.2.cloned.1.call-update) | async-done | bytes 4194320 | tf_op jit(solution)/shard_map/all_gather | solution.py:224
  70.3 667.7 %conditional.1 = (f32[2,16,256,256]{3,1,0,2:T(8,128)S(1)}) conditional(s32[]{:T(128)} %convert_element_type.74, (bf16[8,2,16,256,256]{4,3,2,1,0:T(8,128)(2,1)}, bf16[2,16,256,256]{3,1,0,2:T(8,128)(2,1)}, bf16[512,512]{1,0:T(8,128)(2,1)S(1)}, bf16[512,512]{1,0:T(8,128)(2,1)S(1)}, bf16[8,2,256,16,256]{4,3,2,1,0:T(8,128)(2,1)}, ...), branch_computations={%region_4.5_spmd, %region_5.6_spmd} | conditional | flops 113284751360 | bytes 699400320 | solution.py:269
  83.2 23.1 %copy.85 = bf16[8,2,256,16,256]{4,2,1,3,0:T(8,128)(2,1)} copy(bf16[8,2,256,16,256]{4,3,2,1,0:T(8,128)(2,1)} %get-tuple-element.191) | data formatting | bytes 67108864 | tf_op jit(solution)/shard_map
  106.3 22.8 %fusion.22 = (bf16[2,2,256,16,256]{4,2,1,3,0:T(8,128)(2,1)}, bf16[2,2,256,16,256]{4,2,1,3,0:T(8,128)(2,1)}, bf16[2,2,256,16,256]{4,2,1,3,0:T(8,128)(2,1)}, bf16[2,2,256,16,256]{4,2,1,3,0:T(8,128)(2,1)}) fusion(bf16[8,2,256,16,256]{4,2,1,3,0:T(8,128)(2,1)} %copy.85), kind=kLoop, calls=%fused_computation.53 | loop fusion | bytes 67108864 | tf_op jit(solution)/shard_map/cond/branch_1_fun/slice | solution.py:238
  129.1 20.9 %branch_1_fun.20 = bf16[16,2,32,2176]{3,2,1,0:T(8,128)(2,1)} custom-call(bf16[2,16,512,256]{3,2,1,0:T(8,128)(2,1)} %bitcast.99, bf16[9,4,256,256]{3,2,1,0:T(8,128)(2,1)} %fusion.4.s_ref, bf16[512,512]{1,0:T(8,128)(2,1)S(1)} %get-tuple-element.86.t_ref), custom_call_target="tpu_custom_call" | custom-call | flops 6845104128 | bytes 12845056 | tf_op jit(solution)/shard_map/cond/branch_1_fun/pallas_call | solution.py:85
  155.7 20.8 %branch_1_fun.18 = bf16[16,2,32,2176]{3,2,1,0:T(8,128)(2,1)} custom-call(bf16[2,16,512,256]{3,2,1,0:T(8,128)(2,1)} %bitcast.97, bf16[9,4,256,256]{3,2,1,0:T(8,128)(2,1)} %fusion.4.s_ref, bf16[512,512]{1,0:T(8,128)(2,1)S(1)} %get-tuple-element.86.t_ref), custom_call_target="tpu_custom_call" | custom-call | flops 6845104128 | bytes 12845056 | tf_op jit(solution)/shard_map/cond/branch_1_fun/pallas_call | solution.py:85
  176.5 61.4 %all-to-all-done.3.in_ref = bf16[16,2,32,2176]{3,2,1,0:T(8,128)(2,1)} async-done(((bf16[16,2,32,2176]{3,2,1,0:T(8,128)(2,1)}), bf16[16,2,32,2176]{3,2,1,0:T(8,128)(2,1)}, u32[]{:S(2)}, u32[]{:S(2)}) %all-to-all-start.3) | async-done | bytes 4456480 | tf_op jit(solution)/shard_map/cond/branch_1_fun/all_to_all | solution.py:241
  237.9 20.7 %all-to-all-start.2 = ((bf16[16,2,32,2176]{3,2,1,0:T(8,128)(2,1)}), bf16[16,2,32,2176]{3,2,1,0:T(8,128)(2,1)}, u32[]{:S(2)}, u32[]{:S(2)}) async-start(bf16[16,2,32,2176]{3,2,1,0:T(8,128)(2,1)} %branch_1_fun.18), calls=%async_computation.2 | async-start | bytes 8912896 | tf_op jit(solution)/shard_map/cond/branch_1_fun/all_to_all | solution.py:241
  258.7 20.9 %branch_1_fun.16 = bf16[16,2,32,2176]{3,2,1,0:T(8,128)(2,1)} custom-call(bf16[2,16,512,256]{3,2,1,0:T(8,128)(2,1)} %bitcast.95, bf16[9,4,256,256]{3,2,1,0:T(8,128)(2,1)} %fusion.4.s_ref, bf16[512,512]{1,0:T(8,128)(2,1)S(1)} %get-tuple-element.86.t_ref), custom_call_target="tpu_custom_call" | custom-call | flops 6845104128 | bytes 12845056 | tf_op jit(solution)/shard_map/cond/branch_1_fun/pallas_call | solution.py:85
  279.5 61.4 %all-to-all-done.2.in_ref = bf16[16,2,32,2176]{3,2,1,0:T(8,128)(2,1)} async-done(((bf16[16,2,32,2176]{3,2,1,0:T(8,128)(2,1)}), bf16[16,2,32,2176]{3,2,1,0:T(8,128)(2,1)}, u32[]{:S(2)}, u32[]{:S(2)}) %all-to-all-start.2) | async-done | bytes 4456480 | tf_op jit(solution)/shard_map/cond/branch_1_fun/all_to_all | solution.py:241
  340.9 20.7 %all-to-all-start.1 = ((bf16[16,2,32,2176]{3,2,1,0:T(8,128)(2,1)}), bf16[16,2,32,2176]{3,2,1,0:T(8,128)(2,1)}, u32[]{:S(2)}, u32[]{:S(2)}) async-start(bf16[16,2,32,2176]{3,2,1,0:T(8,128)(2,1)} %branch_1_fun.16), calls=%async_computation.1 | async-start | bytes 8912896 | tf_op jit(solution)/shard_map/cond/branch_1_fun/all_to_all | solution.py:241
  361.7 20.8 %branch_1_fun.14 = bf16[16,2,32,2176]{3,2,1,0:T(8,128)(2,1)} custom-call(bf16[2,16,512,256]{3,2,1,0:T(8,128)(2,1)} %bitcast.93, bf16[9,4,256,256]{3,2,1,0:T(8,128)(2,1)} %fusion.4.s_ref, bf16[512,512]{1,0:T(8,128)(2,1)S(1)} %get-tuple-element.86.t_ref), custom_call_target="tpu_custom_call" | custom-call | flops 6845104128 | bytes 12845056 | tf_op jit(solution)/shard_map/cond/branch_1_fun/pallas_call | solution.py:85
  382.5 61.4 %all-to-all-done.1.in_ref = bf16[16,2,32,2176]{3,2,1,0:T(8,128)(2,1)} async-done(((bf16[16,2,32,2176]{3,2,1,0:T(8,128)(2,1)}), bf16[16,2,32,2176]{3,2,1,0:T(8,128)(2,1)}, u32[]{:S(2)}, u32[]{:S(2)}) %all-to-all-start.1) | async-done | bytes 4456480 | tf_op jit(solution)/shard_map/cond/branch_1_fun/all_to_all | solution.py:241
  443.9 21.2 %all-to-all-start = ((bf16[16,2,32,2176]{3,2,1,0:T(8,128)(2,1)}), bf16[16,2,32,2176]{3,2,1,0:T(8,128)(2,1)}, u32[]{:S(2)}, u32[]{:S(2)}) async-start(bf16[16,2,32,2176]{3,2,1,0:T(8,128)(2,1)} %branch_1_fun.14), calls=%async_computation | async-start | bytes 8912896 | tf_op jit(solution)/shard_map/cond/branch_1_fun/all_to_all | solution.py:241
  471.6 58.0 %branch_1_fun.13.refs_1_ = bf16[8,16,512,256]{3,2,1,0:T(8,128)(2,1)} custom-call(bf16[8,2,16,256,256]{4,3,2,1,0:T(8,128)(2,1)} %get-tuple-element.74.maps_ref.refs_0_, bf16[2,16,256,256]{3,2,1,0:T(8,128)(2,1)} %copy.84.vol_ref, bf16[512,512]{1,0:T(8,128)(2,1)S(1)} %get-tuple-element.76.right_ref.refs_4_, bf16[512,512]{1,0:T(8,128)(2,1)S(1)} %get-tuple-element.77.left_ref.refs_5_), custom_call_target="tpu_custom_call" | custom-call | flops 34359738368 | bytes 67108864 | tf_op jit(solution)/shard_map/cond/branch_1_fun/pallas_call | solution.py:146
  558.8 18.0 %branch_1_fun.19 = bf16[256,64,256]{2,1,0:T(8,128)(2,1)} custom-call(s32[256,256]{1,0:T(8,128)} %get-tuple-element.196.rel_ref, bf16[16,2,32,2176]{3,2,1,0:T(8,128)(2,1)} %all-to-all-done.2.in_ref), custom_call_target="tpu_custom_call" | custom-call | flops 4294967296 | bytes 12845056 | tf_op jit(solution)/shard_map/cond/branch_1_fun/pallas_call | solution.py:116
  617.3 18.0 %branch_1_fun.15 = bf16[256,64,256]{2,1,0:T(8,128)(2,1)} custom-call(s32[256,256]{1,0:T(8,128)} %get-tuple-element.196.rel_ref, bf16[16,2,32,2176]{3,2,1,0:T(8,128)(2,1)} %all-to-all-done.in_ref), custom_call_target="tpu_custom_call" | custom-call | flops 4294967296 | bytes 12845056 | tf_op jit(solution)/shard_map/cond/branch_1_fun/pallas_call | solution.py:116
  646.8 19.7 %branch_1_fun.22.refs_6_ = f32[2,16,256,256]{3,2,1,0:T(8,128)} custom-call(bf16[8,2,16,256,256]{4,3,2,1,0:T(8,128)(2,1)} %get-tuple-element.74.maps_ref.refs_0_, bf16[8,16,512,256]{3,2,1,0:T(8,128)(2,1)} %branch_1_fun.13.refs_1_, bf16[2,2,16,256,256]{4,3,2,1,0:T(8,128)(2,1)} %bitcast.85, s32[256,256]{1,0:T(8,128)S(1)} %copy-done.2, ...), custom_call_target="tpu_custom_call" | custom-call | flops 8589934592 | bytes 41943040 | tf_op jit(solution)/shard_map/cond/branch_1_fun/pallas_call | solution.py:191
  666.5 20.9 %branch_1_fun.23.refs_6_ = f32[2,16,256,256]{3,2,1,0:T(8,128)} custom-call(bf16[8,2,16,256,256]{4,3,2,1,0:T(8,128)(2,1)} %get-tuple-element.74.maps_ref.refs_0_, bf16[8,16,512,256]{3,2,1,0:T(8,128)(2,1)} %branch_1_fun.13.refs_1_, bf16[2,2,16,256,256]{4,3,2,1,0:T(8,128)(2,1)} %bitcast.79, s32[256,256]{1,0:T(8,128)S(1)} %copy-done.2, ...), custom_call_target="tpu_custom_call" | custom-call | flops 8589934592 | bytes 41943040 | tf_op jit(solution)/shard_map/cond/branch_1_fun/pallas_call | solution.py:191
  687.4 21.0 %branch_1_fun.24.refs_6_ = f32[2,16,256,256]{3,2,1,0:T(8,128)} custom-call(bf16[8,2,16,256,256]{4,3,2,1,0:T(8,128)(2,1)} %get-tuple-element.74.maps_ref.refs_0_, bf16[8,16,512,256]{3,2,1,0:T(8,128)(2,1)} %branch_1_fun.13.refs_1_, bf16[2,2,16,256,256]{4,3,2,1,0:T(8,128)(2,1)} %bitcast.80, s32[256,256]{1,0:T(8,128)S(1)} %copy-done.2, ...), custom_call_target="tpu_custom_call" | custom-call | flops 8589934592 | bytes 41943040 | tf_op jit(solution)/shard_map/cond/branch_1_fun/pallas_call | solution.py:191
  708.3 21.1 %branch_1_fun.25 = f32[2,16,256,256]{3,2,1,0:T(8,128)} custom-call(bf16[8,2,16,256,256]{4,3,2,1,0:T(8,128)(2,1)} %get-tuple-element.74.maps_ref.refs_0_, bf16[8,16,512,256]{3,2,1,0:T(8,128)(2,1)} %branch_1_fun.13.refs_1_, bf16[2,2,16,256,256]{4,3,2,1,0:T(8,128)(2,1)} %bitcast.84, s32[256,256]{1,0:T(8,128)S(1)} %copy-done.2, ...), custom_call_target="tpu_custom_call" | custom-call | flops 8589934592 | bytes 41943040 | tf_op jit(solution)/shard_map/cond/branch_1_fun/pallas_call | solution.py:191
  742.2 47.6 %collective-permute-done = bf16[2,8,256,256]{3,1,0,2:T(8,128)(2,1)} collective-permute-done((bf16[2,8,256,256]{3,1,0,2:T(8,128)(2,1)S(1)}, bf16[2,8,256,256]{3,1,0,2:T(8,128)(2,1)}, u32[]{:S(2)}, u32[]{:S(2)}) %collective-permute-start) | collective-permute-done | bytes 2097184 | tf_op jit(solution)/shard_map/ppermute | solution.py:282
  794.2 52.9 %all_to_all.52 = bf16[2,8,256,256]{3,1,0,2:T(8,128)(2,1)S(1)} all-to-all(bf16[2,8,256,256]{3,1,0,2:T(8,128)(2,1)S(1)} %subtract_convert_fusion), channel_id=1, replica_groups=mesh['cuts'=16,'coil'=2] {'cuts'}, dimensions={2} | all-to-all | bytes 4194304 | tf_op jit(solution)/shard_map/all_to_all | solution.py:285
  847.8 28.6 %all_to_all.53 = bf16[2,2,8,8,16,256]{5,4,3,2,0,1:T(8,128)(2,1)S(1)} all-to-all(bf16[2,2,8,8,16,256]{5,4,3,2,0,1:T(8,128)(2,1)S(1)} %copy.90), channel_id=1, replica_groups=mesh['cuts'=16,'coil'=2] {'coil'}, dimensions={1} | all-to-all | bytes 4194304 | tf_op jit(solution)/shard_map/all_to_all | solution.py:289
  (58 shorter events, 128.4 us)
Async XLA Ops:
  6.5 7.7 copy-start.5
  6.5 7.9 copy-start.6
  6.5 63.7 %all-gather.2.cloned.1.call-start = ((), (), s32[]{:S(2)}) async-start(), calls=%async_computation.10 | async-start | bytes 6291456 | tf_op jit(solution)/shard_map/all_gather | solution.py:224
  11.8 2.5 copy-start.4
  14.4 1.4 copy-start.3
  150.0 87.9 %all-to-all-start.3 = ((bf16[16,2,32,2176]{3,2,1,0:T(8,128)(2,1)}), bf16[16,2,32,2176]{3,2,1,0:T(8,128)(2,1)}, u32[]{:S(2)}, u32[]{:S(2)}) async-start(bf16[16,2,32,2176]{3,2,1,0:T(8,128)(2,1)} %branch_1_fun.20), calls=%async_computation.3 | async-start | bytes 8912896 | tf_op jit(solution)/shard_map/cond/branch_1_fun/all_to_all | solution.py:241
  237.9 103.0 %all-to-all-start.2 = ((bf16[16,2,32,2176]{3,2,1,0:T(8,128)(2,1)}), bf16[16,2,32,2176]{3,2,1,0:T(8,128)(2,1)}, u32[]{:S(2)}, u32[]{:S(2)}) async-start(bf16[16,2,32,2176]{3,2,1,0:T(8,128)(2,1)} %branch_1_fun.18), calls=%async_computation.2 | async-start | bytes 8912896 | tf_op jit(solution)/shard_map/cond/branch_1_fun/all_to_all | solution.py:241
  340.9 103.0 %all-to-all-start.1 = ((bf16[16,2,32,2176]{3,2,1,0:T(8,128)(2,1)}), bf16[16,2,32,2176]{3,2,1,0:T(8,128)(2,1)}, u32[]{:S(2)}, u32[]{:S(2)}) async-start(bf16[16,2,32,2176]{3,2,1,0:T(8,128)(2,1)} %branch_1_fun.16), calls=%async_computation.1 | async-start | bytes 8912896 | tf_op jit(solution)/shard_map/cond/branch_1_fun/all_to_all | solution.py:241
  443.9 173.4 %all-to-all-start = ((bf16[16,2,32,2176]{3,2,1,0:T(8,128)(2,1)}), bf16[16,2,32,2176]{3,2,1,0:T(8,128)(2,1)}, u32[]{:S(2)}, u32[]{:S(2)}) async-start(bf16[16,2,32,2176]{3,2,1,0:T(8,128)(2,1)} %branch_1_fun.14), calls=%async_computation | async-start | bytes 8912896 | tf_op jit(solution)/shard_map/cond/branch_1_fun/all_to_all | solution.py:241
  635.4 11.4 %copy-start.2 = (s32[256,256]{1,0:T(8,128)S(1)}, s32[256,256]{1,0:T(8,128)}, u32[]{:S(2)}) copy-start(s32[256,256]{1,0:T(8,128)} %get-tuple-element.87.refs_3_) | copy-start | bytes 786436 | tf_op jit(solution)/shard_map/cond
  738.0 3.3 copy-start
  741.6 48.2 %collective-permute-start = (bf16[2,8,256,256]{3,1,0,2:T(8,128)(2,1)S(1)}, bf16[2,8,256,256]{3,1,0,2:T(8,128)(2,1)}, u32[]{:S(2)}, u32[]{:S(2)}) collective-permute-start(bf16[2,8,256,256]{3,1,0,2:T(8,128)(2,1)S(1)} %dynamic-slice_convert_fusion), channel_id=1, source_target_pairs={{0,1},{1,0},{2,3},{3,2},{4,5},{5,4},{6,7},{7,6},{8,9},{9,8},{10,11... | collective-permute-start | bytes 6291464 | tf_op jit(solution)/shard_map/ppermute | solution.py:282
Sparse Core Ops, SparseCore 0:
  10.8 59.4 all-gather.1

commit v2 on v1

v2 whole, which is shorter than its diff:
```python
import functools
import math

import jax
import jax.numpy as jnp
from jax import lax
from jax.experimental import pallas as pl
from jax.experimental.pallas import tpu as pltpu
from jax.sharding import PartitionSpec as P

F32 = jnp.float32
BF16 = jnp.bfloat16
VMEM = 56 * 1024 * 1024


def tables(length):
    counter = jnp.arange(length, dtype=jnp.int32)
    product = counter[:, None] * counter[None, :] % length
    angles = product.astype(jnp.float32) * (2.0 * math.pi / length)
    factor = 1.0 / math.sqrt(length)
    return (
        (jnp.cos(angles) * factor).astype(jnp.bfloat16),
        (jnp.sin(angles) * factor).astype(jnp.bfloat16),
    )


def dot(a, b):
    return lax.dot_general(a, b, (((1,), (0,)), ((), ())), preferred_element_type=F32)


def cost(flops, bytes_accessed):
    return pl.CostEstimate(flops=int(flops), bytes_accessed=int(bytes_accessed), transcendentals=0)


def layout(line_mask, parts):
    edge = line_mask.shape[1]
    slab = line_mask.shape[0] // parts
    slots = edge // 2 * (slab + 1)
    half = edge // 2
    low = [max(half * k - (edge if k % 2 == 0 else half), 0) for k in range(slab)]
    high = [min(half * k + (edge if k % 2 == 0 else 3 * half), slots) for k in range(slab)]
    start_of_window = [min(at, slots - 2 * edge) for at in low]
    low, high, start_of_window = (jnp.array(v, jnp.int32) for v in (low, high, start_of_window))
    sampled = line_mask != 0
    upper = jnp.triu(jnp.ones((edge, edge), BF16), 1)
    rank = jnp.dot(sampled.astype(BF16), upper, preferred_element_type=F32).astype(jnp.int32)
    count = jnp.sum(sampled.astype(jnp.int32), axis=1).reshape(parts, slab)
    before = jnp.cumsum(count, axis=1) - count
    shift = lax.cummax(low[None, :] - before, axis=1)
    start = before + shift
    fits = jnp.all(start + count <= high[None, :])
    place = jnp.where(sampled, start.reshape(-1, 1) + rank, -1)
    window = jnp.tile(start_of_window, parts)[:, None]
    relative = jnp.where(sampled, place - window, -1)
    return fits, place, relative, slots


def compact_kernel(tiles, slots, k_ref, s_ref, t_ref, out_ref, lines_ref):
    slab, _, edge = lines_ref.shape
    rows = out_ref.shape[2]
    parts = out_ref.shape[0]
    step = 32

    @pl.loop(0, edge // step)
    def _(at):
        first = pl.multiple_of(at * step, step)
        for r in range(2):
            block = jnp.swapaxes(k_ref[0, r, pl.ds(first, step)], 0, 1)
            lines_ref[:, pl.ds(pl.multiple_of(r * edge + first, step), step), :] = block

    def tile(at, width):
        picked = None
        for j in range(4):
            k = jnp.clip(2 * at - 1 + j, 0, slab - 1)
            term = dot(lines_ref[k], s_ref[at, j][:, :width])
            picked = term if picked is None else picked + term
        moved = dot(t_ref[...], picked.astype(BF16)).astype(BF16)
        return moved.reshape(parts, rows, width)

    @pl.loop(0, tiles)
    def _(at):
        out_ref[:, 0, :, pl.ds(pl.multiple_of(at * edge, edge), edge)] = tile(at, edge)

    rest = slots - tiles * edge
    if rest:
        out_ref[:, 0, :, tiles * edge :] = tile(tiles, rest)


def compact(data, first_coil, coils, select, table, parts, slots):
    _, _, edge, slab, _ = data.shape
    tiles = slots // edge
    rows = 2 * edge // parts
    return pl.pallas_call(
        functools.partial(compact_kernel, tiles, slots),
        grid=(coils,),
        in_specs=[
            pl.BlockSpec((1, 2, edge, slab, edge), lambda c: (first_coil + c, 0, 0, 0, 0)),
            pl.BlockSpec(select.shape, lambda c: (0, 0, 0, 0)),
            pl.BlockSpec(table.shape, lambda c: (0, 0)),
        ],
        out_specs=pl.BlockSpec((parts, 1, rows, slots), lambda c: (0, c, 0, 0)),
        out_shape=jax.ShapeDtypeStruct((parts, coils, rows, slots), BF16),
        scratch_shapes=[pltpu.VMEM((slab, 2 * edge, edge), BF16)],
        compiler_params=pltpu.CompilerParams(vmem_limit_bytes=VMEM),
        cost_estimate=cost(
            coils * 4 * slots * edge * 6 * edge, 4 * coils * edge * (slab * edge + slots)
        ),
    )(data, select, table)


def expand_kernel(windows, rel_ref, in_ref, out_ref, lines_ref):
    edge = rel_ref.shape[1]
    slab, rows, _ = lines_ref.shape
    place = lax.broadcasted_iota(jnp.int32, (2 * edge, edge), 0)
    for k, at in enumerate(windows):
        chosen = jnp.where(place == rel_ref[k : k + 1, :], 1.0, 0.0).astype(BF16)
        source = in_ref[0, :, :, at : at + 2 * edge].reshape(rows, 2 * edge)
        lines_ref[k] = dot(source, chosen).astype(BF16)
    for at in range(0, rows, 16):
        out_ref[at : at + 16] = jnp.swapaxes(lines_ref[:, at : at + 16, :], 0, 1)


def expand(arrived, relative, windows):
    parts, coils, rows, slots = arrived.shape
    edge = relative.shape[1]
    slab = relative.shape[0] // parts
    rows = coils * rows
    return pl.pallas_call(
        functools.partial(expand_kernel, windows),
        grid=(parts,),
        in_specs=[
            pl.BlockSpec((slab, edge), lambda d: (d, 0)),
            pl.BlockSpec((1,) + arrived.shape[1:], lambda d: (d, 0, 0, 0)),
        ],
        out_specs=pl.BlockSpec((rows, slab, edge), lambda d: (0, d, 0)),
        out_shape=jax.ShapeDtypeStruct((rows, parts * slab, edge), BF16),
        scratch_shapes=[pltpu.VMEM((slab, rows, edge), BF16)],
        compiler_params=pltpu.CompilerParams(vmem_limit_bytes=VMEM),
        cost_estimate=cost(parts * slab * rows * edge * edge * 4, 2 * (arrived.size + parts * slab * rows * edge)),
    )(relative, arrived)


def forward_kernel(maps_ref, vol_ref, right_ref, left_ref, out_ref):
    edge = vol_ref.shape[3]
    for i in range(vol_ref.shape[1]):
        map_real, map_imag = maps_ref[0, 0, i].astype(F32), maps_ref[0, 1, i].astype(F32)
        vol_real, vol_imag = vol_ref[0, i].astype(F32), vol_ref[1, i].astype(F32)
        real = (map_real * vol_real - map_imag * vol_imag).astype(BF16)
        imag = (map_real * vol_imag + map_imag * vol_real).astype(BF16)
        along = dot(jnp.concatenate([real, imag], axis=1), right_ref[...]).astype(BF16)
        stacked = jnp.concatenate([along[:, :edge], along[:, edge:]], axis=0)
        out_ref[0, i] = dot(left_ref[...], stacked).astype(BF16)


def forward(maps, volume, right, left, group):
    coils, _, deep, edge, _ = maps.shape
    return pl.pallas_call(
        forward_kernel,
        grid=(deep // group, coils),
        in_specs=[
            pl.BlockSpec((1, 2, group, edge, edge), lambda x, c: (c, 0, x, 0, 0)),
            pl.BlockSpec((2, group, edge, edge), lambda x, c: (0, x, 0, 0)),
            pl.BlockSpec(right.shape, lambda x, c: (0, 0)),
            pl.BlockSpec(left.shape, lambda x, c: (0, 0)),
        ],
        out_specs=pl.BlockSpec((1, group, 2 * edge, edge), lambda x, c: (c, x, 0, 0)),
        out_shape=jax.ShapeDtypeStruct((coils, deep, 2 * edge, edge), BF16),
        compiler_params=pltpu.CompilerParams(vmem_limit_bytes=VMEM),
        cost_estimate=cost(coils * deep * edge**3 * 16, 4 * maps.size),
    )(maps, volume, right, left)


def backward_kernel(first, at_ref, *refs):
    if first:
        maps_ref, k_ref, h_ref, mask_ref, left_ref, right_ref, out_ref, sum_ref = refs
    else:
        maps_ref, k_ref, h_ref, mask_ref, left_ref, right_ref, before_ref, out_ref, sum_ref = refs
    edge = mask_ref.shape[1]
    sampled = mask_ref[...].astype(F32)
    sampled = jnp.concatenate([sampled, sampled], axis=0)

    @pl.when(pl.program_id(1) == 0)
    def _():
        sum_ref[...] = jnp.zeros_like(sum_ref) if first else before_ref[...]

    for i in range(k_ref.shape[1]):
        hybrid = h_ref[0, :, i].reshape(2 * edge, edge)
        residual = (sampled * (k_ref[0, i].astype(F32) - hybrid.astype(F32))).astype(BF16)
        back = dot(left_ref[...], residual).astype(BF16)
        back = jnp.concatenate([back[:edge], back[edge:]], axis=1)
        back = dot(back, right_ref[...]).astype(BF16).astype(F32)
        real, imag = back[:, :edge], back[:, edge:]
        map_real, map_imag = maps_ref[0, 0, i].astype(F32), maps_ref[0, 1, i].astype(F32)
        sum_ref[0, i] += map_real * real + map_imag * imag
        sum_ref[1, i] += map_real * imag - map_imag * real

    @pl.when(pl.program_id(1) == pl.num_programs(1) - 1)
    def _():
        out_ref[...] = sum_ref[...].astype(out_ref.dtype)


def backward(maps, coil_kspace, hybrid, line_mask, left, right, before, first_coil, first_x, count, group, kind):
    coils, _, _, edge, _ = hybrid.shape
    group = min(group, count)
    first = before is None
    block = (2, group, edge, edge)
    spec = pltpu.PrefetchScalarGridSpec(
        num_scalar_prefetch=1,
        grid=(count // group, coils),
        in_specs=[
            pl.BlockSpec((1, 2, group, edge, edge), lambda x, c, at: (first_coil + c, 0, at[0] + x, 0, 0)),
            pl.BlockSpec((1, group, 2 * edge, edge), lambda x, c, at: (first_coil + c, at[0] + x, 0, 0)),
            pl.BlockSpec((1, 2, group, edge, edge), lambda x, c, at: (c, 0, at[0] + x, 0, 0)),
            pl.BlockSpec(line_mask.shape, lambda x, c, at: (0, 0)),
            pl.BlockSpec(left.shape, lambda x, c, at: (0, 0)),
            pl.BlockSpec(right.shape, lambda x, c, at: (0, 0)),
        ]
        + ([] if first else [pl.BlockSpec(block, lambda x, c, at: (0, at[0] + x, 0, 0))]),
        out_specs=pl.BlockSpec(block, lambda x, c, at: (0, x, 0, 0)),
        scratch_shapes=[pltpu.VMEM(block, F32)],
    )
    start = jnp.full((1,), first_x // group, jnp.int32)
    return pl.pallas_call(
        functools.partial(backward_kernel, first),
        grid_spec=spec,
        out_shape=jax.ShapeDtypeStruct((2, count, edge, edge), kind),
        compiler_params=pltpu.CompilerParams(vmem_limit_bytes=VMEM),
        cost_estimate=cost(coils * count * edge**3 * 16, count * edge**2 * (12 * coils + 16)),
    )(start, maps, coil_kspace, hybrid, line_mask, left, right, *([] if first else [before]))


def body(coil_groups, volume, coil_maps, kspace, line_mask):
    coils, _, deep, edge, _ = coil_maps.shape
    slab = kspace.shape[3]
    parts = edge // slab
    me = lax.axis_index("cuts")
    mine = lax.axis_index("coil")
    cos_table, sin_table = tables(edge)
    turn = jnp.block([[cos_table, sin_table], [-sin_table, cos_table]])
    turn_back = jnp.block([[cos_table, -sin_table], [sin_table, cos_table]])
    by_destination = turn_back.reshape(2, parts, deep, 2 * edge).transpose(1, 0, 2, 3).reshape(2 * edge, 2 * edge)
    fits, place, relative, slots = layout(line_mask, parts)
    half = edge // 2
    windows = tuple(
        min(max(half * k - (edge if k % 2 == 0 else half), 0), slots - 2 * edge) for k in range(slab)
    )
    if coils % 2 == 0 and coils > 2:
        sizes = [1] + [2] * (coils // 2 - 1) + [1]
    else:
        sizes = [1] * coils
    firsts = [sum(sizes[:i]) for i in range(len(sizes))]
    group = min(4, deep)

    def step(pack, unpack):
        arrived = [exchange(pack(0))]
        full_slab = lax.all_gather(volume, "coil", axis=2, tiled=True)
        coil_kspace = forward(coil_maps, full_slab, turn_back, turn, group)
        total = None
        for i in range(1, len(sizes) + 1):
            if i < len(sizes):
                sent = pack(i)
                if i == 2:
                    sent, coil_kspace = lax.optimization_barrier((sent, coil_kspace))
                elif i > 2:
                    sent, total = lax.optimization_barrier((sent, total))
                arrived.append(exchange(sent))
            hybrid = unpack(i - 1, arrived[i - 1])
            at = functools.partial(
                backward, coil_maps, coil_kspace, hybrid, line_mask, turn_back, turn, total, firsts[i - 1]
            )
            if i < len(sizes):
                total = at(0, deep, group, F32)
        return finish(coil_groups, mine, full_slab, at, deep)

    def exchange(sent):
        return lax.all_to_all(sent, "cuts", split_axis=0, concat_axis=0, tiled=True)

    def send_sampled():
        own = lax.dynamic_slice_in_dim(place, me * slab, slab, 0)
        tiles = -(-slots // edge)
        member = jnp.clip(2 * jnp.arange(tiles)[:, None] - 1 + jnp.arange(4)[None, :], -1, slab)
        padded = jnp.pad(own, ((1, 1), (0, 0)), constant_values=-1)
        offset = padded[member + 1] - edge * jnp.arange(tiles)[:, None, None]
        select = (offset[..., None] == jnp.arange(edge)).astype(BF16)

        def pack(i):
            return compact(kspace, firsts[i], sizes[i], select, by_destination, parts, slots)

        def unpack(i, arrived):
            return expand(arrived, relative, windows).reshape(sizes[i], 2, deep, edge, edge)

        return step(pack, unpack)

    def send_all():
        def pack(i):
            part = lax.slice_in_dim(kspace, firsts[i], firsts[i] + sizes[i], axis=0)
            data = part.transpose(0, 3, 1, 2, 4).reshape(sizes[i], slab, 2 * edge, edge)
            moved = jnp.einsum("xn,ckny->xcky", by_destination, data, preferred_element_type=F32).astype(BF16)
            return moved.reshape(parts, 2, deep, sizes[i], slab, edge)

        def unpack(i, arrived):
            return arrived.transpose(3, 1, 2, 0, 4, 5).reshape(sizes[i], 2, deep, edge, edge)

        return step(pack, unpack)

    return lax.cond(fits, send_sampled, send_all)


def finish(coil_groups, mine, full_slab, gradient, deep):
    edge = full_slab.shape[2]
    parts = edge // deep
    pieces = min(2, deep // coil_groups)
    share = deep // coil_groups // pieces
    rings = [[(i, (i + s) % coil_groups) for i in range(coil_groups)] for s in range(coil_groups)]
    away = [
        [
            lax.ppermute(
                gradient((p * coil_groups + lax.rem(mine + s, coil_groups)) * share, share, share, BF16), "coil", rings[s]
            )
            for s in range(1, coil_groups)
        ]
        for p in range(pieces)
    ]
    out = []
    for p in range(pieces):
        at = (p * coil_groups + mine) * share
        summed = gradient(at, share, share, F32)
        for term in away[p]:
            summed = summed + term.astype(F32)
        base = lax.dynamic_slice_in_dim(full_slab, at, share, 1).astype(F32)
        updated = (base - 0.5 * summed).astype(BF16)
        updated = lax.all_to_all(updated, "cuts", split_axis=2, concat_axis=1, tiled=True)
        slab = updated.shape[2]
        updated = updated.reshape(2, coil_groups, parts // coil_groups, share, slab, edge)
        whole = jnp.zeros((2, parts // coil_groups, coil_groups, share, slab, edge), BF16)
        for s in range(coil_groups):
            to = lax.rem(mine + s, coil_groups)
            source = lax.rem(mine + coil_groups - s, coil_groups)
            moved = lax.dynamic_index_in_dim(updated, to, 1, keepdims=False)
            if s:
                moved = lax.ppermute(moved, "coil", rings[s])
            whole = lax.dynamic_update_index_in_dim(whole, moved[:, :, None], source, 2)
        out.append(whole)
    out = jnp.stack(out, axis=2)
    return out.reshape(2, edge // coil_groups, slab, edge)


def solution(mesh):
    placed = (
        P(None, "cuts", "coil", None),
        P("coil", None, "cuts", None, None),
        P("coil", None, None, "cuts", None),
        P(),
    )
    return jax.shard_map(
        functools.partial(body, mesh.shape["coil"]),
        mesh=mesh,
        in_specs=placed,
        out_specs=P(None, "coil", "cuts", None),
        check_vma=False,
    )
```

time: 893 us -> 668 us (0.75)
  local copies, waits for them, and re-layouts: 119 us -> 14.4 us
  waiting for transfers between devices: 286 us -> 184 us
  blocking collectives: 81.5 us -> 0 us
  Pallas kernels: 296 us -> 342 us
  starting transfers between devices: 68.9 us -> 79.8 us
    all_to_all x4 -> x7, waiting for transfers between devices: 184 us -> 95.7 us  [the longest x5 51.6 us: exchange(): return lax.all_to_all(sent, 'cuts', split_axis=0, concat_axis=0, tiled=True)]
    all_to_all x2 -> x0, blocking collectives: 81.5 us -> none  [the longest x1 52.9 us: finish(): lax.all_to_all(updated, 'cuts', split_axis=2, concat_axis=1, tiled=True)]
    pallas_call x4 -> x0, local copies, waits for them, and re-layouts: 45.6 us -> none  [expand(): pl.pallas_call(functools.partial(expand_kernel, windows), grid=(parts,),...]
    another operation x2, local copies, waits for them, and re-layouts: 29.7 us -> 0.22 us  [finish(): out = jnp.stack(out, axis=2)]
    slice x1 -> x0, local copies, waits for them, and re-layouts: 22.8 us -> none  [send_sampled(): part = lax.slice_in_dim(kspace, i * each, (i + 1) * each, axis=0)]
    pallas_call x4 -> x5, Pallas kernels: 71.5 us -> 91.4 us  [expand(): pl.pallas_call(functools.partial(expand_kernel, windows), grid=(parts,),...]
    all_gather x1, waiting for transfers between devices: 54.2 us -> 36.8 us  [step(): full_slab = lax.all_gather(volume, 'coil', axis=2, tiled=True)]
    pallas_call x4 -> x8, Pallas kernels: 82.7 us -> 96.7 us  [backward(): pl.pallas_call(functools.partial(backward_kernel, first), grid_spec=spec,...]
  transfers between devices with their start and end apart: 6 -> 12, of which waited for: 5 -> 10; matrix products, arithmetic and copies ran while one was open for 5% -> 1% of each run, Pallas kernels for 20% -> 47%
where the time goes in v2:
time: 668 us; the launch traced here: 655 us
  Pallas kernels  342 us (51%)
  waiting for transfers between devices  184 us (28%)
  starting transfers between devices  79.8 us (12%)
  between operations  14.6 us (2%)
  local copies, waits for them, and re-layouts  14.4 us (2%)
  other arithmetic  14 us (2%)
    pallas_call x8, Pallas kernels, backward(): pl.pallas_call(functools.partial(backward_kernel, first), grid_spec=spec,...  96.7 us
    pallas_call x5, Pallas kernels, compact(): pl.pallas_call(functools.partial(compact_kernel, tiles, slots), grid=(coi...  96.3 us
    pallas_call x5, Pallas kernels, expand(): pl.pallas_call(functools.partial(expand_kernel, windows), grid=(parts,),...  91.4 us
    pallas_call x1, Pallas kernels, forward(): pl.pallas_call(forward_kernel, grid=(deep // group, coils), in_specs=[pl....  58 us
    all_to_all x5, starting transfers between devices, exchange(): return lax.all_to_all(sent, 'cuts', split_axis=0, concat_axis=0, tiled=True)  57.4 us
    all_to_all x5, waiting for transfers between devices, exchange(): return lax.all_to_all(sent, 'cuts', split_axis=0, concat_axis=0, tiled=True)  51.6 us
    all_to_all x2, waiting for transfers between devices, finish(): lax.all_to_all(updated, 'cuts', split_axis=2, concat_axis=1, tiled=True)  44.1 us
    all_gather x1, waiting for transfers between devices, step(): full_slab = lax.all_gather(volume, 'coil', axis=2, tiled=True)  36.8 us
  transfers between devices with their start and end apart: 12, of which 10 were waited for; matrix products, arithmetic and copies ran while one was open for 1% of the time, Pallas kernels for 47%

profile of v2, /device:TPU:0, one launch (start us, length us, event | category | flops | bytes accessed | tf_op | source)
XLA Modules:
  0.0 655.5 jit_solution(7204265859394644548)
XLA Ops:
  13.6 633.2 %conditional.1 = (bf16[2,128,16,256]{3,2,1,0:T(8,128)(2,1)S(1)}) conditional(s32[]{:T(128)} %convert_element_type.102, (bf16[2,16,128,256]{3,2,1,0:T(8,128)(2,1)}, s32[]{:T(128)}, bf16[8,2,256,16,256]{4,3,2,1,0:T(8,128)(2,1)}, bf16[512,512]{1,0:T(8,128)(2,1)S(1)}, bf16[8,2,16,256,256]{4,3,2,1,0:T(8,128)(2,1)}, ...), branch_computations={%region_4.5_spmd, %region_5.6_spmd} | conditional | flops 113292091392 | bytes 785908224 | solution.py:306
  26.9 13.9 %branch_1_fun.26 = bf16[16,1,32,2176]{3,2,1,0:T(8,128)(2,1)} custom-call(bf16[8,2,256,16,256]{4,3,2,1,0:T(8,128)(2,1)} %get-tuple-element.88.k_ref, bf16[9,4,256,256]{3,2,1,0:T(8,128)(2,1)} %fusion.5.s_ref, bf16[512,512]{1,0:T(8,128)(2,1)S(1)} %get-tuple-element.95.t_ref), custom_call_target="tpu_custom_call" | custom-call | flops 3422552064 | bytes 6422528 | tf_op jit(solution)/shard_map/cond/branch_1_fun/pallas_call | solution.py:93
  48.3 22.9 %branch_1_fun.24 = bf16[16,2,32,2176]{3,2,1,0:T(8,128)(2,1)} custom-call(bf16[8,2,256,16,256]{4,3,2,1,0:T(8,128)(2,1)} %get-tuple-element.88.k_ref, bf16[9,4,256,256]{3,2,1,0:T(8,128)(2,1)} %fusion.5.s_ref, bf16[512,512]{1,0:T(8,128)(2,1)S(1)} %get-tuple-element.95.t_ref), custom_call_target="tpu_custom_call" | custom-call | flops 6845104128 | bytes 12845056 | tf_op jit(solution)/shard_map/cond/branch_1_fun/pallas_call | solution.py:93
  71.1 20.6 %all-to-all-done.2.in_ref = bf16[16,1,32,2176]{3,2,1,0:T(8,128)(2,1)} async-done(((bf16[16,1,32,2176]{3,2,1,0:T(8,128)(2,1)}), bf16[16,1,32,2176]{3,2,1,0:T(8,128)(2,1)}, u32[]{:S(2)}, u32[]{:S(2)}) %all-to-all-start.2) | async-done | bytes 2228256 | tf_op jit(solution)/shard_map/cond/branch_1_fun/all_to_all | solution.py:276
  91.7 11.8 %all-to-all-start.1 = ((bf16[16,2,32,2176]{3,2,1,0:T(8,128)(2,1)}), bf16[16,2,32,2176]{3,2,1,0:T(8,128)(2,1)}, u32[]{:S(2)}, u32[]{:S(2)}) async-start(bf16[16,2,32,2176]{3,2,1,0:T(8,128)(2,1)} %branch_1_fun.24), calls=%async_computation.1 | async-start | bytes 8912896 | tf_op jit(solution)/shard_map/cond/branch_1_fun/all_to_all | solution.py:276
  104.2 22.9 %branch_1_fun.19 = bf16[16,2,32,2176]{3,2,1,0:T(8,128)(2,1)} custom-call(bf16[8,2,256,16,256]{4,3,2,1,0:T(8,128)(2,1)} %get-tuple-element.88.k_ref, bf16[9,4,256,256]{3,2,1,0:T(8,128)(2,1)} %fusion.5.s_ref, bf16[512,512]{1,0:T(8,128)(2,1)S(1)} %get-tuple-element.95.t_ref), custom_call_target="tpu_custom_call" | custom-call | flops 6845104128 | bytes 12845056 | tf_op jit(solution)/shard_map/cond/branch_1_fun/pallas_call | solution.py:93
  127.1 36.8 %all-gather.5.cloned.1.call-done.vol_ref = bf16[2,16,256,256]{3,2,1,0:T(8,128)(2,1)} async-done(((bf16[2,16,128,256]{3,2,1,0:T(8,128)(2,1)}), bf16[2,16,256,256]{3,2,1,0:T(8,128)(2,1)}) %all-gather.5.cloned.1.call-update) | async-done | bytes 4194320 | tf_op jit(solution)/shard_map/cond/branch_1_fun/all_gather | solution.py:256
  163.9 58.0 %branch_1_fun.20.refs_1_ = bf16[8,16,512,256]{3,2,1,0:T(8,128)(2,1)} custom-call(bf16[8,2,16,256,256]{4,3,2,1,0:T(8,128)(2,1)} %get-tuple-element.87.maps_ref.refs_0_, bf16[2,16,256,256]{3,2,1,0:T(8,128)(2,1)} %all-gather.5.cloned.1.call-done.vol_ref, bf16[512,512]{1,0:T(8,128)(2,1)S(1)} %get-tuple-element.96.right_ref.refs_4_, ...), custom_call_target="tpu_custom_call" | custom-call | flops 34359738368 | bytes 67108864 | tf_op jit(solution)/shard_map/cond/branch_1_fun/pallas_call | solution.py:157
  227.8 22.9 %branch_1_fun.23 = bf16[16,2,32,2176]{3,2,1,0:T(8,128)(2,1)} custom-call(bf16[8,2,256,16,256]{4,3,2,1,0:T(8,128)(2,1)} %get-tuple-element.88.k_ref, bf16[9,4,256,256]{3,2,1,0:T(8,128)(2,1)} %fusion.5.s_ref, bf16[512,512]{1,0:T(8,128)(2,1)S(1)} %get-tuple-element.95.t_ref), custom_call_target="tpu_custom_call" | custom-call | flops 6845104128 | bytes 12845056 | tf_op jit(solution)/shard_map/cond/branch_1_fun/pallas_call | solution.py:93
  250.6 17.2 %branch_1_fun.27 = bf16[32,256,256]{2,1,0:T(8,128)(2,1)} custom-call(s32[256,256]{1,0:T(8,128)} %get-tuple-element.133.rel_ref, bf16[16,1,32,2176]{3,2,1,0:T(8,128)(2,1)} %all-to-all-done.2.in_ref), custom_call_target="tpu_custom_call" | custom-call | flops 2147483648 | bytes 6422528 | tf_op jit(solution)/shard_map/cond/branch_1_fun/pallas_call | solution.py:128
  278.9 19.0 %branch_1_fun.25 = bf16[64,256,256]{2,1,0:T(8,128)(2,1)} custom-call(s32[256,256]{1,0:T(8,128)} %get-tuple-element.133.rel_ref, bf16[16,2,32,2176]{3,2,1,0:T(8,128)(2,1)} %all-to-all-done.1.in_ref), custom_call_target="tpu_custom_call" | custom-call | flops 4294967296 | bytes 12845056 | tf_op jit(solution)/shard_map/cond/branch_1_fun/pallas_call | solution.py:128
  298.0 21.3 %branch_1_fun.29.refs_6_ = f32[2,16,256,256]{3,2,1,0:T(8,128)} custom-call(s32[1]{0:T(128)} %constant.209.clone.at_ref, bf16[8,2,16,256,256]{4,3,2,1,0:T(8,128)(2,1)} %get-tuple-element.87.maps_ref.refs_0_, bf16[8,16,512,256]{3,2,1,0:T(8,128)(2,1)} %branch_1_fun.20.refs_1_, bf16[2,2,16,256,256]{4,3,2,1,0:T(8,128)(2,1)} %bitcast.141, ...), custom_call_target="tpu_custom_call" | custom-call | flops 8589934592 | bytes 41943040 | tf_op jit(solution)/shard_map/cond/branch_1_fun/pallas_call | solution.py:223
  319.3 11.5 %all-to-all-start.4 = ((bf16[16,2,32,2176]{3,2,1,0:T(8,128)(2,1)}), bf16[16,2,32,2176]{3,2,1,0:T(8,128)(2,1)}, u32[]{:S(2)}, u32[]{:S(2)}) async-start(bf16[16,2,32,2176]{3,2,1,0:T(8,128)(2,1)} %branch_1_fun.23), calls=%async_computation.4 | async-start | bytes 8912896 | tf_op jit(solution)/shard_map/cond/branch_1_fun/all_to_all | solution.py:276
  330.8 13.9 %branch_1_fun.21 = bf16[16,1,32,2176]{3,2,1,0:T(8,128)(2,1)} custom-call(bf16[8,2,256,16,256]{4,3,2,1,0:T(8,128)(2,1)} %get-tuple-element.88.k_ref, bf16[9,4,256,256]{3,2,1,0:T(8,128)(2,1)} %fusion.5.s_ref, bf16[512,512]{1,0:T(8,128)(2,1)S(1)} %copy-done.3), custom_call_target="tpu_custom_call" | custom-call | flops 3422552064 | bytes 6422528 | tf_op jit(solution)/shard_map/cond/branch_1_fun/pallas_call | solution.py:93
  344.6 19.0 %branch_1_fun.22 = bf16[64,256,256]{2,1,0:T(8,128)(2,1)} custom-call(s32[256,256]{1,0:T(8,128)} %get-tuple-element.133.rel_ref, bf16[16,2,32,2176]{3,2,1,0:T(8,128)(2,1)} %all-to-all-done.in_ref), custom_call_target="tpu_custom_call" | custom-call | flops 4294967296 | bytes 12845056 | tf_op jit(solution)/shard_map/cond/branch_1_fun/pallas_call | solution.py:128
  363.7 21.3 %branch_1_fun.30.refs_6_ = f32[2,16,256,256]{3,2,1,0:T(8,128)} custom-call(s32[1]{0:T(128)} %constant.209.clone.at_ref, bf16[8,2,16,256,256]{4,3,2,1,0:T(8,128)(2,1)} %get-tuple-element.87.maps_ref.refs_0_, bf16[8,16,512,256]{3,2,1,0:T(8,128)(2,1)} %branch_1_fun.20.refs_1_, bf16[2,2,16,256,256]{4,3,2,1,0:T(8,128)(2,1)} %bitcast.142, ...), custom_call_target="tpu_custom_call" | custom-call | flops 8589934592 | bytes 41943040 | tf_op jit(solution)/shard_map/cond/branch_1_fun/pallas_call | solution.py:223
  385.0 28.0 %all-to-all-done.4.in_ref = bf16[16,2,32,2176]{3,2,1,0:T(8,128)(2,1)} async-done(((bf16[16,2,32,2176]{3,2,1,0:T(8,128)(2,1)}), bf16[16,2,32,2176]{3,2,1,0:T(8,128)(2,1)}, u32[]{:S(2)}, u32[]{:S(2)}) %all-to-all-start.4) | async-done | bytes 4456480 | tf_op jit(solution)/shard_map/cond/branch_1_fun/all_to_all | solution.py:276
  413.0 20.9 %all-to-all-start.3 = ((bf16[16,1,32,2176]{3,2,1,0:T(8,128)(2,1)}), bf16[16,1,32,2176]{3,2,1,0:T(8,128)(2,1)S(1)}, u32[]{:S(2)}, u32[]{:S(2)}) async-start(bf16[16,1,32,2176]{3,2,1,0:T(8,128)(2,1)} %branch_1_fun.21), calls=%async_computation.3 | async-start | bytes 4456448 | tf_op jit(solution)/shard_map/cond/branch_1_fun/all_to_all | solution.py:276
  433.9 19.0 %branch_1_fun.32 = bf16[64,256,256]{2,1,0:T(8,128)(2,1)} custom-call(s32[256,256]{1,0:T(8,128)} %get-tuple-element.133.rel_ref, bf16[16,2,32,2176]{3,2,1,0:T(8,128)(2,1)} %all-to-all-done.4.in_ref), custom_call_target="tpu_custom_call" | custom-call | flops 4294967296 | bytes 12845056 | tf_op jit(solution)/shard_map/cond/branch_1_fun/pallas_call | solution.py:128
  453.0 21.3 %branch_1_fun.33.refs_6_ = f32[2,16,256,256]{3,2,1,0:T(8,128)} custom-call(s32[1]{0:T(128)} %constant.209.clone.at_ref, bf16[8,2,16,256,256]{4,3,2,1,0:T(8,128)(2,1)} %get-tuple-element.87.maps_ref.refs_0_, bf16[8,16,512,256]{3,2,1,0:T(8,128)(2,1)} %branch_1_fun.20.refs_1_, bf16[2,2,16,256,256]{4,3,2,1,0:T(8,128)(2,1)} %bitcast.140, ...), custom_call_target="tpu_custom_call" | custom-call | flops 8589934592 | bytes 41943040 | tf_op jit(solution)/shard_map/cond/branch_1_fun/pallas_call | solution.py:223
  478.6 17.1 %branch_1_fun.31 = bf16[32,256,256]{2,1,0:T(8,128)(2,1)} custom-call(s32[256,256]{1,0:T(8,128)} %get-tuple-element.133.rel_ref, bf16[16,1,32,2176]{3,2,1,0:T(8,128)(2,1)} %copy-done.7), custom_call_target="tpu_custom_call" | custom-call | flops 2147483648 | bytes 6422528 | tf_op jit(solution)/shard_map/cond/branch_1_fun/pallas_call | solution.py:128
  527.2 22.4 %collective-permute-done.2 = bf16[2,4,256,256]{3,2,1,0:T(8,128)(2,1)} collective-permute-done((bf16[2,4,256,256]{3,2,1,0:T(8,128)(2,1)}, bf16[2,4,256,256]{3,2,1,0:T(8,128)(2,1)}, u32[]{:S(2)}, u32[]{:S(2)}) %collective-permute-start.2) | collective-permute-done | bytes 1048608 | tf_op jit(solution)/shard_map/cond/branch_1_fun/ppermute | solution.py:317
  567.9 21.1 %all-to-all-done.6 = bf16[2,4,256,256]{3,1,0,2:T(4,128)(2,1)S(1)} async-done(((bf16[2,4,256,256]{3,1,0,2:T(4,128)(2,1)}), bf16[2,4,256,256]{3,1,0,2:T(4,128)(2,1)S(1)}, u32[]{:S(2)}, u32[]{:S(2)}) %all-to-all-start.6) | async-done | bytes 1048608 | tf_op jit(solution)/shard_map/cond/branch_1_fun/all_to_all | solution.py:332
  595.9 22.9 %all-to-all-done.5 = bf16[2,4,256,256]{3,1,0,2:T(4,128)(2,1)S(1)} async-done(((bf16[2,4,256,256]{3,1,0,2:T(4,128)(2,1)}), bf16[2,4,256,256]{3,1,0,2:T(4,128)(2,1)S(1)}, u32[]{:S(2)}, u32[]{:S(2)}) %all-to-all-start.5) | async-done | bytes 1048608 | tf_op jit(solution)/shard_map/cond/branch_1_fun/all_to_all | solution.py:332
  (80 shorter events, 129.3 us)
Async XLA Ops:
  7.6 0.5 copy-start.11
  8.4 0.7 copy-start.10
  9.2 4.2 copy-start.9
  18.9 208.8 %copy-start.2 = (bf16[512,512]{1,0:T(8,128)(2,1)}, bf16[512,512]{1,0:T(8,128)(2,1)S(1)}, u32[]{:S(2)}) copy-start(bf16[512,512]{1,0:T(8,128)(2,1)S(1)} %get-tuple-element.95.t_ref) | copy-start | bytes 1572868 | tf_op jit(solution)/shard_map/cond
  40.8 50.9 %all-to-all-start.2 = ((bf16[16,1,32,2176]{3,2,1,0:T(8,128)(2,1)}), bf16[16,1,32,2176]{3,2,1,0:T(8,128)(2,1)}, u32[]{:S(2)}, u32[]{:S(2)}) async-start(bf16[16,1,32,2176]{3,2,1,0:T(8,128)(2,1)} %branch_1_fun.26), calls=%async_computation.2 | async-start | bytes 4456448 | tf_op jit(solution)/shard_map/cond/branch_1_fun/all_to_all | solution.py:276
  91.7 130.2 %all-to-all-start.1 = ((bf16[16,2,32,2176]{3,2,1,0:T(8,128)(2,1)}), bf16[16,2,32,2176]{3,2,1,0:T(8,128)(2,1)}, u32[]{:S(2)}, u32[]{:S(2)}) async-start(bf16[16,2,32,2176]{3,2,1,0:T(8,128)(2,1)} %branch_1_fun.24), calls=%async_computation.1 | async-start | bytes 8912896 | tf_op jit(solution)/shard_map/cond/branch_1_fun/all_to_all | solution.py:276
  103.5 60.4 %all-gather.5.cloned.1.call-start = ((), (), s32[]{:S(2)}) async-start(), calls=%async_computation.15 | async-start | bytes 6291456 | tf_op jit(solution)/shard_map/cond/branch_1_fun/all_gather | solution.py:256
  221.9 97.4 %all-to-all-start = ((bf16[16,2,32,2176]{3,2,1,0:T(8,128)(2,1)}), bf16[16,2,32,2176]{3,2,1,0:T(8,128)(2,1)}, u32[]{:S(2)}, u32[]{:S(2)}) async-start(bf16[16,2,32,2176]{3,2,1,0:T(8,128)(2,1)} %branch_1_fun.19), calls=%async_computation | async-start | bytes 8912896 | tf_op jit(solution)/shard_map/cond/branch_1_fun/all_to_all | solution.py:276
  250.6 17.2 %copy-start.1 = (s32[256,256]{1,0:T(8,128)S(1)}, s32[256,256]{1,0:T(8,128)}, u32[]{:S(2)}) copy-start(s32[256,256]{1,0:T(8,128)} %get-tuple-element.101.refs_3_) | copy-start | bytes 786436 | tf_op jit(solution)/shard_map/cond
  319.3 11.5 %copy-start.3 = (bf16[512,512]{1,0:T(8,128)(2,1)S(1)}, bf16[512,512]{1,0:T(8,128)(2,1)}, u32[]{:S(2)}) copy-start(bf16[512,512]{1,0:T(8,128)(2,1)} %copy-done.2) | copy-start | bytes 1572868 | tf_op jit(solution)/shard_map/cond
  319.3 93.7 %all-to-all-start.4 = ((bf16[16,2,32,2176]{3,2,1,0:T(8,128)(2,1)}), bf16[16,2,32,2176]{3,2,1,0:T(8,128)(2,1)}, u32[]{:S(2)}, u32[]{:S(2)}) async-start(bf16[16,2,32,2176]{3,2,1,0:T(8,128)(2,1)} %branch_1_fun.23), calls=%async_computation.4 | async-start | bytes 8912896 | tf_op jit(solution)/shard_map/cond/branch_1_fun/all_to_all | solution.py:276
  413.0 64.3 %all-to-all-start.3 = ((bf16[16,1,32,2176]{3,2,1,0:T(8,128)(2,1)}), bf16[16,1,32,2176]{3,2,1,0:T(8,128)(2,1)S(1)}, u32[]{:S(2)}, u32[]{:S(2)}) async-start(bf16[16,1,32,2176]{3,2,1,0:T(8,128)(2,1)} %branch_1_fun.21), calls=%async_computation.3 | async-start | bytes 4456448 | tf_op jit(solution)/shard_map/cond/branch_1_fun/all_to_all | solution.py:276
  477.3 1.4 copy-start.7
  501.0 26.2 %collective-permute-start = (bf16[2,4,256,256]{3,2,1,0:T(8,128)(2,1)}, bf16[2,4,256,256]{3,2,1,0:T(8,128)(2,1)S(1)}, u32[]{:S(2)}, u32[]{:S(2)}) collective-permute-start(bf16[2,4,256,256]{3,2,1,0:T(8,128)(2,1)} %branch_1_fun.35), channel_id=1, source_target_pairs={{0,1},{1,0},{2,3},{3,2},{4,5},{5,4},{6,7},{7,6},{8,9},{9,8},{10,11... | collective-permute-start | bytes 3145736 | tf_op jit(solution)/shard_map/cond/branch_1_fun/ppermute | solution.py:317
  506.8 42.8 %collective-permute-start.2 = (bf16[2,4,256,256]{3,2,1,0:T(8,128)(2,1)}, bf16[2,4,256,256]{3,2,1,0:T(8,128)(2,1)}, u32[]{:S(2)}, u32[]{:S(2)}) collective-permute-start(bf16[2,4,256,256]{3,2,1,0:T(8,128)(2,1)} %branch_1_fun.37), channel_id=1, source_target_pairs={{0,1},{1,0},{2,3},{3,2},{4,5},{5,4},{6,7},{7,6},{8,9},{9,8},{10,11... | collective-permute-start | bytes 3145736 | tf_op jit(solution)/shard_map/cond/branch_1_fun/ppermute | solution.py:317
  513.8 35.8 %copy-start.5 = (f32[2,4,256,256]{3,2,1,0:T(8,128)S(1)}, f32[2,4,256,256]{3,2,1,0:T(8,128)}, u32[]{:S(2)}) copy-start(f32[2,4,256,256]{3,2,1,0:T(8,128)} %branch_1_fun.34) | copy-start | bytes 6291460 | tf_op jit(solution)/shard_map/cond
  554.8 34.2 %all-to-all-start.6 = ((bf16[2,4,256,256]{3,1,0,2:T(4,128)(2,1)}), bf16[2,4,256,256]{3,1,0,2:T(4,128)(2,1)S(1)}, u32[]{:S(2)}, u32[]{:S(2)}) async-start(bf16[2,4,256,256]{3,1,0,2:T(4,128)(2,1)} %copy.60), calls=%async_computation.6 | async-start | bytes 2097152 | tf_op jit(solution)/shard_map/cond/branch_1_fun/all_to_all | solution.py:332
  589.0 29.8 %all-to-all-start.5 = ((bf16[2,4,256,256]{3,1,0,2:T(4,128)(2,1)}), bf16[2,4,256,256]{3,1,0,2:T(4,128)(2,1)S(1)}, u32[]{:S(2)}, u32[]{:S(2)}) async-start(bf16[2,4,256,256]{3,1,0,2:T(4,128)(2,1)} %copy.57), calls=%async_computation.5 | async-start | bytes 2097152 | tf_op jit(solution)/shard_map/cond/branch_1_fun/all_to_all | solution.py:332
  620.5 14.9 %collective-permute-start.3 = (bf16[2,8,4,16,256]{4,3,2,1,0:T(8,128)(2,1)S(1)}, bf16[2,8,4,16,256]{4,3,2,1,0:T(8,128)(2,1)}, u32[]{:S(2)}, u32[]{:S(2)}) collective-permute-start(bf16[2,8,4,16,256]{4,3,2,1,0:T(8,128)(2,1)S(1)} %bitcast.155), channel_id=1, source_target_pairs={{0,1},{1,0},{2,3},{3,2},{4,5},{5,4},{6,7},{7,6},{8,9},{9,8},{10,11... | collective-permute-start | bytes 1572872 | tf_op jit(solution)/shard_map/cond/branch_1_fun/ppermute | solution.py:341
  621.3 25.0 %collective-permute-start.1 = (bf16[2,8,4,16,256]{4,3,2,1,0:T(8,128)(2,1)S(1)}, bf16[2,8,4,16,256]{4,3,2,1,0:T(8,128)(2,1)S(1)}, u32[]{:S(2)}, u32[]{:S(2)}) collective-permute-start(bf16[2,8,4,16,256]{4,3,2,1,0:T(8,128)(2,1)S(1)} %bitcast.157), channel_id=1, source_target_pairs={{0,1},{1,0},{2,3},{3,2},{4,5},{5,4},{6,7},{7,6},{8,9},{9,8},{10,11... | collective-permute-start | bytes 1572872 | tf_op jit(solution)/shard_map/cond/branch_1_fun/ppermute | solution.py:341
  646.8 1.3 copy-start.8
Sparse Core Ops, SparseCore 0:
  105.9 58.0 all-gather.4

commit v3 on v2

v3 whole, which is shorter than its diff:
```python
import functools
import math

import jax
import jax.numpy as jnp
from jax import lax
from jax.experimental import pallas as pl
from jax.experimental.pallas import tpu as pltpu
from jax.sharding import PartitionSpec as P

F32 = jnp.float32
BF16 = jnp.bfloat16
VMEM = 56 * 1024 * 1024


def tables(length):
    counter = jnp.arange(length, dtype=jnp.int32)
    product = counter[:, None] * counter[None, :] % length
    angles = product.astype(jnp.float32) * (2.0 * math.pi / length)
    factor = 1.0 / math.sqrt(length)
    return (
        (jnp.cos(angles) * factor).astype(jnp.bfloat16),
        (jnp.sin(angles) * factor).astype(jnp.bfloat16),
    )


def dot(a, b):
    return lax.dot_general(a, b, (((1,), (0,)), ((), ())), preferred_element_type=F32)


def cost(flops, bytes_accessed):
    return pl.CostEstimate(flops=int(flops), bytes_accessed=int(bytes_accessed), transcendentals=0)


def layout(line_mask, parts):
    edge = line_mask.shape[1]
    slab = line_mask.shape[0] // parts
    half = edge // 2
    sampled = line_mask != 0
    upper = jnp.triu(jnp.ones((edge, edge), BF16), 1)
    rank = jnp.dot(sampled.astype(BF16), upper, preferred_element_type=F32).astype(jnp.int32)
    over = jnp.maximum(jnp.sum(sampled.astype(jnp.int32), axis=1).reshape(parts, slab) - half, 0)
    fits = jnp.all(jnp.sum(over, axis=1) <= half)
    before = (jnp.cumsum(over, axis=1) - over).reshape(-1, 1)
    place = jnp.where(sampled, rank + jnp.where(rank < half, 0, before), -1)
    return fits, place, half * (slab + 1)


def compact_kernel(pieces, k_ref, s_ref, t_ref, *refs):
    out_refs, lines_ref, over_ref = refs[:pieces], refs[pieces], refs[pieces + 1]
    slab, _, edge = lines_ref.shape
    half = edge // 2
    parts, _, rows, _ = out_refs[0].shape
    step = 32

    @pl.loop(0, edge // step)
    def _(at):
        first = pl.multiple_of(at * step, step)
        for r in range(2):
            block = jnp.swapaxes(k_ref[0, r, pl.ds(first, step)], 0, 1)
            lines_ref[:, pl.ds(pl.multiple_of(r * edge + first, step), step), :] = block

    def send(picked, places):
        moved = dot(t_ref[...], picked.astype(BF16)).astype(BF16)
        moved = moved.reshape(parts, pieces, rows, picked.shape[1])
        for p in range(pieces):
            out_refs[p][:, 0, :, places] = moved[:, p]

    over_ref[...] = jnp.zeros_like(over_ref)

    @pl.loop(0, slab // 2)
    def _(pair):
        one = dot(lines_ref[2 * pair], s_ref[2 * pair])
        two = dot(lines_ref[2 * pair + 1], s_ref[2 * pair + 1])
        over_ref[...] += one[:, half:] + two[:, half:]
        own = jnp.concatenate([one[:, :half], two[:, :half]], axis=1)
        send(own, pl.ds(pl.multiple_of(pair * edge, edge), edge))

    send(over_ref[...], pl.ds(slab * half, half))


def by_destination(table, parts, pieces):
    size = table.shape[0]
    rows = table.reshape(2, parts, pieces, size // (2 * parts * pieces), size)
    return rows.transpose(1, 2, 0, 3, 4).reshape(size, size)


def compact(data, first_coil, coils, pieces, select, table, parts, slots):
    _, _, edge, slab, _ = data.shape
    rows = 2 * edge // parts // pieces
    return pl.pallas_call(
        functools.partial(compact_kernel, pieces),
        grid=(coils,),
        in_specs=[
            pl.BlockSpec((1, 2, edge, slab, edge), lambda c: (first_coil + c, 0, 0, 0, 0)),
            pl.BlockSpec(select.shape, lambda c: (0, 0, 0)),
            pl.BlockSpec(table.shape, lambda c: (0, 0)),
        ],
        out_specs=[pl.BlockSpec((parts, 1, rows, slots), lambda c: (0, c, 0, 0))] * pieces,
        out_shape=[jax.ShapeDtypeStruct((parts, coils, rows, slots), BF16)] * pieces,
        scratch_shapes=[pltpu.VMEM((slab, 2 * edge, edge), BF16), pltpu.VMEM((2 * edge, edge // 2), F32)],
        compiler_params=pltpu.CompilerParams(vmem_limit_bytes=VMEM),
        cost_estimate=cost(coils * 4 * slots * edge * 4 * edge, 4 * coils * edge * (slab * edge + slots)),
    )(data, select, by_destination(table, parts, pieces))


def expand_kernel(place_ref, in_ref, out_ref, lines_ref):
    edge = place_ref.shape[1]
    half = edge // 2
    slab, rows, _ = lines_ref.shape
    places = lax.broadcasted_iota(jnp.int32, (edge, edge), 0)
    shared = in_ref[0, :, :, slab * half :].reshape(rows, half)
    for k in range(slab):
        chosen = jnp.where(places == place_ref[k : k + 1, :], 1.0, 0.0).astype(BF16)
        own = in_ref[0, :, :, k * half : (k + 1) * half].reshape(rows, half)
        lines_ref[k] = dot(jnp.concatenate([own, shared], axis=1), chosen).astype(BF16)
    for at in range(0, rows, 16):
        out_ref[at : at + 16] = jnp.swapaxes(lines_ref[:, at : at + 16, :], 0, 1)


def expand(arrived, place):
    parts, coils, rows, slots = arrived.shape
    edge = place.shape[1]
    slab = place.shape[0] // parts
    rows = coils * rows
    return pl.pallas_call(
        expand_kernel,
        grid=(parts,),
        in_specs=[
            pl.BlockSpec((slab, edge), lambda d: (d, 0)),
            pl.BlockSpec((1,) + arrived.shape[1:], lambda d: (d, 0, 0, 0)),
        ],
        out_specs=pl.BlockSpec((rows, slab, edge), lambda d: (0, d, 0)),
        out_shape=jax.ShapeDtypeStruct((rows, parts * slab, edge), BF16),
        scratch_shapes=[pltpu.VMEM((slab, rows, edge), BF16)],
        compiler_params=pltpu.CompilerParams(vmem_limit_bytes=VMEM),
        cost_estimate=cost(parts * slab * rows * edge * edge * 2, 2 * (arrived.size + parts * slab * rows * edge)),
    )(place, arrived)


def forward_kernel(maps_ref, vol_ref, right_ref, left_ref, out_ref):
    edge = vol_ref.shape[3]
    for i in range(vol_ref.shape[1]):
        map_real, map_imag = maps_ref[0, 0, i].astype(F32), maps_ref[0, 1, i].astype(F32)
        vol_real, vol_imag = vol_ref[0, i].astype(F32), vol_ref[1, i].astype(F32)
        real = (map_real * vol_real - map_imag * vol_imag).astype(BF16)
        imag = (map_real * vol_imag + map_imag * vol_real).astype(BF16)
        along = dot(jnp.concatenate([real, imag], axis=1), right_ref[...]).astype(BF16)
        stacked = jnp.concatenate([along[:, :edge], along[:, edge:]], axis=0)
        out_ref[0, i] = dot(left_ref[...], stacked).astype(BF16)


def forward(maps, volume, right, left, group):
    coils, _, deep, edge, _ = maps.shape
    return pl.pallas_call(
        forward_kernel,
        grid=(deep // group, coils),
        in_specs=[
            pl.BlockSpec((1, 2, group, edge, edge), lambda x, c: (c, 0, x, 0, 0)),
            pl.BlockSpec((2, group, edge, edge), lambda x, c: (0, x, 0, 0)),
            pl.BlockSpec(right.shape, lambda x, c: (0, 0)),
            pl.BlockSpec(left.shape, lambda x, c: (0, 0)),
        ],
        out_specs=pl.BlockSpec((1, group, 2 * edge, edge), lambda x, c: (c, x, 0, 0)),
        out_shape=jax.ShapeDtypeStruct((coils, deep, 2 * edge, edge), BF16),
        compiler_params=pltpu.CompilerParams(vmem_limit_bytes=VMEM),
        cost_estimate=cost(coils * deep * edge**3 * 16, 4 * maps.size),
    )(maps, volume, right, left)


def backward_kernel(first, at_ref, *refs):
    if first:
        maps_ref, k_ref, h_ref, mask_ref, left_ref, right_ref, out_ref, sum_ref = refs
    else:
        maps_ref, k_ref, h_ref, mask_ref, left_ref, right_ref, before_ref, out_ref, sum_ref = refs
    edge = mask_ref.shape[1]
    sampled = mask_ref[...].astype(F32)
    sampled = jnp.concatenate([sampled, sampled], axis=0)

    @pl.when(pl.program_id(1) == 0)
    def _():
        sum_ref[...] = jnp.zeros_like(sum_ref) if first else before_ref[...]

    for i in range(k_ref.shape[1]):
        hybrid = h_ref[0, :, i].reshape(2 * edge, edge)
        residual = (sampled * (k_ref[0, i].astype(F32) - hybrid.astype(F32))).astype(BF16)
        back = dot(left_ref[...], residual).astype(BF16)
        back = jnp.concatenate([back[:edge], back[edge:]], axis=1)
        back = dot(back, right_ref[...]).astype(BF16).astype(F32)
        real, imag = back[:, :edge], back[:, edge:]
        map_real, map_imag = maps_ref[0, 0, i].astype(F32), maps_ref[0, 1, i].astype(F32)
        sum_ref[0, i] += map_real * real + map_imag * imag
        sum_ref[1, i] += map_real * imag - map_imag * real

    @pl.when(pl.program_id(1) == pl.num_programs(1) - 1)
    def _():
        out_ref[...] = sum_ref[...].astype(out_ref.dtype)


def backward(
    maps, coil_kspace, line_mask, left, right, group, hybrid, hybrid_x, before, first_coil, first_x, count, kind
):
    coils, _, _, edge, _ = hybrid.shape
    group = min(group, count)
    first = before is None
    block = (2, group, edge, edge)
    spec = pltpu.PrefetchScalarGridSpec(
        num_scalar_prefetch=1,
        grid=(count // group, coils),
        in_specs=[
            pl.BlockSpec((1, 2, group, edge, edge), lambda x, c, at: (first_coil + c, 0, at[0] + x, 0, 0)),
            pl.BlockSpec((1, group, 2 * edge, edge), lambda x, c, at: (first_coil + c, at[0] + x, 0, 0)),
            pl.BlockSpec((1, 2, group, edge, edge), lambda x, c, at: (c, 0, at[0] + x - hybrid_x // group, 0, 0)),
            pl.BlockSpec(line_mask.shape, lambda x, c, at: (0, 0)),
            pl.BlockSpec(left.shape, lambda x, c, at: (0, 0)),
            pl.BlockSpec(right.shape, lambda x, c, at: (0, 0)),
        ]
        + ([] if first else [pl.BlockSpec(block, lambda x, c, at: (0, at[0] + x, 0, 0))]),
        out_specs=pl.BlockSpec(block, lambda x, c, at: (0, x, 0, 0)),
        scratch_shapes=[pltpu.VMEM(block, F32)],
    )
    start = jnp.full((1,), first_x // group, jnp.int32)
    return pl.pallas_call(
        functools.partial(backward_kernel, first),
        grid_spec=spec,
        out_shape=jax.ShapeDtypeStruct((2, count, edge, edge), kind),
        compiler_params=pltpu.CompilerParams(vmem_limit_bytes=VMEM),
        cost_estimate=cost(coils * count * edge**3 * 16, count * edge**2 * (12 * coils + 16)),
    )(start, maps, coil_kspace, hybrid, line_mask, left, right, *([] if first else [before]))


def body(coil_groups, volume, coil_maps, kspace, line_mask):
    coils, _, deep, edge, _ = coil_maps.shape
    slab = kspace.shape[3]
    parts = edge // slab
    me = lax.axis_index("cuts")
    mine = lax.axis_index("coil")
    cos_table, sin_table = tables(edge)
    turn = jnp.block([[cos_table, sin_table], [-sin_table, cos_table]])
    turn_back = jnp.block([[cos_table, -sin_table], [sin_table, cos_table]])
    fits, place, slots = layout(line_mask, parts)
    if coils >= 6:
        sizes = [1, (coils - 3) // 2, (coils - 2) // 2, 2]
    else:
        sizes = [1] * coils
    firsts = [sum(sizes[:i]) for i in range(len(sizes))]
    pieces = min(2, deep // coil_groups)
    planes = deep // pieces
    last = len(sizes) - 1
    group = min(4, deep)

    def step(pack, unpack):
        full_slab = lax.all_gather(volume, "coil", axis=2, tiled=True)
        arrived = []
        total = coil_kspace = None
        for i in range(last):
            (sent,) = pack(i, 1)
            if i == 1:
                sent, full_slab = lax.optimization_barrier((sent, full_slab))
                coil_kspace = forward(coil_maps, full_slab, turn_back, turn, group)
            elif i == 2:
                sent, coil_kspace = lax.optimization_barrier((sent, coil_kspace))
            arrived.append(exchange(sent))
        if coil_kspace is None:
            coil_kspace = forward(coil_maps, full_slab, turn_back, turn, group)
        back = functools.partial(backward, coil_maps, coil_kspace, line_mask, turn_back, turn, group)
        sent = list(pack(last, pieces))
        for i in range(last):
            if i == last - 1 and total is not None:
                sent[0], total = lax.optimization_barrier((sent[0], total))
            total = back(unpack(i, deep, arrived[i]), 0, total, firsts[i], 0, deep, F32)
        if pieces > 1:
            sent[1], total = lax.optimization_barrier((sent[1], total))
        arrived = [exchange(one) for one in sent]

        def gradient(p):
            hybrid = unpack(last, planes, arrived[p])

            def planes_from(first_x, count, kind, earlier=None):
                before = total
                if earlier is not None:
                    _, before = lax.optimization_barrier((earlier, total))
                return back(hybrid, p * planes, before, firsts[last], first_x, count, kind)

            return planes_from

        return finish(coil_groups, mine, full_slab, gradient, arrived, deep)

    def exchange(sent):
        return lax.all_to_all(sent, "cuts", split_axis=0, concat_axis=0, tiled=True)

    def send_sampled():
        own = lax.dynamic_slice_in_dim(place, me * slab, slab, 0)
        select = (own[..., None] == jnp.arange(edge)).astype(BF16)

        def pack(i, pieces):
            return compact(kspace, firsts[i], sizes[i], pieces, select, turn_back, parts, slots)

        def unpack(i, planes, arrived):
            return expand(arrived, place).reshape(sizes[i], 2, planes, edge, edge)

        return step(pack, unpack)

    def send_all():
        def pack(i, pieces):
            part = lax.slice_in_dim(kspace, firsts[i], firsts[i] + sizes[i], axis=0)
            data = part.transpose(0, 3, 1, 2, 4).reshape(sizes[i], slab, 2 * edge, edge)
            table = by_destination(turn_back, parts, pieces)
            moved = jnp.einsum("xn,ckny->xcky", table, data, preferred_element_type=F32).astype(BF16)
            moved = moved.reshape(parts, pieces, 2, deep // pieces, sizes[i], slab, edge)
            return [moved[:, p] for p in range(pieces)]

        def unpack(i, planes, arrived):
            return arrived.transpose(3, 1, 2, 0, 4, 5).reshape(sizes[i], 2, planes, edge, edge)

        return step(pack, unpack)

    return lax.cond(fits, send_sampled, send_all)


def finish(coil_groups, mine, full_slab, gradient, arrived, deep):
    edge = full_slab.shape[2]
    parts = edge // deep
    share = deep // coil_groups // len(arrived)
    rings = [[(i, (i + s) % coil_groups) for i in range(coil_groups)] for s in range(coil_groups)]
    pieces = [(p, p * coil_groups * share, share) for p in range(len(arrived))]
    if share % 2 == 0:
        p, first, _ = pieces.pop()
        pieces += [(p, first, share // 2), (p, first + coil_groups * share // 2, share // 2)]

    def start(p):
        one = gradient(p)
        mine_of = [piece for piece in pieces if piece[0] == p]
        leave = [
            [one(first + lax.rem(mine + s, coil_groups) * share, share, BF16) for s in range(1, coil_groups)]
            for _, first, share in mine_of
        ]
        away = [[lax.ppermute(term, "coil", ring) for term, ring in zip(terms, rings[1:])] for terms in leave]
        stay = [one(first + mine * share, share, F32, leave) for _, first, share in mine_of]
        return away, stay

    def to_cuts(i, away, summed):
        p, first, share = pieces[i]
        for term in away:
            summed = summed + term.astype(F32)
        base = lax.dynamic_slice_in_dim(full_slab, first + mine * share, share, 1).astype(F32)
        updated = (base - 0.5 * summed).astype(BF16)
        if p + 1 < len(arrived):
            updated, arrived[p + 1] = lax.optimization_barrier((updated, arrived[p + 1]))
        return lax.all_to_all(updated, "cuts", split_axis=2, concat_axis=1, tiled=True)

    def to_groups(updated):
        slab = updated.shape[2]
        share = updated.shape[1] // parts
        updated = updated.reshape(2, coil_groups, parts // coil_groups, share, slab, edge)
        whole = jnp.zeros((2, parts // coil_groups, coil_groups, share, slab, edge), BF16)
        for s in range(coil_groups):
            to = lax.rem(mine + s, coil_groups)
            source = lax.rem(mine + coil_groups - s, coil_groups)
            moved = lax.dynamic_index_in_dim(updated, to, 1, keepdims=False)
            if s:
                moved = lax.ppermute(moved, "coil", rings[s])
            whole = lax.dynamic_update_index_in_dim(whole, moved[:, :, None], source, 2)
        return whole.reshape(2, parts // coil_groups, coil_groups * share, slab, edge)

    out = []
    away, stay = start(0)
    for i, (p, _, _) in enumerate(pieces):
        updated = to_cuts(i, away.pop(0), stay.pop(0))
        if i + 1 < len(pieces):
            if not away:
                away, stay = start(p + 1)
            away[0], updated = lax.optimization_barrier((away[0], updated))
        out.append(to_groups(updated))
    out = jnp.concatenate(out, axis=2)
    return out.reshape(2, edge // coil_groups, out.shape[3], edge)


def solution(mesh):
    placed = (
        P(None, "cuts", "coil", None),
        P("coil", None, "cuts", None, None),
        P("coil", None, None, "cuts", None),
        P(),
    )
    return jax.shard_map(
        functools.partial(body, mesh.shape["coil"]),
        mesh=mesh,
        in_specs=placed,
        out_specs=P(None, "coil", "cuts", None),
        check_vma=False,
    )
```

time: 668 us -> 585 us (0.88)
  waiting for transfers between devices: 184 us -> 108 us
  Pallas kernels: 342 us -> 303 us
  starting transfers between devices: 79.8 us -> 103 us
  local copies, waits for them, and re-layouts: 14.4 us -> 21.6 us
    pallas_call x10 -> x9, Pallas kernels: 188 us -> 150 us  [the longest x4 75.5 us: compact(): pl.pallas_call(functools.partial(compact_kernel, pieces), grid=(coils,),...]
    all_to_all x2 -> x3, waiting for transfers between devices: 44.1 us -> 7.97 us  [to_cuts(): lax.all_to_all(updated, 'cuts', split_axis=2, concat_axis=1, tiled=True)]
    all_to_all x5, starting transfers between devices: 57.4 us -> 77.7 us  [exchange(): return lax.all_to_all(sent, 'cuts', split_axis=0, concat_axis=0, tiled=True)]
    all_gather x1, waiting for transfers between devices: 36.8 us -> 19 us  [step(): full_slab = lax.all_gather(volume, 'coil', axis=2, tiled=True)]
    ppermute x4 -> x6, waiting for transfers between devices: 51 us -> 35.8 us  [the longest x3 18.5 us: start(): lax.ppermute(term, 'coil', ring)]
    pallas_call x8 -> x9, Pallas kernels: 96.7 us -> 94.9 us  [backward(): pl.pallas_call(functools.partial(backward_kernel, first), grid_spec=spec,...]
    all_to_all x2 -> x3, starting transfers between devices: 18.1 us -> 16.7 us  [to_cuts(): lax.all_to_all(updated, 'cuts', split_axis=2, concat_axis=1, tiled=True)]
  transfers between devices with their start and end apart: 12 -> 15, of which waited for: 10 -> 8; matrix products, arithmetic and copies ran while one was open for 1% -> 3% of each run, Pallas kernels for 47% -> 53%
where the time goes in v3:
time: 585 us; the launch traced here: 574 us
  Pallas kernels  303 us (52%)
  waiting for transfers between devices  108 us (18%)
  starting transfers between devices  103 us (18%)
  local copies, waits for them, and re-layouts  21.6 us (4%)
  between operations  14.6 us (2%)
  other arithmetic  14.5 us (2%)
  loops' own time  8.71 us (1%)
    pallas_call x9, Pallas kernels, backward(): pl.pallas_call(functools.partial(backward_kernel, first), grid_spec=spec,...  94.9 us
    all_to_all x5, starting transfers between devices, exchange(): return lax.all_to_all(sent, 'cuts', split_axis=0, concat_axis=0, tiled=True)  77.7 us
    pallas_call x4, Pallas kernels, compact(): pl.pallas_call(functools.partial(compact_kernel, pieces), grid=(coils,),...  75.5 us
    pallas_call x5, Pallas kernels, expand(): pl.pallas_call(expand_kernel, grid=(parts,), in_specs=[pl.BlockSpec((slab...  74.2 us
    pallas_call x1, Pallas kernels, forward(): pl.pallas_call(forward_kernel, grid=(deep // group, coils), in_specs=[pl....  58 us
    all_to_all x5, waiting for transfers between devices, exchange(): return lax.all_to_all(sent, 'cuts', split_axis=0, concat_axis=0, tiled=True)  45 us
    all_gather x1, waiting for transfers between devices, step(): full_slab = lax.all_gather(volume, 'coil', axis=2, tiled=True)  19 us
    ppermute x3, waiting for transfers between devices, start(): lax.ppermute(term, 'coil', ring)  18.5 us
  transfers between devices with their start and end apart: 15, of which 8 were waited for; matrix products, arithmetic and copies ran while one was open for 3% of the time, Pallas kernels for 53%

profile of v3, /device:TPU:0, one launch (start us, length us, event | category | flops | bytes accessed | tf_op | source)
XLA Modules:
  0.0 574.0 jit_solution(15467626728630645123)
XLA Ops:
  13.6 551.7 %conditional.1 = (bf16[2,128,16,256]{3,2,1,0:T(8,128)(2,1)S(1)}) conditional(s32[]{:T(128)} %convert_element_type.116, (s32[]{:T(128)}, bf16[512,512]{1,0:T(8,128)(2,1)S(1)}, bf16[8,2,256,16,256]{4,3,2,1,0:T(8,128)(2,1)}, bf16[2,16,128,256]{3,2,1,0:T(8,128)(2,1)}, bf16[8,2,16,256,256]{4,3,2,1,0:T(8,128)(2,1)}, ...), branch_computations={%region_4.5_spmd, %region_5.6_spmd} | conditional | flops 95573770240 | bytes 789578240 | solution.py:318
  26.9 11.4 %branch_1_fun.24 = bf16[16,1,32,2176]{3,2,1,0:T(8,128)(2,1)} custom-call(bf16[8,2,256,16,256]{4,3,2,1,0:T(8,128)(2,1)} %get-tuple-element.93.k_ref, bf16[16,256,256]{2,1,0:T(8,128)(2,1)} %fusion.s_ref, bf16[512,512]{1,0:T(8,128)(2,1)} %bitcast.183), custom_call_target="tpu_custom_call" | custom-call | flops 2281701376 | bytes 6422528 | tf_op jit(solution)/shard_map/cond/branch_1_fun/pallas_call | solution.py:91
  45.7 18.9 %branch_1_fun.20 = bf16[16,2,32,2176]{3,2,1,0:T(8,128)(2,1)} custom-call(bf16[8,2,256,16,256]{4,3,2,1,0:T(8,128)(2,1)} %get-tuple-element.93.k_ref, bf16[16,256,256]{2,1,0:T(8,128)(2,1)} %fusion.s_ref, bf16[512,512]{1,0:T(8,128)(2,1)} %bitcast.184), custom_call_target="tpu_custom_call" | custom-call | flops 4563402752 | bytes 12845056 | tf_op jit(solution)/shard_map/cond/branch_1_fun/pallas_call | solution.py:91
  64.6 19.0 %all-gather.5.cloned.1.call-done.vol_ref = bf16[2,16,256,256]{3,2,1,0:T(8,128)(2,1)} async-done(((bf16[2,16,128,256]{3,2,1,0:T(8,128)(2,1)}), bf16[2,16,256,256]{3,2,1,0:T(8,128)(2,1)}) %all-gather.5.cloned.1.call-update) | async-done | bytes 4194320 | tf_op jit(solution)/shard_map/cond/branch_1_fun/all_gather | solution.py:253
  90.4 11.8 %all-to-all-start = ((bf16[16,2,32,2176]{3,2,1,0:T(8,128)(2,1)}), bf16[16,2,32,2176]{3,2,1,0:T(8,128)(2,1)}, u32[]{:S(2)}, u32[]{:S(2)}) async-start(bf16[16,2,32,2176]{3,2,1,0:T(8,128)(2,1)} %branch_1_fun.20), calls=%async_computation | async-start | bytes 8912896 | tf_op jit(solution)/shard_map/cond/branch_1_fun/all_to_all | solution.py:290
  102.2 26.3 %branch_1_fun.19 = bf16[16,3,32,2176]{3,2,1,0:T(8,128)(2,1)} custom-call(bf16[8,2,256,16,256]{4,3,2,1,0:T(8,128)(2,1)} %get-tuple-element.93.k_ref, bf16[16,256,256]{2,1,0:T(8,128)(2,1)} %fusion.s_ref, bf16[512,512]{1,0:T(8,128)(2,1)} %bitcast.185), custom_call_target="tpu_custom_call" | custom-call | flops 6845104128 | bytes 19267584 | tf_op jit(solution)/shard_map/cond/branch_1_fun/pallas_call | solution.py:91
  128.5 58.0 %branch_1_fun.21.refs_1_ = bf16[8,16,512,256]{3,2,1,0:T(8,128)(2,1)} custom-call(bf16[8,2,16,256,256]{4,3,2,1,0:T(8,128)(2,1)} %get-tuple-element.92.maps_ref.refs_0_, bf16[2,16,256,256]{3,2,1,0:T(8,128)(2,1)} %all-gather.5.cloned.1.call-done.vol_ref, bf16[512,512]{1,0:T(8,128)(2,1)S(1)} %get-tuple-element.100.right_ref.refs_4_, ...), custom_call_target="tpu_custom_call" | custom-call | flops 34359738368 | bytes 67108864 | tf_op jit(solution)/shard_map/cond/branch_1_fun/pallas_call | solution.py:155
  186.5 18.7 %all-to-all-start.3 = ((bf16[16,3,32,2176]{3,2,1,0:T(8,128)(2,1)}), bf16[16,3,32,2176]{3,2,1,0:T(8,128)(2,1)}, u32[]{:S(2)}, u32[]{:S(2)}) async-start(bf16[16,3,32,2176]{3,2,1,0:T(8,128)(2,1)} %branch_1_fun.19), calls=%async_computation.3 | async-start | bytes 13369344 | tf_op jit(solution)/shard_map/cond/branch_1_fun/all_to_all | solution.py:290
  206.0 18.8 %branch_1_fun.22 = (bf16[16,2,16,2176]{3,2,1,0:T(8,128)(2,1)}, bf16[16,2,16,2176]{3,2,1,0:T(8,128)(2,1)}) custom-call(bf16[8,2,256,16,256]{4,3,2,1,0:T(8,128)(2,1)} %get-tuple-element.93.k_ref, bf16[16,256,256]{2,1,0:T(8,128)(2,1)} %fusion.s_ref, bf16[512,512]{1,0:T(8,128)(2,1)} %bitcast.199), custom_call_target="tpu_custom_call" | custom-call | flops 4563402752 | bytes 12845056 | tf_op jit(solution)/shard_map/cond/branch_1_fun/pallas_call | solution.py:91
  224.9 14.0 %branch_1_fun.25 = bf16[32,256,256]{2,1,0:T(8,128)(2,1)} custom-call(s32[256,256]{1,0:T(8,128)} %copy-done.2, bf16[16,1,32,2176]{3,2,1,0:T(8,128)(2,1)} %copy-done.5), custom_call_target="tpu_custom_call" | custom-call | flops 1073741824 | bytes 6422528 | tf_op jit(solution)/shard_map/cond/branch_1_fun/pallas_call | solution.py:126
  238.9 11.1 %branch_1_fun.26.refs_6_ = f32[2,16,256,256]{3,2,1,0:T(8,128)} custom-call(s32[1]{0:T(128)} %constant.258.clone.at_ref, bf16[8,2,16,256,256]{4,3,2,1,0:T(8,128)(2,1)} %get-tuple-element.92.maps_ref.refs_0_, bf16[8,16,512,256]{3,2,1,0:T(8,128)(2,1)} %branch_1_fun.21.refs_1_, bf16[1,2,16,256,256]{4,3,2,1,0:T(8,128)(2,1)} %bitcast.181, ...), custom_call_target="tpu_custom_call" | custom-call | flops 4294967296 | bytes 29360128 | tf_op jit(solution)/shard_map/cond/branch_1_fun/pallas_call | solution.py:223
  250.0 15.5 %branch_1_fun.23 = bf16[64,256,256]{2,1,0:T(8,128)(2,1)} custom-call(s32[256,256]{1,0:T(8,128)} %copy-done.2, bf16[16,2,32,2176]{3,2,1,0:T(8,128)(2,1)} %all-to-all-done.in_ref), custom_call_target="tpu_custom_call" | custom-call | flops 2147483648 | bytes 12845056 | tf_op jit(solution)/shard_map/cond/branch_1_fun/pallas_call | solution.py:126
  265.5 21.2 %branch_1_fun.27.refs_6_ = f32[2,16,256,256]{3,2,1,0:T(8,128)} custom-call(s32[1]{0:T(128)} %constant.258.clone.at_ref, bf16[8,2,16,256,256]{4,3,2,1,0:T(8,128)(2,1)} %get-tuple-element.92.maps_ref.refs_0_, bf16[8,16,512,256]{3,2,1,0:T(8,128)(2,1)} %branch_1_fun.21.refs_1_, bf16[2,2,16,256,256]{4,3,2,1,0:T(8,128)(2,1)} %bitcast.179, ...), custom_call_target="tpu_custom_call" | custom-call | flops 8589934592 | bytes 41943040 | tf_op jit(solution)/shard_map/cond/branch_1_fun/pallas_call | solution.py:223
  286.8 39.4 %all-to-all-done.3.in_ref = bf16[16,3,32,2176]{3,2,1,0:T(8,128)(2,1)} async-done(((bf16[16,3,32,2176]{3,2,1,0:T(8,128)(2,1)}), bf16[16,3,32,2176]{3,2,1,0:T(8,128)(2,1)}, u32[]{:S(2)}, u32[]{:S(2)}) %all-to-all-start.3) | async-done | bytes 6684704 | tf_op jit(solution)/shard_map/cond/branch_1_fun/all_to_all | solution.py:290
  326.2 29.9 %all-to-all-start.2 = ((bf16[16,2,16,2176]{3,2,1,0:T(8,128)(2,1)}), bf16[16,2,16,2176]{3,2,1,0:T(8,128)(2,1)S(1)}, u32[]{:S(2)}, u32[]{:S(2)}) async-start(bf16[16,2,16,2176]{3,2,1,0:T(8,128)(2,1)} %get-tuple-element.108), calls=%async_computation.2 | async-start | bytes 4456448 | tf_op jit(solution)/shard_map/cond/branch_1_fun/all_to_all | solution.py:290
  356.1 16.8 %branch_1_fun.29 = bf16[96,256,256]{2,1,0:T(8,128)(2,1)} custom-call(s32[256,256]{1,0:T(8,128)} %copy-done.2, bf16[16,3,32,2176]{3,2,1,0:T(8,128)(2,1)} %all-to-all-done.3.in_ref), custom_call_target="tpu_custom_call" | custom-call | flops 3221225472 | bytes 19267584 | tf_op jit(solution)/shard_map/cond/branch_1_fun/pallas_call | solution.py:126
  372.9 28.4 %branch_1_fun.30.refs_6_ = f32[2,16,256,256]{3,2,1,0:T(8,128)} custom-call(s32[1]{0:T(128)} %constant.258.clone.at_ref, bf16[8,2,16,256,256]{4,3,2,1,0:T(8,128)(2,1)} %get-tuple-element.92.maps_ref.refs_0_, bf16[8,16,512,256]{3,2,1,0:T(8,128)(2,1)} %branch_1_fun.21.refs_1_, bf16[3,2,16,256,256]{4,3,2,1,0:T(8,128)(2,1)} %bitcast.173, ...), custom_call_target="tpu_custom_call" | custom-call | flops 12884901888 | bytes 54525952 | tf_op jit(solution)/shard_map/cond/branch_1_fun/pallas_call | solution.py:223
  402.6 10.0 %all-to-all-start.4 = ((bf16[16,2,16,2176]{3,2,1,0:T(8,128)(2,1)}), bf16[16,2,16,2176]{3,2,1,0:T(8,128)(2,1)S(1)}, u32[]{:S(2)}, u32[]{:S(2)}) async-start(bf16[16,2,16,2176]{3,2,1,0:T(8,128)(2,1)} %get-tuple-element.114), calls=%async_computation.4 | async-start | bytes 4456448 | tf_op jit(solution)/shard_map/cond/branch_1_fun/all_to_all | solution.py:290
  412.6 14.0 %branch_1_fun.28 = bf16[32,256,256]{2,1,0:T(8,128)(2,1)} custom-call(s32[256,256]{1,0:T(8,128)} %copy-done.2, bf16[16,2,16,2176]{3,2,1,0:T(8,128)(2,1)} %copy-done.4), custom_call_target="tpu_custom_call" | custom-call | flops 1073741824 | bytes 6422528 | tf_op jit(solution)/shard_map/cond/branch_1_fun/pallas_call | solution.py:126
  435.2 7.5 %branch_1_fun.32 = f32[2,4,256,256]{3,2,1,0:T(8,128)} custom-call(s32[1]{0:T(128)} %bitcast.73.at_ref, bf16[8,2,16,256,256]{4,3,2,1,0:T(8,128)(2,1)} %get-tuple-element.92.maps_ref.refs_0_, bf16[8,16,512,256]{3,2,1,0:T(8,128)(2,1)} %branch_1_fun.21.refs_1_, bf16[2,2,8,256,256]{4,3,2,1,0:T(8,128)(2,1)} %bitcast.177, s32[256,256]{1,0:T(8,128)S(1)} %copy-done.1, ...), custom_call_target="tpu_custom_call" | custom-call | flops 2147483648 | bytes 10485760 | tf_op jit(solution)/shard_map/cond/branch_1_fun/pallas_call | solution.py:223
  442.8 16.7 %collective-permute-done = bf16[2,4,256,256]{3,2,1,0:T(8,128)(2,1)} collective-permute-done((bf16[2,4,256,256]{3,2,1,0:T(8,128)(2,1)}, bf16[2,4,256,256]{3,2,1,0:T(8,128)(2,1)}, u32[]{:S(2)}, u32[]{:S(2)}) %collective-permute-start) | collective-permute-done | bytes 1048608 | tf_op jit(solution)/shard_map/cond/branch_1_fun/ppermute | solution.py:338
  473.0 14.0 %branch_1_fun.33 = bf16[32,256,256]{2,1,0:T(8,128)(2,1)} custom-call(s32[256,256]{1,0:T(8,128)} %copy-done.2, bf16[16,2,16,2176]{3,2,1,0:T(8,128)(2,1)} %copy-done.3), custom_call_target="tpu_custom_call" | custom-call | flops 1073741824 | bytes 6422528 | tf_op jit(solution)/shard_map/cond/branch_1_fun/pallas_call | solution.py:126
  521.3 8.0 %all-to-all-done.6 = bf16[2,2,256,256]{3,1,0,2:T(2,128)(2,1)S(1)} async-done(((bf16[2,2,256,256]{3,1,0,2:T(2,128)(2,1)}), bf16[2,2,256,256]{3,1,0,2:T(2,128)(2,1)S(1)}, u32[]{:S(2)}, u32[]{:S(2)}) %all-to-all-start.6) | async-done | bytes 524320 | tf_op jit(solution)/shard_map/cond/branch_1_fun/all_to_all | solution.py:350
  542.4 11.7 %collective-permute-done.2 = bf16[2,8,4,16,256]{4,3,2,1,0:T(8,128)(2,1)} collective-permute-done((bf16[2,8,4,16,256]{4,3,2,1,0:T(8,128)(2,1)}, bf16[2,8,4,16,256]{4,3,2,1,0:T(8,128)(2,1)}, u32[]{:S(2)}, u32[]{:S(2)}) %collective-permute-start.2) | collective-permute-done | bytes 524320 | tf_op jit(solution)/shard_map/cond/branch_1_fun/ppermute | solution.py:362
  (89 shorter events, 109.6 us)
Async XLA Ops:
  7.6 0.5 copy-start.10
  7.6 5.2 copy-start.9
  21.7 61.9 %all-gather.5.cloned.1.call-start = ((), (), s32[]{:S(2)}) async-start(), calls=%async_computation.17 | async-start | bytes 6291456 | tf_op jit(solution)/shard_map/cond/branch_1_fun/all_gather | solution.py:253
  25.2 13.1 %copy-start.2 = (s32[256,256]{1,0:T(8,128)}, s32[256,256]{1,0:T(8,128)S(1)}, u32[]{:S(2)}) copy-start(s32[256,256]{1,0:T(8,128)S(1)} %add_select_fusion.place_ref) | copy-start | bytes 786436 | tf_op jit(solution)/shard_map/cond
  38.3 50.8 %all-to-all-start.1 = ((bf16[16,1,32,2176]{3,2,1,0:T(8,128)(2,1)}), bf16[16,1,32,2176]{3,2,1,0:T(8,128)(2,1)S(1)}, u32[]{:S(2)}, u32[]{:S(2)}) async-start(bf16[16,1,32,2176]{3,2,1,0:T(8,128)(2,1)} %branch_1_fun.24), calls=%async_computation.1 | async-start | bytes 4456448 | tf_op jit(solution)/shard_map/cond/branch_1_fun/all_to_all | solution.py:290
  89.1 1.3 copy-start.5
  90.4 96.1 %all-to-all-start = ((bf16[16,2,32,2176]{3,2,1,0:T(8,128)(2,1)}), bf16[16,2,32,2176]{3,2,1,0:T(8,128)(2,1)}, u32[]{:S(2)}, u32[]{:S(2)}) async-start(bf16[16,2,32,2176]{3,2,1,0:T(8,128)(2,1)} %branch_1_fun.20), calls=%async_computation | async-start | bytes 8912896 | tf_op jit(solution)/shard_map/cond/branch_1_fun/all_to_all | solution.py:290
  186.5 139.8 %all-to-all-start.3 = ((bf16[16,3,32,2176]{3,2,1,0:T(8,128)(2,1)}), bf16[16,3,32,2176]{3,2,1,0:T(8,128)(2,1)}, u32[]{:S(2)}, u32[]{:S(2)}) async-start(bf16[16,3,32,2176]{3,2,1,0:T(8,128)(2,1)} %branch_1_fun.19), calls=%async_computation.3 | async-start | bytes 13369344 | tf_op jit(solution)/shard_map/cond/branch_1_fun/all_to_all | solution.py:290
  224.9 14.0 %copy-start.1 = (s32[256,256]{1,0:T(8,128)S(1)}, s32[256,256]{1,0:T(8,128)}, u32[]{:S(2)}) copy-start(s32[256,256]{1,0:T(8,128)} %get-tuple-element.107.refs_3_) | copy-start | bytes 786436 | tf_op jit(solution)/shard_map/cond
  326.2 75.0 %all-to-all-start.2 = ((bf16[16,2,16,2176]{3,2,1,0:T(8,128)(2,1)}), bf16[16,2,16,2176]{3,2,1,0:T(8,128)(2,1)S(1)}, u32[]{:S(2)}, u32[]{:S(2)}) async-start(bf16[16,2,16,2176]{3,2,1,0:T(8,128)(2,1)} %get-tuple-element.108), calls=%async_computation.2 | async-start | bytes 4456448 | tf_op jit(solution)/shard_map/cond/branch_1_fun/all_to_all | solution.py:290
  401.3 1.3 copy-start.4
  402.6 60.5 %all-to-all-start.4 = ((bf16[16,2,16,2176]{3,2,1,0:T(8,128)(2,1)}), bf16[16,2,16,2176]{3,2,1,0:T(8,128)(2,1)S(1)}, u32[]{:S(2)}, u32[]{:S(2)}) async-start(bf16[16,2,16,2176]{3,2,1,0:T(8,128)(2,1)} %get-tuple-element.114), calls=%async_computation.4 | async-start | bytes 4456448 | tf_op jit(solution)/shard_map/cond/branch_1_fun/all_to_all | solution.py:290
  433.7 25.8 %collective-permute-start = (bf16[2,4,256,256]{3,2,1,0:T(8,128)(2,1)}, bf16[2,4,256,256]{3,2,1,0:T(8,128)(2,1)}, u32[]{:S(2)}, u32[]{:S(2)}) collective-permute-start(bf16[2,4,256,256]{3,2,1,0:T(8,128)(2,1)} %branch_1_fun.31), channel_id=1, source_target_pairs={{0,1},{1,0},{2,3},{3,2},{4,5},{5,4},{6,7},{7,6},{8,9},{9,8},{10,11... | collective-permute-start | bytes 3145736 | tf_op jit(solution)/shard_map/cond/branch_1_fun/ppermute | solution.py:338
  463.1 9.9 %copy-start.3 = (bf16[16,2,16,2176]{3,2,1,0:T(8,128)(2,1)}, bf16[16,2,16,2176]{3,2,1,0:T(8,128)(2,1)S(1)}, u32[]{:S(2)}) copy-start(bf16[16,2,16,2176]{3,2,1,0:T(8,128)(2,1)S(1)} %all-to-all-done.4.in_ref) | copy-start | bytes 6684676 | tf_op jit(solution)/shard_map/cond
  466.9 36.0 %all-to-all-start.5 = ((bf16[2,4,256,256]{3,1,0,2:T(4,128)(2,1)}), bf16[2,4,256,256]{3,1,0,2:T(4,128)(2,1)}, u32[]{:S(2)}, u32[]{:S(2)}) async-start(bf16[2,4,256,256]{3,1,0,2:T(4,128)(2,1)} %copy.103), calls=%async_computation.5 | async-start | bytes 2097152 | tf_op jit(solution)/shard_map/cond/branch_1_fun/all_to_all | solution.py:350
  491.7 14.6 %collective-permute-start.1 = (bf16[2,2,256,256]{3,2,1,0:T(8,128)(2,1)}, bf16[2,2,256,256]{3,2,1,0:T(8,128)(2,1)}, u32[]{:S(2)}, u32[]{:S(2)}) collective-permute-start(bf16[2,2,256,256]{3,2,1,0:T(8,128)(2,1)} %branch_1_fun.34), channel_id=1, source_target_pairs={{0,1},{1,0},{2,3},{3,2},{4,5},{5,4},{6,7},{7,6},{8,9},{9,8},{10,11... | collective-permute-start | bytes 1572872 | tf_op jit(solution)/shard_map/cond/branch_1_fun/ppermute | solution.py:338
  502.9 3.4 copy-start.7
  509.1 20.2 %all-to-all-start.6 = ((bf16[2,2,256,256]{3,1,0,2:T(2,128)(2,1)}), bf16[2,2,256,256]{3,1,0,2:T(2,128)(2,1)S(1)}, u32[]{:S(2)}, u32[]{:S(2)}) async-start(bf16[2,2,256,256]{3,1,0,2:T(2,128)(2,1)} %copy.107), calls=%async_computation.6 | async-start | bytes 1048576 | tf_op jit(solution)/shard_map/cond/branch_1_fun/all_to_all | solution.py:350
  514.8 15.4 %collective-permute-start.3 = (bf16[2,2,256,256]{3,2,1,0:T(8,128)(2,1)}, bf16[2,2,256,256]{3,2,1,0:T(8,128)(2,1)}, u32[]{:S(2)}, u32[]{:S(2)}) collective-permute-start(bf16[2,2,256,256]{3,2,1,0:T(8,128)(2,1)} %branch_1_fun.35), channel_id=1, source_target_pairs={{0,1},{1,0},{2,3},{3,2},{4,5},{5,4},{6,7},{7,6},{8,9},{9,8},{10,11... | collective-permute-start | bytes 1572872 | tf_op jit(solution)/shard_map/cond/branch_1_fun/ppermute | solution.py:338
  533.3 23.0 %all-to-all-start.7 = ((bf16[2,2,256,256]{3,1,0,2:T(2,128)(2,1)}), bf16[2,2,256,256]{3,1,0,2:T(2,128)(2,1)}, u32[]{:S(2)}, u32[]{:S(2)}) async-start(bf16[2,2,256,256]{3,1,0,2:T(2,128)(2,1)} %copy.110), calls=%async_computation.7 | async-start | bytes 1048576 | tf_op jit(solution)/shard_map/cond/branch_1_fun/all_to_all | solution.py:350
  539.1 15.1 %collective-permute-start.2 = (bf16[2,8,4,16,256]{4,3,2,1,0:T(8,128)(2,1)}, bf16[2,8,4,16,256]{4,3,2,1,0:T(8,128)(2,1)}, u32[]{:S(2)}, u32[]{:S(2)}) collective-permute-start(bf16[2,8,4,16,256]{4,3,2,1,0:T(8,128)(2,1)} %dynamic-slice_bitcast_fusion.3), channel_id=1, source_target_pairs={{0,1},{1,0},{2,3},{3,2},{4,5},{5,4},{6,7},{7,6},{8,9},{9,8},{10,11... | collective-permute-start | bytes 1572872 | tf_op jit(solution)/shard_map/cond/branch_1_fun/ppermute | solution.py:362
  541.8 17.3 %collective-permute-start.4 = (bf16[2,8,2,16,256]{4,3,2,1,0:T(8,128)(2,1)S(1)}, bf16[2,8,2,16,256]{4,3,2,1,0:T(8,128)(2,1)S(1)}, u32[]{:S(2)}, u32[]{:S(2)}) collective-permute-start(bf16[2,8,2,16,256]{4,3,2,1,0:T(8,128)(2,1)S(1)} %dynamic-slice_bitcast_fusion.5), channel_id=1, source_target_pairs={{0,1},{1,0},{2,3},{3,2},{4,5},{5,4},{6,7},{7,6},{8,9},{9,8},{10,11... | collective-permute-start | bytes 786440 | tf_op jit(solution)/shard_map/cond/branch_1_fun/ppermute | solution.py:362
  557.5 7.3 %collective-permute-start.5 = (bf16[2,8,2,16,256]{4,3,2,1,0:T(8,128)(2,1)S(1)}, bf16[2,8,2,16,256]{4,3,2,1,0:T(8,128)(2,1)S(1)}, u32[]{:S(2)}, u32[]{:S(2)}) collective-permute-start(bf16[2,8,2,16,256]{4,3,2,1,0:T(8,128)(2,1)S(1)} %dynamic-slice_bitcast_fusion.4), channel_id=1, source_target_pairs={{0,1},{1,0},{2,3},{3,2},{4,5},{5,4},{6,7},{7,6},{8,9},{9,8},{10,11... | collective-permute-start | bytes 786440 | tf_op jit(solution)/shard_map/cond/branch_1_fun/ppermute | solution.py:362
  565.3 1.3 copy-start.8
Sparse Core Ops, SparseCore 0:
  24.1 59.4 all-gather.4

commit v4 on v3

--- a/solution.py
+++ b/solution.py
@@ -11,6 +11,7 @@
 F32 = jnp.float32
 BF16 = jnp.bfloat16
 VMEM = 56 * 1024 * 1024
+STEP = 2
 
 
 def tables(length):
@@ -32,18 +33,36 @@
     return pl.CostEstimate(flops=int(flops), bytes_accessed=int(bytes_accessed), transcendentals=0)
 
 
+def layout_kernel(slab, mask_ref, place_ref, most_ref):
+    edge = mask_ref.shape[1]
+    half = edge // 2
+    row = lax.broadcasted_iota(jnp.int32, (edge, edge), 0)
+    column = lax.broadcasted_iota(jnp.int32, (edge, edge), 1)
+    sampled = mask_ref[...] != 0
+
+    def flags(where):
+        return jnp.where(where, 1.0, 0.0).astype(BF16)
+
+    rank = dot(flags(sampled), flags(row < column))
+    over = jnp.maximum(dot(flags(sampled), flags(row >= 0)) - half, 0.0).astype(BF16)
+    together = lax.div(row, slab) == lax.div(column, slab)
+    before = dot(flags(together & (column < row)), over)
+    most_ref[0] = jnp.max(dot(flags(together), over)).astype(jnp.int32)
+    place = rank + jnp.where(rank < half, 0.0, before)
+    place_ref[...] = jnp.where(sampled, place, -1.0).astype(jnp.int32)
+
+
 def layout(line_mask, parts):
-    edge = line_mask.shape[1]
-    slab = line_mask.shape[0] // parts
-    half = edge // 2
-    sampled = line_mask != 0
-    upper = jnp.triu(jnp.ones((edge, edge), BF16), 1)
-    rank = jnp.dot(sampled.astype(BF16), upper, preferred_element_type=F32).astype(jnp.int32)
-    over = jnp.maximum(jnp.sum(sampled.astype(jnp.int32), axis=1).reshape(parts, slab) - half, 0)
-    fits = jnp.all(jnp.sum(over, axis=1) <= half)
-    before = (jnp.cumsum(over, axis=1) - over).reshape(-1, 1)
-    place = jnp.where(sampled, rank + jnp.where(rank < half, 0, before), -1)
-    return fits, place, half * (slab + 1)
+    lines, edge = line_mask.shape
+    slab = lines // parts
+    place, most = pl.pallas_call(
+        functools.partial(layout_kernel, slab),
+        out_specs=[pl.BlockSpec(memory_space=pltpu.VMEM), pl.BlockSpec(memory_space=pltpu.SMEM)],
+        out_shape=[jax.ShapeDtypeStruct(line_mask.shape, jnp.int32), jax.ShapeDtypeStruct((1,), jnp.int32)],
+        compiler_params=pltpu.CompilerParams(vmem_limit_bytes=VMEM),
+        cost_estimate=cost(8 * edge**3, 8 * edge**2),
+    )(line_mask)
+    return most[0] <= edge // 2, place, edge // 2 * (slab + 1)
 
 
 def compact_kernel(pieces, k_ref, s_ref, t_ref, *refs):
@@ -104,15 +123,16 @@
     )(data, select, by_destination(table, parts, pieces))
 
 
-def expand_kernel(place_ref, in_ref, out_ref, lines_ref):
+def expand_kernel(slab, place_ref, in_ref, out_ref, lines_ref):
     edge = place_ref.shape[1]
     half = edge // 2
-    slab, rows, _ = lines_ref.shape
+    lines, rows, _ = lines_ref.shape
     places = lax.broadcasted_iota(jnp.int32, (edge, edge), 0)
-    shared = in_ref[0, :, :, slab * half :].reshape(rows, half)
-    for k in range(slab):
+    for k in range(lines):
         chosen = jnp.where(places == place_ref[k : k + 1, :], 1.0, 0.0).astype(BF16)
-        own = in_ref[0, :, :, k * half : (k + 1) * half].reshape(rows, half)
+        at = k % slab * half
+        own = in_ref[k // slab, :, :, at : at + half].reshape(rows, half)
+        shared = in_ref[k // slab, :, :, slab * half :].reshape(rows, half)
         lines_ref[k] = dot(jnp.concatenate([own, shared], axis=1), chosen).astype(BF16)
     for at in range(0, rows, 16):
         out_ref[at : at + 16] = jnp.swapaxes(lines_ref[:, at : at + 16, :], 0, 1)
@@ -123,16 +143,17 @@
     edge = place.shape[1]
     slab = place.shape[0] // parts
     rows = coils * rows
+    slabs = STEP if parts % STEP == 0 else 1
     return pl.pallas_call(
-        expand_kernel,
-        grid=(parts,),
+        functools.partial(expand_kernel, slab),
+        grid=(parts // slabs,),
         in_specs=[
-            pl.BlockSpec((slab, edge), lambda d: (d, 0)),
-            pl.BlockSpec((1,) + arrived.shape[1:], lambda d: (d, 0, 0, 0)),
+            pl.BlockSpec((slabs * slab, edge), lambda d: (d, 0)),
+            pl.BlockSpec((slabs,) + arrived.shape[1:], lambda d: (d, 0, 0, 0)),
         ],
-        out_specs=pl.BlockSpec((rows, slab, edge), lambda d: (0, d, 0)),
+        out_specs=pl.BlockSpec((rows, slabs * slab, edge), lambda d: (0, d, 0)),
         out_shape=jax.ShapeDtypeStruct((rows, parts * slab, edge), BF16),
-        scratch_shapes=[pltpu.VMEM((slab, rows, edge), BF16)],
+        scratch_shapes=[pltpu.VMEM((slabs * slab, rows, edge), BF16)],
         compiler_params=pltpu.CompilerParams(vmem_limit_bytes=VMEM),
         cost_estimate=cost(parts * slab * rows * edge * edge * 2, 2 * (arrived.size + parts * slab * rows * edge)),
     )(place, arrived)
@@ -229,6 +250,22 @@
     )(start, maps, coil_kspace, hybrid, line_mask, left, right, *([] if first else [before]))
 
 
+def exchange(sent):
+    return lax.all_to_all(sent, "cuts", split_axis=0, concat_axis=0, tiled=True)
+
+
+def gather(coil_groups, mine, volume):
+    planes, width = volume.shape[:2], volume.shape[2]
+    whole = jnp.zeros(planes + (coil_groups * width, volume.shape[3]), BF16)
+    for s in range(coil_groups):
+        moved = volume
+        if s:
+            moved = lax.ppermute(volume, "coil", [(i, (i + s) % coil_groups) for i in range(coil_groups)])
+        source = lax.rem(mine + coil_groups - s, coil_groups)
+        whole = lax.dynamic_update_slice_in_dim(whole, moved, source * width, 2)
+    return whole
+
+
 def body(coil_groups, volume, coil_maps, kspace, line_mask):
     coils, _, deep, edge, _ = coil_maps.shape
     slab = kspace.shape[3]
@@ -250,7 +287,7 @@
     group = min(4, deep)
 
     def step(pack, unpack):
-        full_slab = lax.all_gather(volume, "coil", axis=2, tiled=True)
+        full_slab = gather(coil_groups, mine, volume)
         arrived = []
         total = coil_kspace = None
         for i in range(last):
@@ -286,9 +323,6 @@
 
         return finish(coil_groups, mine, full_slab, gradient, arrived, deep)
 
-    def exchange(sent):
-        return lax.all_to_all(sent, "cuts", split_axis=0, concat_axis=0, tiled=True)
-
     def send_sampled():
         own = lax.dynamic_slice_in_dim(place, me * slab, slab, 0)
         select = (own[..., None] == jnp.arange(edge)).astype(BF16)
@@ -345,22 +379,23 @@
             summed = summed + term.astype(F32)
         base = lax.dynamic_slice_in_dim(full_slab, first + mine * share, share, 1).astype(F32)
         updated = (base - 0.5 * summed).astype(BF16)
+        updated = updated.reshape(2, share, parts, edge // parts, edge).transpose(2, 0, 1, 3, 4)
         if p + 1 < len(arrived):
             updated, arrived[p + 1] = lax.optimization_barrier((updated, arrived[p + 1]))
-        return lax.all_to_all(updated, "cuts", split_axis=2, concat_axis=1, tiled=True)
+        return exchange(updated)
 
     def to_groups(updated):
-        slab = updated.shape[2]
-        share = updated.shape[1] // parts
-        updated = updated.reshape(2, coil_groups, parts // coil_groups, share, slab, edge)
+        _, _, share, slab, _ = updated.shape
+        updated = updated.reshape(coil_groups, parts // coil_groups, 2, share, slab, edge)
         whole = jnp.zeros((2, parts // coil_groups, coil_groups, share, slab, edge), BF16)
         for s in range(coil_groups):
             to = lax.rem(mine + s, coil_groups)
             source = lax.rem(mine + coil_groups - s, coil_groups)
-            moved = lax.dynamic_index_in_dim(updated, to, 1, keepdims=False)
+            moved = lax.dynamic_index_in_dim(updated, to, 0, keepdims=False)
             if s:
                 moved = lax.ppermute(moved, "coil", rings[s])
-            whole = lax.dynamic_update_index_in_dim(whole, moved[:, :, None], source, 2)
+            moved = moved.transpose(1, 0, 2, 3, 4)[:, :, None]
+            whole = lax.dynamic_update_index_in_dim(whole, moved, source, 2)
         return whole.reshape(2, parts // coil_groups, coil_groups * share, slab, edge)
 
     out = []

time: 585 us -> 552 us (0.944)
  Pallas kernels: 303 us -> 288 us
  between operations: 14.6 us -> 0.96 us
  waiting for transfers between devices: 108 us -> 116 us
    ppermute x0 -> x1, waiting for transfers between devices: none -> 23.6 us  [gather(): lax.ppermute(volume, 'coil', [(i, (i + s) % coil_groups) for i in range(c...]
    all_gather x1 -> x0, waiting for transfers between devices: 19 us -> none  [step(): full_slab = lax.all_gather(volume, 'coil', axis=2, tiled=True)]
    all_to_all x3 -> x0, starting transfers between devices: 16.7 us -> none  [to_cuts(): lax.all_to_all(updated, 'cuts', split_axis=2, concat_axis=1, tiled=True)]
    all_to_all x5 -> x8, starting transfers between devices: 77.7 us -> 93.5 us  [exchange(): return lax.all_to_all(sent, 'cuts', split_axis=0, concat_axis=0, tiled=True)]
    pallas_call x5 -> x6, Pallas kernels: 74.2 us -> 59.6 us  [the longest x5 57.5 us: expand(): pl.pallas_call(functools.partial(expand_kernel, slab), grid=(parts // sla...]
    all_to_all x5 -> x8, waiting for transfers between devices: 45 us -> 57.9 us  [exchange(): return lax.all_to_all(sent, 'cuts', split_axis=0, concat_axis=0, tiled=True)]
    ppermute x3, waiting for transfers between devices: 17.3 us -> 8.44 us  [to_groups(): moved = lax.ppermute(moved, 'coil', rings[s])]
    all_to_all x3 -> x0, waiting for transfers between devices: 7.97 us -> none  [to_cuts(): lax.all_to_all(updated, 'cuts', split_axis=2, concat_axis=1, tiled=True)]
  transfers between devices with their start and end apart: 15 -> 15, of which waited for: 8 -> 9; matrix products, arithmetic and copies ran while one was open for 3% -> 3% of each run, Pallas kernels for 53% -> 51%
where the time goes in v4:
time: 552 us; the launch traced here: 543 us
  Pallas kernels  288 us (52%)
  waiting for transfers between devices  116 us (21%)
  starting transfers between devices  103 us (19%)
  local copies, waits for them, and re-layouts  19.3 us (3%)
  other arithmetic  9.89 us (2%)
  loops' own time  5.62 us (1%)
    pallas_call x9, Pallas kernels, backward(): pl.pallas_call(functools.partial(backward_kernel, first), grid_spec=spec,...  94.8 us
    all_to_all x8, starting transfers between devices, exchange(): return lax.all_to_all(sent, 'cuts', split_axis=0, concat_axis=0, tiled=True)  93.5 us
    pallas_call x4, Pallas kernels, compact(): pl.pallas_call(functools.partial(compact_kernel, pieces), grid=(coils,),...  75.6 us
    pallas_call x1, Pallas kernels, forward(): pl.pallas_call(forward_kernel, grid=(deep // group, coils), in_specs=[pl....  58 us
    all_to_all x8, waiting for transfers between devices, exchange(): return lax.all_to_all(sent, 'cuts', split_axis=0, concat_axis=0, tiled=True)  57.9 us
    pallas_call x5, Pallas kernels, expand(): pl.pallas_call(functools.partial(expand_kernel, slab), grid=(parts // sla...  57.5 us
    ppermute x3, waiting for transfers between devices, start(): lax.ppermute(term, 'coil', ring)  25.7 us
    ppermute x1, waiting for transfers between devices, gather(): lax.ppermute(volume, 'coil', [(i, (i + s) % coil_groups) for i in range(c...  23.6 us
  transfers between devices with their start and end apart: 15, of which 9 were waited for; matrix products, arithmetic and copies ran while one was open for 3% of the time, Pallas kernels for 51%

profile of v4, /device:TPU:0, one launch (start us, length us, event | category | flops | bytes accessed | tf_op | source)
XLA Modules:
  0.0 542.7 jit_solution(16863760262740711488)
XLA Ops:
  4.9 536.2 %conditional.1 = (bf16[2,128,16,256]{3,2,1,0:T(8,128)(2,1)S(1)}) conditional(s32[]{:T(128)} %bitcast.123, (s32[]{:T(128)}, bf16[512,512]{1,0:T(8,128)(2,1)S(1)}, bf16[8,2,256,16,256]{4,3,2,1,0:T(8,128)(2,1)}, bf16[2,16,128,256]{3,2,1,0:T(8,128)(2,1)}, bf16[8,2,16,256,256]{4,3,2,1,0:T(8,128)(2,1)}, /*index=5*/bf16[512,512]{1,0:T(8,128)(2,1)S(1)}, ...), branch_computations={%region_0.1_spmd, %region_1.2_spmd} | conditional | flops 95573508096 | bytes 825754368 | solution.py:352
  13.3 11.5 %branch_1_fun.24 = bf16[16,1,32,2176]{3,2,1,0:T(8,128)(2,1)} custom-call(bf16[8,2,256,16,256]{4,3,2,1,0:T(8,128)(2,1)} %get-tuple-element.65.k_ref, bf16[16,256,256]{2,1,0:T(8,128)(2,1)} %fusion.s_ref, bf16[512,512]{1,0:T(8,128)(2,1)} %bitcast.221), custom_call_target="tpu_custom_call" | custom-call | flops 2281701376 | bytes 6422528 | tf_op jit(solution)/shard_map/cond/branch_1_fun/pallas_call | solution.py:110
  24.8 7.4 %all-to-all-start.1 = ((bf16[16,1,32,2176]{3,2,1,0:T(8,128)(2,1)}), bf16[16,1,32,2176]{3,2,1,0:T(8,128)(2,1)S(1)}, u32[]{:S(2)}, u32[]{:S(2)}) async-start(bf16[16,1,32,2176]{3,2,1,0:T(8,128)(2,1)} %branch_1_fun.24), calls=%async_computation.1 | async-start | bytes 4456448 | tf_op jit(solution)/shard_map/cond/branch_1_fun/all_to_all | solution.py:254
  37.9 18.9 %branch_1_fun.20 = bf16[16,2,32,2176]{3,2,1,0:T(8,128)(2,1)} custom-call(bf16[8,2,256,16,256]{4,3,2,1,0:T(8,128)(2,1)} %get-tuple-element.65.k_ref, bf16[16,256,256]{2,1,0:T(8,128)(2,1)} %fusion.s_ref, bf16[512,512]{1,0:T(8,128)(2,1)} %bitcast.222), custom_call_target="tpu_custom_call" | custom-call | flops 4563402752 | bytes 12845056 | tf_op jit(solution)/shard_map/cond/branch_1_fun/pallas_call | solution.py:110
  56.9 23.6 %collective-permute-done = bf16[2,16,128,256]{3,2,1,0:T(8,128)(2,1)} collective-permute-done((bf16[2,16,128,256]{3,2,1,0:T(8,128)(2,1)}, bf16[2,16,128,256]{3,2,1,0:T(8,128)(2,1)}, u32[]{:S(2)}, u32[]{:S(2)}) %collective-permute-start) | collective-permute-done | bytes 2097184 | tf_op jit(solution)/shard_map/cond/branch_1_fun/ppermute | solution.py:263
  90.8 26.3 %branch_1_fun.19 = bf16[16,3,32,2176]{3,2,1,0:T(8,128)(2,1)} custom-call(bf16[8,2,256,16,256]{4,3,2,1,0:T(8,128)(2,1)} %get-tuple-element.65.k_ref, bf16[16,256,256]{2,1,0:T(8,128)(2,1)} %fusion.s_ref, bf16[512,512]{1,0:T(8,128)(2,1)} %bitcast.223), custom_call_target="tpu_custom_call" | custom-call | flops 6845104128 | bytes 19267584 | tf_op jit(solution)/shard_map/cond/branch_1_fun/pallas_call | solution.py:110
  117.0 58.0 %branch_1_fun.21.refs_1_ = bf16[8,16,512,256]{3,2,1,0:T(8,128)(2,1)} custom-call(bf16[8,2,16,256,256]{4,3,2,1,0:T(8,128)(2,1)} %get-tuple-element.64.maps_ref.refs_0_, bf16[2,16,256,256]{3,2,1,0:T(8,128)(2,1)} %constant_dynamic-update-slice_fusion.2.vol_ref, bf16[512,512]{1,0:T(8,128)(2,1)S(1)} %get-tuple-element.68.right_ref.refs_4_, ...), custom_call_target="tpu_custom_call" | custom-call | flops 34359738368 | bytes 67108864 | tf_op jit(solution)/shard_map/cond/branch_1_fun/pallas_call | solution.py:176
  175.0 18.9 %all-to-all-start.3 = ((bf16[16,3,32,2176]{3,2,1,0:T(8,128)(2,1)}), bf16[16,3,32,2176]{3,2,1,0:T(8,128)(2,1)}, u32[]{:S(2)}, u32[]{:S(2)}) async-start(bf16[16,3,32,2176]{3,2,1,0:T(8,128)(2,1)} %branch_1_fun.19), calls=%async_computation.3 | async-start | bytes 13369344 | tf_op jit(solution)/shard_map/cond/branch_1_fun/all_to_all | solution.py:254
  194.8 18.9 %branch_1_fun.22 = (bf16[16,2,16,2176]{3,2,1,0:T(8,128)(2,1)}, bf16[16,2,16,2176]{3,2,1,0:T(8,128)(2,1)}) custom-call(bf16[8,2,256,16,256]{4,3,2,1,0:T(8,128)(2,1)} %get-tuple-element.65.k_ref, bf16[16,256,256]{2,1,0:T(8,128)(2,1)} %fusion.s_ref, bf16[512,512]{1,0:T(8,128)(2,1)} %bitcast.235), custom_call_target="tpu_custom_call" | custom-call | flops 4563402752 | bytes 12845056 | tf_op jit(solution)/shard_map/cond/branch_1_fun/pallas_call | solution.py:110
  213.8 10.4 %branch_1_fun.25 = bf16[32,256,256]{2,1,0:T(8,128)(2,1)} custom-call(s32[256,256]{1,0:T(8,128)S(1)} %copy-done.8, bf16[16,1,32,2176]{3,2,1,0:T(8,128)(2,1)} %copy-done.3), custom_call_target="tpu_custom_call" | custom-call | flops 1073741824 | bytes 6422528 | tf_op jit(solution)/shard_map/cond/branch_1_fun/pallas_call | solution.py:147
  224.2 11.1 %branch_1_fun.26.refs_6_ = f32[2,16,256,256]{3,2,1,0:T(8,128)} custom-call(s32[1]{0:T(128)} %constant.249.clone.at_ref, bf16[8,2,16,256,256]{4,3,2,1,0:T(8,128)(2,1)} %get-tuple-element.64.maps_ref.refs_0_, bf16[8,16,512,256]{3,2,1,0:T(8,128)(2,1)} %branch_1_fun.21.refs_1_, bf16[1,2,16,256,256]{4,3,2,1,0:T(8,128)(2,1)} %bitcast.219, ...), custom_call_target="tpu_custom_call" | custom-call | flops 4294967296 | bytes 29360128 | tf_op jit(solution)/shard_map/cond/branch_1_fun/pallas_call | solution.py:244
  235.2 12.3 %branch_1_fun.23 = bf16[64,256,256]{2,1,0:T(8,128)(2,1)} custom-call(s32[256,256]{1,0:T(8,128)S(1)} %copy-done.8, bf16[16,2,32,2176]{3,2,1,0:T(8,128)(2,1)} %all-to-all-done.in_ref), custom_call_target="tpu_custom_call" | custom-call | flops 2147483648 | bytes 12845056 | tf_op jit(solution)/shard_map/cond/branch_1_fun/pallas_call | solution.py:147
  247.6 21.3 %branch_1_fun.27.refs_6_ = f32[2,16,256,256]{3,2,1,0:T(8,128)} custom-call(s32[1]{0:T(128)} %constant.249.clone.at_ref, bf16[8,2,16,256,256]{4,3,2,1,0:T(8,128)(2,1)} %get-tuple-element.64.maps_ref.refs_0_, bf16[8,16,512,256]{3,2,1,0:T(8,128)(2,1)} %branch_1_fun.21.refs_1_, bf16[2,2,16,256,256]{4,3,2,1,0:T(8,128)(2,1)} %bitcast.217, ...), custom_call_target="tpu_custom_call" | custom-call | flops 8589934592 | bytes 41943040 | tf_op jit(solution)/shard_map/cond/branch_1_fun/pallas_call | solution.py:244
  268.8 46.1 %all-to-all-done.3.in_ref = bf16[16,3,32,2176]{3,2,1,0:T(8,128)(2,1)} async-done(((bf16[16,3,32,2176]{3,2,1,0:T(8,128)(2,1)}), bf16[16,3,32,2176]{3,2,1,0:T(8,128)(2,1)}, u32[]{:S(2)}, u32[]{:S(2)}) %all-to-all-start.3) | async-done | bytes 6684704 | tf_op jit(solution)/shard_map/cond/branch_1_fun/all_to_all | solution.py:254
  315.0 29.6 %all-to-all-start.2 = ((bf16[16,2,16,2176]{3,2,1,0:T(8,128)(2,1)}), bf16[16,2,16,2176]{3,2,1,0:T(8,128)(2,1)S(1)}, u32[]{:S(2)}, u32[]{:S(2)}) async-start(bf16[16,2,16,2176]{3,2,1,0:T(8,128)(2,1)} %get-tuple-element.76), calls=%async_computation.2 | async-start | bytes 4456448 | tf_op jit(solution)/shard_map/cond/branch_1_fun/all_to_all | solution.py:254
  344.6 13.9 %branch_1_fun.29 = bf16[96,256,256]{2,1,0:T(8,128)(2,1)} custom-call(s32[256,256]{1,0:T(8,128)} %get-tuple-element.66.place_ref, bf16[16,3,32,2176]{3,2,1,0:T(8,128)(2,1)} %all-to-all-done.3.in_ref), custom_call_target="tpu_custom_call" | custom-call | flops 3221225472 | bytes 19267584 | tf_op jit(solution)/shard_map/cond/branch_1_fun/pallas_call | solution.py:147
  358.5 28.4 %branch_1_fun.30.refs_6_ = f32[2,16,256,256]{3,2,1,0:T(8,128)} custom-call(s32[1]{0:T(128)} %constant.249.clone.at_ref, bf16[8,2,16,256,256]{4,3,2,1,0:T(8,128)(2,1)} %get-tuple-element.64.maps_ref.refs_0_, bf16[8,16,512,256]{3,2,1,0:T(8,128)(2,1)} %branch_1_fun.21.refs_1_, bf16[3,2,16,256,256]{4,3,2,1,0:T(8,128)(2,1)} %bitcast.211, ...), custom_call_target="tpu_custom_call" | custom-call | flops 12884901888 | bytes 54525952 | tf_op jit(solution)/shard_map/cond/branch_1_fun/pallas_call | solution.py:244
  389.3 12.0 %all-to-all-start.4 = ((bf16[16,2,16,2176]{3,2,1,0:T(8,128)(2,1)}), bf16[16,2,16,2176]{3,2,1,0:T(8,128)(2,1)S(1)}, u32[]{:S(2)}, u32[]{:S(2)}) async-start(bf16[16,2,16,2176]{3,2,1,0:T(8,128)(2,1)} %get-tuple-element.82), calls=%async_computation.4 | async-start | bytes 4456448 | tf_op jit(solution)/shard_map/cond/branch_1_fun/all_to_all | solution.py:254
  401.3 10.4 %branch_1_fun.28 = bf16[32,256,256]{2,1,0:T(8,128)(2,1)} custom-call(s32[256,256]{1,0:T(8,128)} %get-tuple-element.66.place_ref, bf16[16,2,16,2176]{3,2,1,0:T(8,128)(2,1)} %copy-done.4), custom_call_target="tpu_custom_call" | custom-call | flops 1073741824 | bytes 6422528 | tf_op jit(solution)/shard_map/cond/branch_1_fun/pallas_call | solution.py:147
  420.4 7.5 %branch_1_fun.32 = f32[2,4,256,256]{3,2,1,0:T(8,128)} custom-call(s32[1]{0:T(128)} %bitcast.79.at_ref, bf16[8,2,16,256,256]{4,3,2,1,0:T(8,128)(2,1)} %get-tuple-element.64.maps_ref.refs_0_, bf16[8,16,512,256]{3,2,1,0:T(8,128)(2,1)} %branch_1_fun.21.refs_1_, bf16[2,2,8,256,256]{4,3,2,1,0:T(8,128)(2,1)} %bitcast.215, s32[256,256]{1,0:T(8,128)S(1)} %copy-done.1, ...), custom_call_target="tpu_custom_call" | custom-call | flops 2147483648 | bytes 10485760 | tf_op jit(solution)/shard_map/cond/branch_1_fun/pallas_call | solution.py:244
  427.9 16.8 %collective-permute-done.1 = bf16[2,4,256,256]{3,2,1,0:T(8,128)(2,1)} collective-permute-done((bf16[2,4,256,256]{3,2,1,0:T(8,128)(2,1)}, bf16[2,4,256,256]{3,2,1,0:T(8,128)(2,1)}, u32[]{:S(2)}, u32[]{:S(2)}) %collective-permute-start.1) | collective-permute-done | bytes 1048608 | tf_op jit(solution)/shard_map/cond/branch_1_fun/ppermute | solution.py:372
  448.5 8.0 %all-to-all-start.5 = ((bf16[16,2,4,16,256]{4,3,2,1,0:T(8,128)(2,1)}), bf16[16,2,4,16,256]{4,3,2,1,0:T(8,128)(2,1)}, u32[]{:S(2)}, u32[]{:S(2)}) async-start(bf16[16,2,4,16,256]{4,3,2,1,0:T(8,128)(2,1)} %bitcast.229), calls=%async_computation.5 | async-start | bytes 2097152 | tf_op jit(solution)/shard_map/cond/branch_1_fun/all_to_all | solution.py:254
  456.5 10.4 %branch_1_fun.33 = bf16[32,256,256]{2,1,0:T(8,128)(2,1)} custom-call(s32[256,256]{1,0:T(8,128)} %get-tuple-element.66.place_ref, bf16[16,2,16,2176]{3,2,1,0:T(8,128)(2,1)} %copy-done.2), custom_call_target="tpu_custom_call" | custom-call | flops 1073741824 | bytes 6422528 | tf_op jit(solution)/shard_map/cond/branch_1_fun/pallas_call | solution.py:147
  521.6 10.7 %all-to-all-done.7 = bf16[16,2,2,16,256]{4,3,2,1,0:T(8,128)(2,1)S(1)} async-done(((bf16[16,2,2,16,256]{4,3,2,1,0:T(8,128)(2,1)}), bf16[16,2,2,16,256]{4,3,2,1,0:T(8,128)(2,1)S(1)}, u32[]{:S(2)}, u32[]{:S(2)}) %all-to-all-start.7) | async-done | bytes 524320 | tf_op jit(solution)/shard_map/cond/branch_1_fun/all_to_all | solution.py:254
  (73 shorter events, 103.7 us)
Async XLA Ops:
  24.8 58.8 %all-to-all-start.1 = ((bf16[16,1,32,2176]{3,2,1,0:T(8,128)(2,1)}), bf16[16,1,32,2176]{3,2,1,0:T(8,128)(2,1)S(1)}, u32[]{:S(2)}, u32[]{:S(2)}) async-start(bf16[16,1,32,2176]{3,2,1,0:T(8,128)(2,1)} %branch_1_fun.24), calls=%async_computation.1 | async-start | bytes 4456448 | tf_op jit(solution)/shard_map/cond/branch_1_fun/all_to_all | solution.py:254
  32.2 48.3 %collective-permute-start = (bf16[2,16,128,256]{3,2,1,0:T(8,128)(2,1)}, bf16[2,16,128,256]{3,2,1,0:T(8,128)(2,1)}, u32[]{:S(2)}, u32[]{:S(2)}) collective-permute-start(bf16[2,16,128,256]{3,2,1,0:T(8,128)(2,1)} %get-tuple-element.69), channel_id=1, source_target_pairs={{0,1},{1,0},{2,3},{3,2},{4,5},{5,4},{6,7},{7,6},{8,9},{9,8},{10,11... | collective-permute-start | bytes 6291464 | tf_op jit(solution)/shard_map/cond/branch_1_fun/ppermute | solution.py:263
  33.7 2.6 copy-start.6
  83.6 1.4 copy-start.3
  85.0 90.1 %all-to-all-start = ((bf16[16,2,32,2176]{3,2,1,0:T(8,128)(2,1)}), bf16[16,2,32,2176]{3,2,1,0:T(8,128)(2,1)}, u32[]{:S(2)}, u32[]{:S(2)}) async-start(bf16[16,2,32,2176]{3,2,1,0:T(8,128)(2,1)} %branch_1_fun.20), calls=%async_computation | async-start | bytes 8912896 | tf_op jit(solution)/shard_map/cond/branch_1_fun/all_to_all | solution.py:254
  175.0 139.9 %all-to-all-start.3 = ((bf16[16,3,32,2176]{3,2,1,0:T(8,128)(2,1)}), bf16[16,3,32,2176]{3,2,1,0:T(8,128)(2,1)}, u32[]{:S(2)}, u32[]{:S(2)}) async-start(bf16[16,3,32,2176]{3,2,1,0:T(8,128)(2,1)} %branch_1_fun.19), calls=%async_computation.3 | async-start | bytes 13369344 | tf_op jit(solution)/shard_map/cond/branch_1_fun/all_to_all | solution.py:254
  194.8 18.9 %copy-start.8 = (s32[256,256]{1,0:T(8,128)S(1)}, s32[256,256]{1,0:T(8,128)}, u32[]{:S(2)}) copy-start(s32[256,256]{1,0:T(8,128)} %get-tuple-element.66.place_ref) | copy-start | bytes 786436 | tf_op jit(solution)/shard_map/cond
  213.8 10.4 %copy-start.1 = (s32[256,256]{1,0:T(8,128)S(1)}, s32[256,256]{1,0:T(8,128)}, u32[]{:S(2)}) copy-start(s32[256,256]{1,0:T(8,128)} %get-tuple-element.75.refs_3_) | copy-start | bytes 786436 | tf_op jit(solution)/shard_map/cond
  315.0 73.0 %all-to-all-start.2 = ((bf16[16,2,16,2176]{3,2,1,0:T(8,128)(2,1)}), bf16[16,2,16,2176]{3,2,1,0:T(8,128)(2,1)S(1)}, u32[]{:S(2)}, u32[]{:S(2)}) async-start(bf16[16,2,16,2176]{3,2,1,0:T(8,128)(2,1)} %get-tuple-element.76), calls=%async_computation.2 | async-start | bytes 4456448 | tf_op jit(solution)/shard_map/cond/branch_1_fun/all_to_all | solution.py:254
  388.0 1.3 copy-start.4
  389.3 59.1 %all-to-all-start.4 = ((bf16[16,2,16,2176]{3,2,1,0:T(8,128)(2,1)}), bf16[16,2,16,2176]{3,2,1,0:T(8,128)(2,1)S(1)}, u32[]{:S(2)}, u32[]{:S(2)}) async-start(bf16[16,2,16,2176]{3,2,1,0:T(8,128)(2,1)} %get-tuple-element.82), calls=%async_computation.4 | async-start | bytes 4456448 | tf_op jit(solution)/shard_map/cond/branch_1_fun/all_to_all | solution.py:254
  418.9 25.9 %collective-permute-start.1 = (bf16[2,4,256,256]{3,2,1,0:T(8,128)(2,1)}, bf16[2,4,256,256]{3,2,1,0:T(8,128)(2,1)}, u32[]{:S(2)}, u32[]{:S(2)}) collective-permute-start(bf16[2,4,256,256]{3,2,1,0:T(8,128)(2,1)} %branch_1_fun.31), channel_id=1, source_target_pairs={{0,1},{1,0},{2,3},{3,2},{4,5},{5,4},{6,7},{7,6},{8,9},{9,8},{10,11... | collective-permute-start | bytes 3145736 | tf_op jit(solution)/shard_map/cond/branch_1_fun/ppermute | solution.py:372
  448.5 8.0 %copy-start.2 = (bf16[16,2,16,2176]{3,2,1,0:T(8,128)(2,1)}, bf16[16,2,16,2176]{3,2,1,0:T(8,128)(2,1)S(1)}, u32[]{:S(2)}) copy-start(bf16[16,2,16,2176]{3,2,1,0:T(8,128)(2,1)S(1)} %all-to-all-done.4.in_ref) | copy-start | bytes 6684676 | tf_op jit(solution)/shard_map/cond
  448.5 37.6 %all-to-all-start.5 = ((bf16[16,2,4,16,256]{4,3,2,1,0:T(8,128)(2,1)}), bf16[16,2,4,16,256]{4,3,2,1,0:T(8,128)(2,1)}, u32[]{:S(2)}, u32[]{:S(2)}) async-start(bf16[16,2,4,16,256]{4,3,2,1,0:T(8,128)(2,1)} %bitcast.229), calls=%async_computation.5 | async-start | bytes 2097152 | tf_op jit(solution)/shard_map/cond/branch_1_fun/all_to_all | solution.py:254
  471.7 14.4 %collective-permute-start.2 = (bf16[2,2,256,256]{3,2,1,0:T(8,128)(2,1)}, bf16[2,2,256,256]{3,2,1,0:T(8,128)(2,1)S(1)}, u32[]{:S(2)}, u32[]{:S(2)}) collective-permute-start(bf16[2,2,256,256]{3,2,1,0:T(8,128)(2,1)} %branch_1_fun.34), channel_id=1, source_target_pairs={{0,1},{1,0},{2,3},{3,2},{4,5},{5,4},{6,7},{7,6},{8,9},{9,8},{10,11... | collective-permute-start | bytes 1572872 | tf_op jit(solution)/shard_map/cond/branch_1_fun/ppermute | solution.py:372
  482.9 11.4 %copy-start.10 = (bf16[2,2,256,256]{3,2,1,0:T(8,128)(2,1)S(1)}, bf16[2,2,256,256]{3,2,1,0:T(8,128)(2,1)}, u32[]{:S(2)}) copy-start(bf16[2,2,256,256]{3,2,1,0:T(8,128)(2,1)} %branch_1_fun.35) | copy-start | bytes 1572868 | tf_op jit(solution)/shard_map/cond
  488.5 20.7 %all-to-all-start.6 = ((bf16[16,2,2,16,256]{4,3,2,1,0:T(8,128)(2,1)}), bf16[16,2,2,16,256]{4,3,2,1,0:T(8,128)(2,1)S(1)}, u32[]{:S(2)}, u32[]{:S(2)}) async-start(bf16[16,2,2,16,256]{4,3,2,1,0:T(8,128)(2,1)} %bitcast.192), calls=%async_computation.6 | async-start | bytes 1048576 | tf_op jit(solution)/shard_map/cond/branch_1_fun/all_to_all | solution.py:254
  494.3 14.9 %collective-permute-start.4 = (bf16[2,2,256,256]{3,2,1,0:T(8,128)(2,1)S(1)}, bf16[2,2,256,256]{3,2,1,0:T(8,128)(2,1)}, u32[]{:S(2)}, u32[]{:S(2)}) collective-permute-start(bf16[2,2,256,256]{3,2,1,0:T(8,128)(2,1)S(1)} %copy-done.10), channel_id=1, source_target_pairs={{0,1},{1,0},{2,3},{3,2},{4,5},{5,4},{6,7},{7,6},{8,9},{9,8},{10,11... | collective-permute-start | bytes 1572872 | tf_op jit(solution)/shard_map/cond/branch_1_fun/ppermute | solution.py:372
  502.9 16.9 %collective-permute-start.3 = (bf16[8,2,4,16,256]{4,3,2,1,0:T(8,128)(2,1)}, bf16[8,2,4,16,256]{4,3,2,1,0:T(8,128)(2,1)S(1)}, u32[]{:S(2)}, u32[]{:S(2)}) collective-permute-start(bf16[8,2,4,16,256]{4,3,2,1,0:T(8,128)(2,1)} %get-tuple-element.135), channel_id=1, source_target_pairs={{0,1},{1,0},{2,3},{3,2},{4,5},{5,4},{6,7},{7,6},{8,9},{9,8},{10,11... | collective-permute-start | bytes 1572872 | tf_op jit(solution)/shard_map/cond/branch_1_fun/ppermute | solution.py:396
  511.7 20.5 %all-to-all-start.7 = ((bf16[16,2,2,16,256]{4,3,2,1,0:T(8,128)(2,1)}), bf16[16,2,2,16,256]{4,3,2,1,0:T(8,128)(2,1)S(1)}, u32[]{:S(2)}, u32[]{:S(2)}) async-start(bf16[16,2,2,16,256]{4,3,2,1,0:T(8,128)(2,1)} %bitcast.191), calls=%async_computation.7 | async-start | bytes 1048576 | tf_op jit(solution)/shard_map/cond/branch_1_fun/all_to_all | solution.py:254
  519.9 14.0 %collective-permute-start.5 = (bf16[8,2,2,16,256]{4,3,2,1,0:T(8,128)(2,1)S(1)}, bf16[8,2,2,16,256]{4,3,2,1,0:T(8,128)(2,1)S(1)}, u32[]{:S(2)}, u32[]{:S(2)}) collective-permute-start(bf16[8,2,2,16,256]{4,3,2,1,0:T(8,128)(2,1)S(1)} %get-tuple-element.137), channel_id=1, source_target_pairs={{0,1},{1,0},{2,3},{3,2},{4,5},{5,4},{6,7},{7,6},{8,9},{9,8},{10,11... | collective-permute-start | bytes 786440 | tf_op jit(solution)/shard_map/cond/branch_1_fun/ppermute | solution.py:396
  532.3 8.3 %collective-permute-start.6 = (bf16[8,2,2,16,256]{4,3,2,0,1:T(8,128)(2,1)S(1)}, bf16[8,2,2,16,256]{4,3,2,0,1:T(8,128)(2,1)S(1)}, u32[]{:S(2)}, u32[]{:S(2)}) collective-permute-start(bf16[8,2,2,16,256]{4,3,2,0,1:T(8,128)(2,1)S(1)} %copy.92), channel_id=1, source_target_pairs={{0,1},{1,0},{2,3},{3,2},{4,5},{5,4},{6,7},{7,6},{8,9},{9,8},{10,11... | collective-permute-start | bytes 786440 | tf_op jit(solution)/shard_map/cond/branch_1_fun/ppermute | solution.py:396
  541.1 1.3 copy-start.9

commit v5 on v4

--- a/solution.py
+++ b/solution.py
@@ -3,6 +3,7 @@
 
 import jax
 import jax.numpy as jnp
+import numpy as np
 from jax import lax
 from jax.experimental import pallas as pl
 from jax.experimental.pallas import tpu as pltpu
@@ -15,14 +16,10 @@
 
 
 def tables(length):
-    counter = jnp.arange(length, dtype=jnp.int32)
-    product = counter[:, None] * counter[None, :] % length
-    angles = product.astype(jnp.float32) * (2.0 * math.pi / length)
+    counter = np.arange(length)
+    angles = (counter[:, None] * counter[None, :] % length) * (2.0 * math.pi / length)
     factor = 1.0 / math.sqrt(length)
-    return (
-        (jnp.cos(angles) * factor).astype(jnp.bfloat16),
-        (jnp.sin(angles) * factor).astype(jnp.bfloat16),
-    )
+    return (np.cos(angles) * factor).astype(BF16), (np.sin(angles) * factor).astype(BF16)
 
 
 def dot(a, b):
@@ -69,7 +66,7 @@
     out_refs, lines_ref, over_ref = refs[:pieces], refs[pieces], refs[pieces + 1]
     slab, _, edge = lines_ref.shape
     half = edge // 2
-    parts, _, rows, _ = out_refs[0].shape
+    parts = out_refs[0].shape[0]
     step = 32
 
     @pl.loop(0, edge // step)
@@ -81,9 +78,12 @@
 
     def send(picked, places):
         moved = dot(t_ref[...], picked.astype(BF16)).astype(BF16)
-        moved = moved.reshape(parts, pieces, rows, picked.shape[1])
-        for p in range(pieces):
-            out_refs[p][:, 0, :, places] = moved[:, p]
+        moved = moved.reshape(parts, 2 * edge // parts, picked.shape[1])
+        first = 0
+        for out_ref in out_refs:
+            rows = out_ref.shape[2]
+            out_ref[:, 0, :, places] = moved[:, first : first + rows]
+            first += rows
 
     over_ref[...] = jnp.zeros_like(over_ref)
 
@@ -99,24 +99,26 @@
 
 
 def by_destination(table, parts, pieces):
-    size = table.shape[0]
-    rows = table.reshape(2, parts, pieces, size // (2 * parts * pieces), size)
-    return rows.transpose(1, 2, 0, 3, 4).reshape(size, size)
+    size = table.shape[0] // 2
+    rows = np.arange(2 * size).reshape(2, parts, size // parts)
+    cuts = np.split(rows, np.cumsum(pieces)[:-1], axis=2)
+    order = [cut.transpose(1, 0, 2).reshape(parts, -1) for cut in cuts]
+    return table[np.concatenate(order, axis=1).reshape(-1)]
 
 
 def compact(data, first_coil, coils, pieces, select, table, parts, slots):
     _, _, edge, slab, _ = data.shape
-    rows = 2 * edge // parts // pieces
+    blocks = [(parts, 1, 2 * planes, slots) for planes in pieces]
     return pl.pallas_call(
-        functools.partial(compact_kernel, pieces),
+        functools.partial(compact_kernel, len(pieces)),
         grid=(coils,),
         in_specs=[
             pl.BlockSpec((1, 2, edge, slab, edge), lambda c: (first_coil + c, 0, 0, 0, 0)),
             pl.BlockSpec(select.shape, lambda c: (0, 0, 0)),
             pl.BlockSpec(table.shape, lambda c: (0, 0)),
         ],
-        out_specs=[pl.BlockSpec((parts, 1, rows, slots), lambda c: (0, c, 0, 0))] * pieces,
-        out_shape=[jax.ShapeDtypeStruct((parts, coils, rows, slots), BF16)] * pieces,
+        out_specs=[pl.BlockSpec(block, lambda c: (0, c, 0, 0)) for block in blocks],
+        out_shape=[jax.ShapeDtypeStruct((parts, coils) + block[2:], BF16) for block in blocks],
         scratch_shapes=[pltpu.VMEM((slab, 2 * edge, edge), BF16), pltpu.VMEM((2 * edge, edge // 2), F32)],
         compiler_params=pltpu.CompilerParams(vmem_limit_bytes=VMEM),
         cost_estimate=cost(coils * 4 * slots * edge * 4 * edge, 4 * coils * edge * (slab * edge + slots)),
@@ -161,12 +163,17 @@
 
 def forward_kernel(maps_ref, vol_ref, right_ref, left_ref, out_ref):
     edge = vol_ref.shape[3]
-    for i in range(vol_ref.shape[1]):
+    group = vol_ref.shape[1]
+    rows = []
+    for i in range(group):
         map_real, map_imag = maps_ref[0, 0, i].astype(F32), maps_ref[0, 1, i].astype(F32)
         vol_real, vol_imag = vol_ref[0, i].astype(F32), vol_ref[1, i].astype(F32)
         real = (map_real * vol_real - map_imag * vol_imag).astype(BF16)
         imag = (map_real * vol_imag + map_imag * vol_real).astype(BF16)
-        along = dot(jnp.concatenate([real, imag], axis=1), right_ref[...]).astype(BF16)
+        rows.append(jnp.concatenate([real, imag], axis=1))
+    planes = dot(jnp.concatenate(rows, axis=0), right_ref[...]).astype(BF16)
+    for i in range(group):
+        along = planes[i * edge : (i + 1) * edge]
         stacked = jnp.concatenate([along[:, :edge], along[:, edge:]], axis=0)
         out_ref[0, i] = dot(left_ref[...], stacked).astype(BF16)
 
@@ -195,19 +202,23 @@
     else:
         maps_ref, k_ref, h_ref, mask_ref, left_ref, right_ref, before_ref, out_ref, sum_ref = refs
     edge = mask_ref.shape[1]
-    sampled = mask_ref[...].astype(F32)
+    sampled = mask_ref[...].astype(F32).astype(BF16)
     sampled = jnp.concatenate([sampled, sampled], axis=0)
 
     @pl.when(pl.program_id(1) == 0)
     def _():
         sum_ref[...] = jnp.zeros_like(sum_ref) if first else before_ref[...]
 
-    for i in range(k_ref.shape[1]):
+    group = k_ref.shape[1]
+    rows = []
+    for i in range(group):
         hybrid = h_ref[0, :, i].reshape(2 * edge, edge)
-        residual = (sampled * (k_ref[0, i].astype(F32) - hybrid.astype(F32))).astype(BF16)
+        residual = sampled * (k_ref[0, i] - hybrid)
         back = dot(left_ref[...], residual).astype(BF16)
-        back = jnp.concatenate([back[:edge], back[edge:]], axis=1)
-        back = dot(back, right_ref[...]).astype(BF16).astype(F32)
+        rows.append(jnp.concatenate([back[:edge], back[edge:]], axis=1))
+    planes = dot(jnp.concatenate(rows, axis=0), right_ref[...]).astype(BF16)
+    for i in range(group):
+        back = planes[i * edge : (i + 1) * edge].astype(F32)
         real, imag = back[:, :edge], back[:, edge:]
         map_real, map_imag = maps_ref[0, 0, i].astype(F32), maps_ref[0, 1, i].astype(F32)
         sum_ref[0, i] += map_real * real + map_imag * imag
@@ -219,7 +230,19 @@
 
 
 def backward(
-    maps, coil_kspace, line_mask, left, right, group, hybrid, hybrid_x, before, first_coil, first_x, count, kind
+    maps,
+    coil_kspace,
+    line_mask,
+    left,
+    right,
+    group,
+    hybrid,
+    hybrid_x,
+    before,
+    first_coil,
+    first_x,
+    count,
+    kind,
 ):
     coils, _, _, edge, _ = hybrid.shape
     group = min(group, count)
@@ -273,16 +296,16 @@
     me = lax.axis_index("cuts")
     mine = lax.axis_index("coil")
     cos_table, sin_table = tables(edge)
-    turn = jnp.block([[cos_table, sin_table], [-sin_table, cos_table]])
-    turn_back = jnp.block([[cos_table, -sin_table], [sin_table, cos_table]])
+    turn = np.block([[cos_table, sin_table], [-sin_table, cos_table]])
+    turn_back = np.block([[cos_table, -sin_table], [sin_table, cos_table]])
     fits, place, slots = layout(line_mask, parts)
-    if coils >= 6:
-        sizes = [1, (coils - 3) // 2, (coils - 2) // 2, 2]
+    if coils >= 8:
+        sizes = [1, coils - 5, 4]
     else:
         sizes = [1] * coils
     firsts = [sum(sizes[:i]) for i in range(len(sizes))]
-    pieces = min(2, deep // coil_groups)
-    planes = deep // pieces
+    quarter = deep // 4
+    pieces = [3 * quarter, quarter] if deep % (4 * coil_groups) == 0 else [deep]
     last = len(sizes) - 1
     group = min(4, deep)
 
@@ -291,12 +314,10 @@
         arrived = []
         total = coil_kspace = None
         for i in range(last):
-            (sent,) = pack(i, 1)
+            (sent,) = pack(i, [deep])
             if i == 1:
                 sent, full_slab = lax.optimization_barrier((sent, full_slab))
                 coil_kspace = forward(coil_maps, full_slab, turn_back, turn, group)
-            elif i == 2:
-                sent, coil_kspace = lax.optimization_barrier((sent, coil_kspace))
             arrived.append(exchange(sent))
         if coil_kspace is None:
             coil_kspace = forward(coil_maps, full_slab, turn_back, turn, group)
@@ -305,19 +326,20 @@
         for i in range(last):
             if i == last - 1 and total is not None:
                 sent[0], total = lax.optimization_barrier((sent[0], total))
-            total = back(unpack(i, deep, arrived[i]), 0, total, firsts[i], 0, deep, F32)
-        if pieces > 1:
+            hybrid = unpack(i, deep, arrived[i])
+            total = back(hybrid, 0, total, firsts[i], 0, deep, F32)
+        if len(pieces) > 1:
             sent[1], total = lax.optimization_barrier((sent[1], total))
         arrived = [exchange(one) for one in sent]
 
         def gradient(p):
-            hybrid = unpack(last, planes, arrived[p])
+            hybrid = unpack(last, pieces[p], arrived[p])
 
             def planes_from(first_x, count, kind, earlier=None):
                 before = total
                 if earlier is not None:
                     _, before = lax.optimization_barrier((earlier, total))
-                return back(hybrid, p * planes, before, firsts[last], first_x, count, kind)
+                return back(hybrid, sum(pieces[:p]), before, firsts[last], first_x, count, kind)
 
             return planes_from
 
@@ -341,8 +363,9 @@
             data = part.transpose(0, 3, 1, 2, 4).reshape(sizes[i], slab, 2 * edge, edge)
             table = by_destination(turn_back, parts, pieces)
             moved = jnp.einsum("xn,ckny->xcky", table, data, preferred_element_type=F32).astype(BF16)
-            moved = moved.reshape(parts, pieces, 2, deep // pieces, sizes[i], slab, edge)
-            return [moved[:, p] for p in range(pieces)]
+            moved = moved.reshape(parts, 2 * deep, sizes[i], slab, edge)
+            out = jnp.split(moved, [2 * sum(pieces[:p]) for p in range(1, len(pieces))], axis=1)
+            return [one.reshape(parts, 2, one.shape[1] // 2, sizes[i], slab, edge) for one in out]
 
         def unpack(i, planes, arrived):
             return arrived.transpose(3, 1, 2, 0, 4, 5).reshape(sizes[i], 2, planes, edge, edge)
@@ -355,23 +378,26 @@
 def finish(coil_groups, mine, full_slab, gradient, arrived, deep):
     edge = full_slab.shape[2]
     parts = edge // deep
-    share = deep // coil_groups // len(arrived)
     rings = [[(i, (i + s) % coil_groups) for i in range(coil_groups)] for s in range(coil_groups)]
-    pieces = [(p, p * coil_groups * share, share) for p in range(len(arrived))]
-    if share % 2 == 0:
-        p, first, _ = pieces.pop()
-        pieces += [(p, first, share // 2), (p, first + coil_groups * share // 2, share // 2)]
-
-    def start(p):
+    quarter = deep // coil_groups // 4
+    if len(arrived) > 1:
+        pieces = [(0, 0, 2 * quarter), (0, deep // 2, quarter), (1, deep * 3 // 4, quarter)]
+    else:
+        pieces = [(0, 0, deep // coil_groups)]
+
+    def leave(p):
         one = gradient(p)
-        mine_of = [piece for piece in pieces if piece[0] == p]
-        leave = [
+        return one, [
             [one(first + lax.rem(mine + s, coil_groups) * share, share, BF16) for s in range(1, coil_groups)]
-            for _, first, share in mine_of
+            for at, first, share in pieces
+            if at == p
         ]
-        away = [[lax.ppermute(term, "coil", ring) for term, ring in zip(terms, rings[1:])] for terms in leave]
-        stay = [one(first + mine * share, share, F32, leave) for _, first, share in mine_of]
-        return away, stay
+
+    def send(terms):
+        return [[lax.ppermute(term, "coil", ring) for term, ring in zip(piece, rings[1:])] for piece in terms]
+
+    def stay(p, one, terms):
+        return [one(first + mine * share, share, F32, terms) for at, first, share in pieces if at == p]
 
     def to_cuts(i, away, summed):
         p, first, share = pieces[i]
@@ -380,9 +406,9 @@
         base = lax.dynamic_slice_in_dim(full_slab, first + mine * share, share, 1).astype(F32)
         updated = (base - 0.5 * summed).astype(BF16)
         updated = updated.reshape(2, share, parts, edge // parts, edge).transpose(2, 0, 1, 3, 4)
-        if p + 1 < len(arrived):
+        if i == 0 and len(arrived) > 1:
             updated, arrived[p + 1] = lax.optimization_barrier((updated, arrived[p + 1]))
-        return exchange(updated)
+        return updated
 
     def to_groups(updated):
         _, _, share, slab, _ = updated.shape
@@ -399,12 +425,16 @@
         return whole.reshape(2, parts // coil_groups, coil_groups * share, slab, edge)
 
     out = []
-    away, stay = start(0)
+    one, terms = leave(0)
+    away, here = send(terms), stay(0, one, terms)
     for i, (p, _, _) in enumerate(pieces):
-        updated = to_cuts(i, away.pop(0), stay.pop(0))
+        updated = to_cuts(i, away.pop(0), here.pop(0))
+        if i + 1 < len(pieces) and not away:
+            one, terms = leave(p + 1)
+            updated, terms = lax.optimization_barrier((updated, terms))
+            away, here = send(terms), stay(p + 1, one, terms)
+        updated = exchange(updated)
         if i + 1 < len(pieces):
-            if not away:
-                away, stay = start(p + 1)
             away[0], updated = lax.optimization_barrier((away[0], updated))
         out.append(to_groups(updated))
     out = jnp.concatenate(out, axis=2)

time: 552 us -> 529 us (0.958); the launches traced: 543 us -> 525 us
  Pallas kernels: 288 us -> 257 us
  waiting for transfers between devices: 116 us -> 144 us
    all_to_all x8 -> x7, waiting for transfers between devices: 57.9 us -> 107 us  [exchange(): return lax.all_to_all(sent, 'cuts', split_axis=0, concat_axis=0, tiled=True)]
    ppermute x3, waiting for transfers between devices: 25.7 us -> 10.8 us  [send(): lax.ppermute(term, 'coil', ring)]
    pallas_call x9 -> x8, Pallas kernels: 94.8 us -> 85.8 us  [backward(): pl.pallas_call(functools.partial(backward_kernel, first), grid_spec=spec,...]
    pallas_call x5 -> x4, Pallas kernels: 57.5 us -> 48.5 us  [expand(): pl.pallas_call(functools.partial(expand_kernel, slab), grid=(parts // sla...]
    pallas_call x1, Pallas kernels: 58 us -> 50 us  [forward(): pl.pallas_call(forward_kernel, grid=(deep // group, coils), in_specs=[pl....]
    ppermute x1, waiting for transfers between devices: 23.6 us -> 16.5 us  [gather(): lax.ppermute(volume, 'coil', [(i, (i + s) % coil_groups) for i in range(c...]
    pallas_call x4 -> x3, Pallas kernels: 75.6 us -> 71.1 us  [compact(): pl.pallas_call(functools.partial(compact_kernel, len(pieces)), grid=(coil...]
    all_to_all x8 -> x7, starting transfers between devices: 93.5 us -> 90.3 us  [exchange(): return lax.all_to_all(sent, 'cuts', split_axis=0, concat_axis=0, tiled=True)]
  transfers between devices with their start and end apart: 15 -> 14, of which waited for: 9 -> 8; matrix products, arithmetic and copies ran while one was open for 3% -> 3% of each run, Pallas kernels for 51% -> 46%
where the time goes in v5:
time: 529 us; the launch traced here: 525 us
  Pallas kernels  257 us (49%)
  waiting for transfers between devices  144 us (27%)
  starting transfers between devices  98.2 us (19%)
  local copies, waits for them, and re-layouts  17.3 us (3%)
  other arithmetic  7.46 us (1%)
    all_to_all x7, waiting for transfers between devices, exchange(): return lax.all_to_all(sent, 'cuts', split_axis=0, concat_axis=0, tiled=True)  107 us
    all_to_all x7, starting transfers between devices, exchange(): return lax.all_to_all(sent, 'cuts', split_axis=0, concat_axis=0, tiled=True)  90.3 us
    pallas_call x8, Pallas kernels, backward(): pl.pallas_call(functools.partial(backward_kernel, first), grid_spec=spec,...  85.8 us
    pallas_call x3, Pallas kernels, compact(): pl.pallas_call(functools.partial(compact_kernel, len(pieces)), grid=(coil...  71.1 us
    pallas_call x1, Pallas kernels, forward(): pl.pallas_call(forward_kernel, grid=(deep // group, coils), in_specs=[pl....  50 us
    pallas_call x4, Pallas kernels, expand(): pl.pallas_call(functools.partial(expand_kernel, slab), grid=(parts // sla...  48.5 us
    ppermute x1, waiting for transfers between devices, gather(): lax.ppermute(volume, 'coil', [(i, (i + s) % coil_groups) for i in range(c...  16.5 us
    ppermute x3, waiting for transfers between devices, send(): lax.ppermute(term, 'coil', ring)  10.8 us
  transfers between devices with their start and end apart: 14, of which 8 were waited for; matrix products, arithmetic and copies ran while one was open for 3% of the time, Pallas kernels for 46%

profile of v5, /device:TPU:0, one launch (start us, length us, event | category | flops | bytes accessed | tf_op | source)
XLA Modules:
  0.0 525.5 jit_solution(5130123555112156236)
XLA Ops:
  2.8 521.4 %conditional.1 = (bf16[2,128,16,256]{3,2,1,0:T(8,128)(2,1)S(1)}) conditional(s32[]{:T(128)} %bitcast.102, (s32[]{:T(128)}, bf16[8,2,256,16,256]{4,3,2,1,0:T(8,128)(2,1)}, bf16[512,512]{1,0:T(8,128)(2,1)}, bf16[2,16,128,256]{3,2,1,0:T(8,128)(2,1)}, bf16[8,2,16,256,256]{4,3,2,1,0:T(8,128)(2,1)}, /*index=5*/bf16[512,512]{1,0:T(8,128)(2,1)}, ...), branch_computations={%region_0.1_spmd, %region_1.2_spmd} | conditional | flops 95573508096 | bytes 804258688 | solution.py:375
  5.4 11.5 %branch_1_fun.19 = bf16[16,1,32,2176]{3,2,1,0:T(8,128)(2,1)} custom-call(bf16[8,2,256,16,256]{4,3,2,1,0:T(8,128)(2,1)} %get-tuple-element.80.k_ref, bf16[16,256,256]{2,1,0:T(8,128)(2,1)} %fusion.3.s_ref, bf16[512,512]{1,0:T(8,128)(2,1)} %get-tuple-element.90.t_ref), custom_call_target="tpu_custom_call" | custom-call | flops 2281701376 | bytes 6422528 | tf_op jit(solution)/shard_map/cond/branch_1_fun/pallas_call | solution.py:112
  16.9 7.4 %all-to-all-start = ((bf16[16,1,32,2176]{3,2,1,0:T(8,128)(2,1)}), bf16[16,1,32,2176]{3,2,1,0:T(8,128)(2,1)S(1)}, u32[]{:S(2)}, u32[]{:S(2)}) async-start(bf16[16,1,32,2176]{3,2,1,0:T(8,128)(2,1)} %branch_1_fun.19), calls=%async_computation | async-start | bytes 4456448 | tf_op jit(solution)/shard_map/cond/branch_1_fun/all_to_all | solution.py:277
  30.0 26.0 %branch_1_fun.16 = bf16[16,3,32,2176]{3,2,1,0:T(8,128)(2,1)} custom-call(bf16[8,2,256,16,256]{4,3,2,1,0:T(8,128)(2,1)} %get-tuple-element.80.k_ref, bf16[16,256,256]{2,1,0:T(8,128)(2,1)} %fusion.3.s_ref, bf16[512,512]{1,0:T(8,128)(2,1)S(1)} %copy-done.16), custom_call_target="tpu_custom_call" | custom-call | flops 6845104128 | bytes 19267584 | tf_op jit(solution)/shard_map/cond/branch_1_fun/pallas_call | solution.py:112
  56.0 16.5 %collective-permute-done = bf16[2,16,128,256]{3,2,1,0:T(8,128)(2,1)} collective-permute-done((bf16[2,16,128,256]{3,2,1,0:T(8,128)(2,1)}, bf16[2,16,128,256]{3,2,1,0:T(8,128)(2,1)}, u32[]{:S(2)}, u32[]{:S(2)}) %collective-permute-start) | collective-permute-done | bytes 2097184 | tf_op jit(solution)/shard_map/cond/branch_1_fun/ppermute | solution.py:286
  83.0 33.6 %branch_1_fun.18 = (bf16[16,4,24,2176]{3,2,1,0:T(8,128)(2,1)}, bf16[16,4,8,2176]{3,2,1,0:T(8,128)(2,1)}) custom-call(bf16[8,2,256,16,256]{4,3,2,1,0:T(8,128)(2,1)} %get-tuple-element.80.k_ref, bf16[16,256,256]{2,1,0:T(8,128)(2,1)} %fusion.3.s_ref, bf16[512,512]{1,0:T(8,128)(2,1)} %get-tuple-element.88.t_ref), custom_call_target="tpu_custom_call" | custom-call | flops 9126805504 | bytes 25690112 | tf_op jit(solution)/shard_map/cond/branch_1_fun/pallas_call | solution.py:112
  116.6 50.0 %branch_1_fun.17.refs_1_ = bf16[8,16,512,256]{3,2,1,0:T(8,128)(2,1)} custom-call(bf16[8,2,16,256,256]{4,3,2,1,0:T(8,128)(2,1)} %get-tuple-element.79.maps_ref.refs_0_, bf16[2,16,256,256]{3,2,1,0:T(8,128)(2,1)} %constant_dynamic-update-slice_fusion.2.vol_ref, bf16[512,512]{1,0:T(8,128)(2,1)S(1)} %copy-done.3, bf16[512,512]{1,0:T(8,128)(2,1)S(1)} %copy-done.1), custom_call_target="tpu_custom_call" | custom-call | flops 34359738368 | bytes 67108864 | tf_op jit(solution)/shard_map/cond/branch_1_fun/pallas_call | solution.py:183
  166.6 10.4 %branch_1_fun.20 = bf16[32,256,256]{2,1,0:T(8,128)(2,1)} custom-call(s32[256,256]{1,0:T(8,128)S(1)} %copy-done.11, bf16[16,1,32,2176]{3,2,1,0:T(8,128)(2,1)} %copy-done.8), custom_call_target="tpu_custom_call" | custom-call | flops 1073741824 | bytes 6422528 | tf_op jit(solution)/shard_map/cond/branch_1_fun/pallas_call | solution.py:149
  177.0 10.6 %branch_1_fun.21.refs_6_ = f32[2,16,256,256]{3,2,1,0:T(8,128)} custom-call(s32[1]{0:T(128)} %constant.241.clone.at_ref, bf16[8,2,16,256,256]{4,3,2,1,0:T(8,128)(2,1)} %get-tuple-element.79.maps_ref.refs_0_, bf16[8,16,512,256]{3,2,1,0:T(8,128)(2,1)} %branch_1_fun.17.refs_1_, bf16[1,2,16,256,256]{4,3,2,1,0:T(8,128)(2,1)} %bitcast.186, ...), custom_call_target="tpu_custom_call" | custom-call | flops 4294967296 | bytes 29360128 | tf_op jit(solution)/shard_map/cond/branch_1_fun/pallas_call | solution.py:267
  187.7 16.4 %all-to-all-done.2.in_ref = bf16[16,3,32,2176]{3,2,1,0:T(8,128)(2,1)} async-done(((bf16[16,3,32,2176]{3,2,1,0:T(8,128)(2,1)}), bf16[16,3,32,2176]{3,2,1,0:T(8,128)(2,1)}, u32[]{:S(2)}, u32[]{:S(2)}) %all-to-all-start.2) | async-done | bytes 6684704 | tf_op jit(solution)/shard_map/cond/branch_1_fun/all_to_all | solution.py:277
  204.0 29.7 %all-to-all-start.1 = ((bf16[16,4,24,2176]{3,2,1,0:T(8,128)(2,1)}), bf16[16,4,24,2176]{3,2,1,0:T(8,128)(2,1)}, u32[]{:S(2)}, u32[]{:S(2)}) async-start(bf16[16,4,24,2176]{3,2,1,0:T(8,128)(2,1)} %get-tuple-element.92), calls=%async_computation.1 | async-start | bytes 13369344 | tf_op jit(solution)/shard_map/cond/branch_1_fun/all_to_all | solution.py:277
  233.7 13.9 %branch_1_fun.23 = bf16[96,256,256]{2,1,0:T(8,128)(2,1)} custom-call(s32[256,256]{1,0:T(8,128)S(1)} %copy-done.11, bf16[16,3,32,2176]{3,2,1,0:T(8,128)(2,1)} %all-to-all-done.2.in_ref), custom_call_target="tpu_custom_call" | custom-call | flops 3221225472 | bytes 19267584 | tf_op jit(solution)/shard_map/cond/branch_1_fun/pallas_call | solution.py:149
  247.6 27.0 %branch_1_fun.24.refs_6_ = f32[2,16,256,256]{3,2,1,0:T(8,128)} custom-call(s32[1]{0:T(128)} %constant.241.clone.at_ref, bf16[8,2,16,256,256]{4,3,2,1,0:T(8,128)(2,1)} %get-tuple-element.79.maps_ref.refs_0_, bf16[8,16,512,256]{3,2,1,0:T(8,128)(2,1)} %branch_1_fun.17.refs_1_, bf16[3,2,16,256,256]{4,3,2,1,0:T(8,128)(2,1)} %bitcast.180, ...), custom_call_target="tpu_custom_call" | custom-call | flops 12884901888 | bytes 54525952 | tf_op jit(solution)/shard_map/cond/branch_1_fun/pallas_call | solution.py:267
  274.6 80.2 %all-to-all-done.1.in_ref = bf16[16,4,24,2176]{3,2,1,0:T(8,128)(2,1)} async-done(((bf16[16,4,24,2176]{3,2,1,0:T(8,128)(2,1)}), bf16[16,4,24,2176]{3,2,1,0:T(8,128)(2,1)}, u32[]{:S(2)}, u32[]{:S(2)}) %all-to-all-start.1) | async-done | bytes 6684704 | tf_op jit(solution)/shard_map/cond/branch_1_fun/all_to_all | solution.py:277
  354.8 29.7 %all-to-all-start.3 = ((bf16[16,4,8,2176]{3,2,1,0:T(8,128)(2,1)}), bf16[16,4,8,2176]{3,2,1,0:T(8,128)(2,1)S(1)}, u32[]{:S(2)}, u32[]{:S(2)}) async-start(bf16[16,4,8,2176]{3,2,1,0:T(8,128)(2,1)} %get-tuple-element.98), calls=%async_computation.3 | async-start | bytes 4456448 | tf_op jit(solution)/shard_map/cond/branch_1_fun/all_to_all | solution.py:277
  384.5 13.9 %branch_1_fun.22 = bf16[96,256,256]{2,1,0:T(8,128)(2,1)} custom-call(s32[256,256]{1,0:T(8,128)} %get-tuple-element.81.place_ref, bf16[16,4,24,2176]{3,2,1,0:T(8,128)(2,1)} %all-to-all-done.1.in_ref), custom_call_target="tpu_custom_call" | custom-call | flops 3221225472 | bytes 19267584 | tf_op jit(solution)/shard_map/cond/branch_1_fun/pallas_call | solution.py:149
  398.4 10.2 %branch_1_fun.26 = bf16[2,4,256,256]{3,2,1,0:T(8,128)(2,1)} custom-call(s32[1]{0:T(128)} %bitcast.66.at_ref, bf16[8,2,16,256,256]{4,3,2,1,0:T(8,128)(2,1)} %get-tuple-element.79.maps_ref.refs_0_, bf16[8,16,512,256]{3,2,1,0:T(8,128)(2,1)} %branch_1_fun.17.refs_1_, bf16[4,2,12,256,256]{4,3,2,1,0:T(8,128)(2,1)} %bitcast.173, s32[256,256]{1,0:T(8,128)S(1)} %copy-done.5, ...), custom_call_target="tpu_custom_call" | custom-call | flops 4294967296 | bytes 16777216 | tf_op jit(solution)/shard_map/cond/branch_1_fun/pallas_call | solution.py:267
  416.7 10.6 %branch_1_fun.27 = f32[2,4,256,256]{3,2,1,0:T(8,128)} custom-call(s32[1]{0:T(128)} %bitcast.65.at_ref, bf16[8,2,16,256,256]{4,3,2,1,0:T(8,128)(2,1)} %get-tuple-element.79.maps_ref.refs_0_, bf16[8,16,512,256]{3,2,1,0:T(8,128)(2,1)} %branch_1_fun.17.refs_1_, bf16[4,2,12,256,256]{4,3,2,1,0:T(8,128)(2,1)} %bitcast.175, s32[256,256]{1,0:T(8,128)S(1)} %copy-done.5, ...), custom_call_target="tpu_custom_call" | custom-call | flops 4294967296 | bytes 16777216 | tf_op jit(solution)/shard_map/cond/branch_1_fun/pallas_call | solution.py:267
  427.3 7.1 %collective-permute-done.2 = bf16[2,4,256,256]{3,2,1,0:T(8,128)(2,1)} collective-permute-done((bf16[2,4,256,256]{3,2,1,0:T(8,128)(2,1)}, bf16[2,4,256,256]{3,2,1,0:T(8,128)(2,1)}, u32[]{:S(2)}, u32[]{:S(2)}) %collective-permute-start.2) | collective-permute-done | bytes 1048608 | tf_op jit(solution)/shard_map/cond/branch_1_fun/ppermute | solution.py:397
  445.2 6.9 %branch_1_fun.28 = f32[2,2,256,256]{3,2,1,0:T(8,128)} custom-call(s32[1]{0:T(128)} %bitcast.77.at_ref, bf16[8,2,16,256,256]{4,3,2,1,0:T(8,128)(2,1)} %get-tuple-element.79.maps_ref.refs_0_, bf16[8,16,512,256]{3,2,1,0:T(8,128)(2,1)} %branch_1_fun.17.refs_1_, bf16[4,2,12,256,256]{4,3,2,1,0:T(8,128)(2,1)} %bitcast.176, s32[256,256]{1,0:T(8,128)S(1)} %copy-done.5, ...), custom_call_target="tpu_custom_call" | custom-call | flops 2147483648 | bytes 8388608 | tf_op jit(solution)/shard_map/cond/branch_1_fun/pallas_call | solution.py:267
  452.2 10.3 %branch_1_fun.29 = bf16[32,256,256]{2,1,0:T(8,128)(2,1)} custom-call(s32[256,256]{1,0:T(8,128)S(1)} %copy-done.12, bf16[16,4,8,2176]{3,2,1,0:T(8,128)(2,1)} %copy-done.7), custom_call_target="tpu_custom_call" | custom-call | flops 1073741824 | bytes 6422528 | tf_op jit(solution)/shard_map/cond/branch_1_fun/pallas_call | solution.py:149
  481.7 6.9 %branch_1_fun.31 = f32[2,2,256,256]{3,2,1,0:T(8,128)} custom-call(s32[1]{0:T(128)} %bitcast.90.at_ref, bf16[8,2,16,256,256]{4,3,2,1,0:T(8,128)(2,1)} %get-tuple-element.79.maps_ref.refs_0_, bf16[8,16,512,256]{3,2,1,0:T(8,128)(2,1)} %branch_1_fun.17.refs_1_, bf16[4,2,4,256,256]{4,3,2,1,0:T(8,128)(2,1)} %bitcast.184, s32[256,256]{1,0:T(8,128)S(1)} %copy-done.5, ...), custom_call_target="tpu_custom_call" | custom-call | flops 2147483648 | bytes 8388608 | tf_op jit(solution)/shard_map/cond/branch_1_fun/pallas_call | solution.py:267
  505.2 10.1 %all-to-all-done.6 = bf16[16,2,2,16,256]{4,3,2,1,0:T(8,128)(2,1)S(1)} async-done(((bf16[16,2,2,16,256]{4,3,2,1,0:T(8,128)(2,1)}), bf16[16,2,2,16,256]{4,3,2,1,0:T(8,128)(2,1)S(1)}, u32[]{:S(2)}, u32[]{:S(2)}) %all-to-all-start.6) | async-done | bytes 524320 | tf_op jit(solution)/shard_map/cond/branch_1_fun/all_to_all | solution.py:277
  516.2 7.4 %collective-permute-done.6 = bf16[8,2,2,16,256]{4,3,2,0,1:T(8,128)(2,1)S(1)} collective-permute-done((bf16[8,2,2,16,256]{4,3,2,0,1:T(8,128)(2,1)S(1)}, bf16[8,2,2,16,256]{4,3,2,0,1:T(8,128)(2,1)S(1)}, u32[]{:S(2)}, u32[]{:S(2)}) %collective-permute-start.6) | collective-permute-done | bytes 262176 | tf_op jit(solution)/shard_map/cond/branch_1_fun/ppermute | solution.py:422
  (71 shorter events, 77.8 us)
Async XLA Ops:
  16.9 58.9 %all-to-all-start = ((bf16[16,1,32,2176]{3,2,1,0:T(8,128)(2,1)}), bf16[16,1,32,2176]{3,2,1,0:T(8,128)(2,1)S(1)}, u32[]{:S(2)}, u32[]{:S(2)}) async-start(bf16[16,1,32,2176]{3,2,1,0:T(8,128)(2,1)} %branch_1_fun.19), calls=%async_computation | async-start | bytes 4456448 | tf_op jit(solution)/shard_map/cond/branch_1_fun/all_to_all | solution.py:277
  24.3 48.3 %collective-permute-start = (bf16[2,16,128,256]{3,2,1,0:T(8,128)(2,1)}, bf16[2,16,128,256]{3,2,1,0:T(8,128)(2,1)}, u32[]{:S(2)}, u32[]{:S(2)}) collective-permute-start(bf16[2,16,128,256]{3,2,1,0:T(8,128)(2,1)} %get-tuple-element.84), channel_id=1, source_target_pairs={{0,1},{1,0},{2,3},{3,2},{4,5},{5,4},{6,7},{7,6},{8,9},{9,8},{10,11... | collective-permute-start | bytes 6291464 | tf_op jit(solution)/shard_map/cond/branch_1_fun/ppermute | solution.py:286
  25.8 2.6 copy-start.10
  25.8 4.1 copy-start.16
  77.2 126.8 %all-to-all-start.2 = ((bf16[16,3,32,2176]{3,2,1,0:T(8,128)(2,1)}), bf16[16,3,32,2176]{3,2,1,0:T(8,128)(2,1)}, u32[]{:S(2)}, u32[]{:S(2)}) async-start(bf16[16,3,32,2176]{3,2,1,0:T(8,128)(2,1)} %branch_1_fun.16), calls=%async_computation.2 | async-start | bytes 13369344 | tf_op jit(solution)/shard_map/cond/branch_1_fun/all_to_all | solution.py:277
  83.0 33.6 %copy-start.1 = (bf16[512,512]{1,0:T(8,128)(2,1)S(1)}, bf16[512,512]{1,0:T(8,128)(2,1)}, u32[]{:S(2)}) copy-start(bf16[512,512]{1,0:T(8,128)(2,1)} %get-tuple-element.87.left_ref.refs_5_) | copy-start | bytes 1572868 | tf_op jit(solution)/shard_map/cond
  83.0 33.6 %copy-start.3 = (bf16[512,512]{1,0:T(8,128)(2,1)S(1)}, bf16[512,512]{1,0:T(8,128)(2,1)}, u32[]{:S(2)}) copy-start(bf16[512,512]{1,0:T(8,128)(2,1)} %get-tuple-element.86.right_ref.refs_4_) | copy-start | bytes 1572868 | tf_op jit(solution)/shard_map/cond
  116.6 50.0 %copy-start.11 = (s32[256,256]{1,0:T(8,128)S(1)}, s32[256,256]{1,0:T(8,128)}, u32[]{:S(2)}) copy-start(s32[256,256]{1,0:T(8,128)} %get-tuple-element.81.place_ref) | copy-start | bytes 786436 | tf_op jit(solution)/shard_map/cond
  166.6 10.4 %copy-start.5 = (s32[256,256]{1,0:T(8,128)S(1)}, s32[256,256]{1,0:T(8,128)}, u32[]{:S(2)}) copy-start(s32[256,256]{1,0:T(8,128)} %get-tuple-element.91.refs_3_) | copy-start | bytes 786436 | tf_op jit(solution)/shard_map/cond
  204.0 150.7 %all-to-all-start.1 = ((bf16[16,4,24,2176]{3,2,1,0:T(8,128)(2,1)}), bf16[16,4,24,2176]{3,2,1,0:T(8,128)(2,1)}, u32[]{:S(2)}, u32[]{:S(2)}) async-start(bf16[16,4,24,2176]{3,2,1,0:T(8,128)(2,1)} %get-tuple-element.92), calls=%async_computation.1 | async-start | bytes 13369344 | tf_op jit(solution)/shard_map/cond/branch_1_fun/all_to_all | solution.py:277
  354.8 83.3 %all-to-all-start.3 = ((bf16[16,4,8,2176]{3,2,1,0:T(8,128)(2,1)}), bf16[16,4,8,2176]{3,2,1,0:T(8,128)(2,1)S(1)}, u32[]{:S(2)}, u32[]{:S(2)}) async-start(bf16[16,4,8,2176]{3,2,1,0:T(8,128)(2,1)} %get-tuple-element.98), calls=%async_computation.3 | async-start | bytes 4456448 | tf_op jit(solution)/shard_map/cond/branch_1_fun/all_to_all | solution.py:277
  408.6 25.7 %collective-permute-start.2 = (bf16[2,4,256,256]{3,2,1,0:T(8,128)(2,1)}, bf16[2,4,256,256]{3,2,1,0:T(8,128)(2,1)}, u32[]{:S(2)}, u32[]{:S(2)}) collective-permute-start(bf16[2,4,256,256]{3,2,1,0:T(8,128)(2,1)} %branch_1_fun.26), channel_id=1, source_target_pairs={{0,1},{1,0},{2,3},{3,2},{4,5},{5,4},{6,7},{7,6},{8,9},{9,8},{10,11... | collective-permute-start | bytes 3145736 | tf_op jit(solution)/shard_map/cond/branch_1_fun/ppermute | solution.py:397
  438.0 14.1 %copy-start.7 = (bf16[16,4,8,2176]{3,2,1,0:T(8,128)(2,1)}, bf16[16,4,8,2176]{3,2,1,0:T(8,128)(2,1)S(1)}, u32[]{:S(2)}) copy-start(bf16[16,4,8,2176]{3,2,1,0:T(8,128)(2,1)S(1)} %all-to-all-done.3.in_ref) | copy-start | bytes 6684676 | tf_op jit(solution)/shard_map/cond
  438.0 31.2 %all-to-all-start.4 = ((bf16[16,2,4,16,256]{4,3,2,1,0:T(8,128)(2,1)}), bf16[16,2,4,16,256]{4,3,2,1,0:T(8,128)(2,1)}, u32[]{:S(2)}, u32[]{:S(2)}) async-start(bf16[16,2,4,16,256]{4,3,2,1,0:T(8,128)(2,1)} %bitcast.194), calls=%async_computation.4 | async-start | bytes 2097152 | tf_op jit(solution)/shard_map/cond/branch_1_fun/all_to_all | solution.py:277
  443.8 25.4 %collective-permute-start.1 = (bf16[2,2,256,256]{3,2,1,0:T(8,128)(2,1)}, bf16[2,2,256,256]{3,2,1,0:T(8,128)(2,1)}, u32[]{:S(2)}, u32[]{:S(2)}) collective-permute-start(bf16[2,2,256,256]{3,2,1,0:T(8,128)(2,1)} %branch_1_fun.25), channel_id=1, source_target_pairs={{0,1},{1,0},{2,3},{3,2},{4,5},{5,4},{6,7},{7,6},{8,9},{9,8},{10,11... | collective-permute-start | bytes 1572872 | tf_op jit(solution)/shard_map/cond/branch_1_fun/ppermute | solution.py:397
  445.2 6.9 %copy-start.12 = (s32[256,256]{1,0:T(8,128)S(1)}, s32[256,256]{1,0:T(8,128)}, u32[]{:S(2)}) copy-start(s32[256,256]{1,0:T(8,128)} %get-tuple-element.81.place_ref) | copy-start | bytes 786436 | tf_op jit(solution)/shard_map/cond
  462.5 6.8 %copy-start.14 = (f32[2,2,256,256]{3,2,1,0:T(8,128)S(1)}, f32[2,2,256,256]{3,2,1,0:T(8,128)}, u32[]{:S(2)}) copy-start(f32[2,2,256,256]{3,2,1,0:T(8,128)} %branch_1_fun.28) | copy-start | bytes 3145732 | tf_op jit(solution)/shard_map/cond
  469.2 8.2 %copy-start.20 = (bf16[2,2,256,256]{3,2,1,0:T(8,128)(2,1)S(1)}, bf16[2,2,256,256]{3,2,1,0:T(8,128)(2,1)}, u32[]{:S(2)}) copy-start(bf16[2,2,256,256]{3,2,1,0:T(8,128)(2,1)} %branch_1_fun.30) | copy-start | bytes 1572868 | tf_op jit(solution)/shard_map/cond
  471.6 20.7 %all-to-all-start.5 = ((bf16[16,2,2,16,256]{4,3,2,1,0:T(8,128)(2,1)}), bf16[16,2,2,16,256]{4,3,2,1,0:T(8,128)(2,1)S(1)}, u32[]{:S(2)}, u32[]{:S(2)}) async-start(bf16[16,2,2,16,256]{4,3,2,1,0:T(8,128)(2,1)} %bitcast.165), calls=%async_computation.5 | async-start | bytes 1048576 | tf_op jit(solution)/shard_map/cond/branch_1_fun/all_to_all | solution.py:277
  477.5 14.8 %collective-permute-start.4 = (bf16[2,2,256,256]{3,2,1,0:T(8,128)(2,1)S(1)}, bf16[2,2,256,256]{3,2,1,0:T(8,128)(2,1)S(1)}, u32[]{:S(2)}, u32[]{:S(2)}) collective-permute-start(bf16[2,2,256,256]{3,2,1,0:T(8,128)(2,1)S(1)} %copy-done.20), channel_id=1, source_target_pairs={{0,1},{1,0},{2,3},{3,2},{4,5},{5,4},{6,7},{7,6},{8,9},{9,8},{10,11... | collective-permute-start | bytes 1572872 | tf_op jit(solution)/shard_map/cond/branch_1_fun/ppermute | solution.py:397
  480.3 22.8 %collective-permute-start.3 = (bf16[8,2,4,16,256]{4,3,2,1,0:T(8,128)(2,1)}, bf16[8,2,4,16,256]{4,3,2,1,0:T(8,128)(2,1)}, u32[]{:S(2)}, u32[]{:S(2)}) collective-permute-start(bf16[8,2,4,16,256]{4,3,2,1,0:T(8,128)(2,1)} %get-tuple-element.159), channel_id=1, source_target_pairs={{0,1},{1,0},{2,3},{3,2},{4,5},{5,4},{6,7},{7,6},{8,9},{9,8},{10,11... | collective-permute-start | bytes 1572872 | tf_op jit(solution)/shard_map/cond/branch_1_fun/ppermute | solution.py:422
  494.7 20.5 %all-to-all-start.6 = ((bf16[16,2,2,16,256]{4,3,2,1,0:T(8,128)(2,1)}), bf16[16,2,2,16,256]{4,3,2,1,0:T(8,128)(2,1)S(1)}, u32[]{:S(2)}, u32[]{:S(2)}) async-start(bf16[16,2,2,16,256]{4,3,2,1,0:T(8,128)(2,1)} %bitcast.164), calls=%async_computation.6 | async-start | bytes 1048576 | tf_op jit(solution)/shard_map/cond/branch_1_fun/all_to_all | solution.py:277
  504.3 11.8 %collective-permute-start.5 = (bf16[8,2,2,16,256]{4,3,2,1,0:T(8,128)(2,1)S(1)}, bf16[8,2,2,16,256]{4,3,2,1,0:T(8,128)(2,1)S(1)}, u32[]{:S(2)}, u32[]{:S(2)}) collective-permute-start(bf16[8,2,2,16,256]{4,3,2,1,0:T(8,128)(2,1)S(1)} %get-tuple-element.161), channel_id=1, source_target_pairs={{0,1},{1,0},{2,3},{3,2},{4,5},{5,4},{6,7},{7,6},{8,9},{9,8},{10,11... | collective-permute-start | bytes 786440 | tf_op jit(solution)/shard_map/cond/branch_1_fun/ppermute | solution.py:422
  515.3 8.3 %collective-permute-start.6 = (bf16[8,2,2,16,256]{4,3,2,0,1:T(8,128)(2,1)S(1)}, bf16[8,2,2,16,256]{4,3,2,0,1:T(8,128)(2,1)S(1)}, u32[]{:S(2)}, u32[]{:S(2)}) collective-permute-start(bf16[8,2,2,16,256]{4,3,2,0,1:T(8,128)(2,1)S(1)} %copy.79), channel_id=1, source_target_pairs={{0,1},{1,0},{2,3},{3,2},{4,5},{5,4},{6,7},{7,6},{8,9},{9,8},{10,11... | collective-permute-start | bytes 786440 | tf_op jit(solution)/shard_map/cond/branch_1_fun/ppermute | solution.py:422
  (2 other events, 2.7 us)

commit v6 on v5

--- a/solution.py
+++ b/solution.py
@@ -12,7 +12,7 @@
 F32 = jnp.float32
 BF16 = jnp.bfloat16
 VMEM = 56 * 1024 * 1024
-STEP = 2
+STEP = 4
 
 
 def tables(length):

time: 529 us -> 540 us (1.021)
  loops' own time: 0.81 us -> 7.07 us
    another operation x1, loops' own time: 0.81 us -> 7.07 us  [body(): return lax.cond(fits, send_sampled, send_all)]
  transfers between devices with their start and end apart: 14 -> 14, of which waited for: 8 -> 8; matrix products, arithmetic and copies ran while one was open for 3% -> 3% of each run, Pallas kernels for 46% -> 45%
where the time goes in v6:
time: 540 us; the launch traced here: 531 us
  Pallas kernels  255 us (47%)
  waiting for transfers between devices  145 us (27%)
  starting transfers between devices  98.7 us (18%)
  local copies, waits for them, and re-layouts  17.3 us (3%)
  other arithmetic  7.46 us (1%)
  loops' own time  7.07 us (1%)
    all_to_all x7, waiting for transfers between devices, exchange(): return lax.all_to_all(sent, 'cuts', split_axis=0, concat_axis=0, tiled=True)  108 us
    all_to_all x7, starting transfers between devices, exchange(): return lax.all_to_all(sent, 'cuts', split_axis=0, concat_axis=0, tiled=True)  90.8 us
    pallas_call x8, Pallas kernels, backward(): pl.pallas_call(functools.partial(backward_kernel, first), grid_spec=spec,...  85.8 us
    pallas_call x3, Pallas kernels, compact(): pl.pallas_call(functools.partial(compact_kernel, len(pieces)), grid=(coil...  71.1 us
    pallas_call x1, Pallas kernels, forward(): pl.pallas_call(forward_kernel, grid=(deep // group, coils), in_specs=[pl....  50 us
    pallas_call x4, Pallas kernels, expand(): pl.pallas_call(functools.partial(expand_kernel, slab), grid=(parts // sla...  45.8 us
    ppermute x1, waiting for transfers between devices, gather(): lax.ppermute(volume, 'coil', [(i, (i + s) % coil_groups) for i in range(c...  16.5 us
    ppermute x3, waiting for transfers between devices, send(): lax.ppermute(term, 'coil', ring)  10.8 us
  transfers between devices with their start and end apart: 14, of which 8 were waited for; matrix products, arithmetic and copies ran while one was open for 3% of the time, Pallas kernels for 45%

profile of v6, /device:TPU:0, one launch (start us, length us, event | category | flops | bytes accessed | tf_op | source)
XLA Modules:
  0.0 531.2 jit_solution(6153142972565152454)
XLA Ops:
  2.8 526.8 %conditional.1 = (bf16[2,128,16,256]{3,2,1,0:T(8,128)(2,1)S(1)}) conditional(s32[]{:T(128)} %bitcast.102, (s32[]{:T(128)}, bf16[8,2,256,16,256]{4,3,2,1,0:T(8,128)(2,1)}, bf16[512,512]{1,0:T(8,128)(2,1)}, bf16[2,16,128,256]{3,2,1,0:T(8,128)(2,1)}, bf16[8,2,16,256,256]{4,3,2,1,0:T(8,128)(2,1)}, /*index=5*/bf16[512,512]{1,0:T(8,128)(2,1)}, ...), branch_computations={%region_0.1_spmd, %region_1.2_spmd} | conditional | flops 95573508096 | bytes 804258688 | solution.py:375
  11.6 11.5 %branch_1_fun.19 = bf16[16,1,32,2176]{3,2,1,0:T(8,128)(2,1)} custom-call(bf16[8,2,256,16,256]{4,3,2,1,0:T(8,128)(2,1)} %get-tuple-element.80.k_ref, bf16[16,256,256]{2,1,0:T(8,128)(2,1)} %fusion.3.s_ref, bf16[512,512]{1,0:T(8,128)(2,1)} %get-tuple-element.90.t_ref), custom_call_target="tpu_custom_call" | custom-call | flops 2281701376 | bytes 6422528 | tf_op jit(solution)/shard_map/cond/branch_1_fun/pallas_call | solution.py:112
  23.1 7.4 %all-to-all-start = ((bf16[16,1,32,2176]{3,2,1,0:T(8,128)(2,1)}), bf16[16,1,32,2176]{3,2,1,0:T(8,128)(2,1)S(1)}, u32[]{:S(2)}, u32[]{:S(2)}) async-start(bf16[16,1,32,2176]{3,2,1,0:T(8,128)(2,1)} %branch_1_fun.19), calls=%async_computation | async-start | bytes 4456448 | tf_op jit(solution)/shard_map/cond/branch_1_fun/all_to_all | solution.py:277
  36.2 26.0 %branch_1_fun.16 = bf16[16,3,32,2176]{3,2,1,0:T(8,128)(2,1)} custom-call(bf16[8,2,256,16,256]{4,3,2,1,0:T(8,128)(2,1)} %get-tuple-element.80.k_ref, bf16[16,256,256]{2,1,0:T(8,128)(2,1)} %fusion.3.s_ref, bf16[512,512]{1,0:T(8,128)(2,1)S(1)} %copy-done.16), custom_call_target="tpu_custom_call" | custom-call | flops 6845104128 | bytes 19267584 | tf_op jit(solution)/shard_map/cond/branch_1_fun/pallas_call | solution.py:112
  62.3 16.5 %collective-permute-done = bf16[2,16,128,256]{3,2,1,0:T(8,128)(2,1)} collective-permute-done((bf16[2,16,128,256]{3,2,1,0:T(8,128)(2,1)}, bf16[2,16,128,256]{3,2,1,0:T(8,128)(2,1)}, u32[]{:S(2)}, u32[]{:S(2)}) %collective-permute-start) | collective-permute-done | bytes 2097184 | tf_op jit(solution)/shard_map/cond/branch_1_fun/ppermute | solution.py:286
  89.3 33.6 %branch_1_fun.18 = (bf16[16,4,24,2176]{3,2,1,0:T(8,128)(2,1)}, bf16[16,4,8,2176]{3,2,1,0:T(8,128)(2,1)}) custom-call(bf16[8,2,256,16,256]{4,3,2,1,0:T(8,128)(2,1)} %get-tuple-element.80.k_ref, bf16[16,256,256]{2,1,0:T(8,128)(2,1)} %fusion.3.s_ref, bf16[512,512]{1,0:T(8,128)(2,1)} %get-tuple-element.88.t_ref), custom_call_target="tpu_custom_call" | custom-call | flops 9126805504 | bytes 25690112 | tf_op jit(solution)/shard_map/cond/branch_1_fun/pallas_call | solution.py:112
  122.9 50.0 %branch_1_fun.17.refs_1_ = bf16[8,16,512,256]{3,2,1,0:T(8,128)(2,1)} custom-call(bf16[8,2,16,256,256]{4,3,2,1,0:T(8,128)(2,1)} %get-tuple-element.79.maps_ref.refs_0_, bf16[2,16,256,256]{3,2,1,0:T(8,128)(2,1)} %constant_dynamic-update-slice_fusion.2.vol_ref, bf16[512,512]{1,0:T(8,128)(2,1)S(1)} %copy-done.3, bf16[512,512]{1,0:T(8,128)(2,1)S(1)} %copy-done.1), custom_call_target="tpu_custom_call" | custom-call | flops 34359738368 | bytes 67108864 | tf_op jit(solution)/shard_map/cond/branch_1_fun/pallas_call | solution.py:183
  172.9 9.9 %branch_1_fun.20 = bf16[32,256,256]{2,1,0:T(8,128)(2,1)} custom-call(s32[256,256]{1,0:T(8,128)S(1)} %copy-done.11, bf16[16,1,32,2176]{3,2,1,0:T(8,128)(2,1)} %copy-done.8), custom_call_target="tpu_custom_call" | custom-call | flops 1073741824 | bytes 6422528 | tf_op jit(solution)/shard_map/cond/branch_1_fun/pallas_call | solution.py:149
  182.8 10.6 %branch_1_fun.21.refs_6_ = f32[2,16,256,256]{3,2,1,0:T(8,128)} custom-call(s32[1]{0:T(128)} %constant.241.clone.at_ref, bf16[8,2,16,256,256]{4,3,2,1,0:T(8,128)(2,1)} %get-tuple-element.79.maps_ref.refs_0_, bf16[8,16,512,256]{3,2,1,0:T(8,128)(2,1)} %branch_1_fun.17.refs_1_, bf16[1,2,16,256,256]{4,3,2,1,0:T(8,128)(2,1)} %bitcast.186, ...), custom_call_target="tpu_custom_call" | custom-call | flops 4294967296 | bytes 29360128 | tf_op jit(solution)/shard_map/cond/branch_1_fun/pallas_call | solution.py:267
  193.4 16.9 %all-to-all-done.2.in_ref = bf16[16,3,32,2176]{3,2,1,0:T(8,128)(2,1)} async-done(((bf16[16,3,32,2176]{3,2,1,0:T(8,128)(2,1)}), bf16[16,3,32,2176]{3,2,1,0:T(8,128)(2,1)}, u32[]{:S(2)}, u32[]{:S(2)}) %all-to-all-start.2) | async-done | bytes 6684704 | tf_op jit(solution)/shard_map/cond/branch_1_fun/all_to_all | solution.py:277
  210.3 29.7 %all-to-all-start.1 = ((bf16[16,4,24,2176]{3,2,1,0:T(8,128)(2,1)}), bf16[16,4,24,2176]{3,2,1,0:T(8,128)(2,1)}, u32[]{:S(2)}, u32[]{:S(2)}) async-start(bf16[16,4,24,2176]{3,2,1,0:T(8,128)(2,1)} %get-tuple-element.92), calls=%async_computation.1 | async-start | bytes 13369344 | tf_op jit(solution)/shard_map/cond/branch_1_fun/all_to_all | solution.py:277
  240.0 13.0 %branch_1_fun.23 = bf16[96,256,256]{2,1,0:T(8,128)(2,1)} custom-call(s32[256,256]{1,0:T(8,128)S(1)} %copy-done.11, bf16[16,3,32,2176]{3,2,1,0:T(8,128)(2,1)} %all-to-all-done.2.in_ref), custom_call_target="tpu_custom_call" | custom-call | flops 3221225472 | bytes 19267584 | tf_op jit(solution)/shard_map/cond/branch_1_fun/pallas_call | solution.py:149
  253.1 27.0 %branch_1_fun.24.refs_6_ = f32[2,16,256,256]{3,2,1,0:T(8,128)} custom-call(s32[1]{0:T(128)} %constant.241.clone.at_ref, bf16[8,2,16,256,256]{4,3,2,1,0:T(8,128)(2,1)} %get-tuple-element.79.maps_ref.refs_0_, bf16[8,16,512,256]{3,2,1,0:T(8,128)(2,1)} %branch_1_fun.17.refs_1_, bf16[3,2,16,256,256]{4,3,2,1,0:T(8,128)(2,1)} %bitcast.180, ...), custom_call_target="tpu_custom_call" | custom-call | flops 12884901888 | bytes 54525952 | tf_op jit(solution)/shard_map/cond/branch_1_fun/pallas_call | solution.py:267
  280.1 81.0 %all-to-all-done.1.in_ref = bf16[16,4,24,2176]{3,2,1,0:T(8,128)(2,1)} async-done(((bf16[16,4,24,2176]{3,2,1,0:T(8,128)(2,1)}), bf16[16,4,24,2176]{3,2,1,0:T(8,128)(2,1)}, u32[]{:S(2)}, u32[]{:S(2)}) %all-to-all-start.1) | async-done | bytes 6684704 | tf_op jit(solution)/shard_map/cond/branch_1_fun/all_to_all | solution.py:277
  361.0 29.6 %all-to-all-start.3 = ((bf16[16,4,8,2176]{3,2,1,0:T(8,128)(2,1)}), bf16[16,4,8,2176]{3,2,1,0:T(8,128)(2,1)S(1)}, u32[]{:S(2)}, u32[]{:S(2)}) async-start(bf16[16,4,8,2176]{3,2,1,0:T(8,128)(2,1)} %get-tuple-element.98), calls=%async_computation.3 | async-start | bytes 4456448 | tf_op jit(solution)/shard_map/cond/branch_1_fun/all_to_all | solution.py:277
  390.7 13.1 %branch_1_fun.22 = bf16[96,256,256]{2,1,0:T(8,128)(2,1)} custom-call(s32[256,256]{1,0:T(8,128)} %get-tuple-element.81.place_ref, bf16[16,4,24,2176]{3,2,1,0:T(8,128)(2,1)} %all-to-all-done.1.in_ref), custom_call_target="tpu_custom_call" | custom-call | flops 3221225472 | bytes 19267584 | tf_op jit(solution)/shard_map/cond/branch_1_fun/pallas_call | solution.py:149
  403.8 10.2 %branch_1_fun.26 = bf16[2,4,256,256]{3,2,1,0:T(8,128)(2,1)} custom-call(s32[1]{0:T(128)} %bitcast.66.at_ref, bf16[8,2,16,256,256]{4,3,2,1,0:T(8,128)(2,1)} %get-tuple-element.79.maps_ref.refs_0_, bf16[8,16,512,256]{3,2,1,0:T(8,128)(2,1)} %branch_1_fun.17.refs_1_, bf16[4,2,12,256,256]{4,3,2,1,0:T(8,128)(2,1)} %bitcast.173, s32[256,256]{1,0:T(8,128)S(1)} %copy-done.5, ...), custom_call_target="tpu_custom_call" | custom-call | flops 4294967296 | bytes 16777216 | tf_op jit(solution)/shard_map/cond/branch_1_fun/pallas_call | solution.py:267
  422.1 10.6 %branch_1_fun.27 = f32[2,4,256,256]{3,2,1,0:T(8,128)} custom-call(s32[1]{0:T(128)} %bitcast.65.at_ref, bf16[8,2,16,256,256]{4,3,2,1,0:T(8,128)(2,1)} %get-tuple-element.79.maps_ref.refs_0_, bf16[8,16,512,256]{3,2,1,0:T(8,128)(2,1)} %branch_1_fun.17.refs_1_, bf16[4,2,12,256,256]{4,3,2,1,0:T(8,128)(2,1)} %bitcast.175, s32[256,256]{1,0:T(8,128)S(1)} %copy-done.5, ...), custom_call_target="tpu_custom_call" | custom-call | flops 4294967296 | bytes 16777216 | tf_op jit(solution)/shard_map/cond/branch_1_fun/pallas_call | solution.py:267
  432.7 7.1 %collective-permute-done.2 = bf16[2,4,256,256]{3,2,1,0:T(8,128)(2,1)} collective-permute-done((bf16[2,4,256,256]{3,2,1,0:T(8,128)(2,1)}, bf16[2,4,256,256]{3,2,1,0:T(8,128)(2,1)}, u32[]{:S(2)}, u32[]{:S(2)}) %collective-permute-start.2) | collective-permute-done | bytes 1048608 | tf_op jit(solution)/shard_map/cond/branch_1_fun/ppermute | solution.py:397
  450.9 6.9 %branch_1_fun.28 = f32[2,2,256,256]{3,2,1,0:T(8,128)} custom-call(s32[1]{0:T(128)} %bitcast.77.at_ref, bf16[8,2,16,256,256]{4,3,2,1,0:T(8,128)(2,1)} %get-tuple-element.79.maps_ref.refs_0_, bf16[8,16,512,256]{3,2,1,0:T(8,128)(2,1)} %branch_1_fun.17.refs_1_, bf16[4,2,12,256,256]{4,3,2,1,0:T(8,128)(2,1)} %bitcast.176, s32[256,256]{1,0:T(8,128)S(1)} %copy-done.5, ...), custom_call_target="tpu_custom_call" | custom-call | flops 2147483648 | bytes 8388608 | tf_op jit(solution)/shard_map/cond/branch_1_fun/pallas_call | solution.py:267
  457.9 9.8 %branch_1_fun.29 = bf16[32,256,256]{2,1,0:T(8,128)(2,1)} custom-call(s32[256,256]{1,0:T(8,128)S(1)} %copy-done.12, bf16[16,4,8,2176]{3,2,1,0:T(8,128)(2,1)} %copy-done.7), custom_call_target="tpu_custom_call" | custom-call | flops 1073741824 | bytes 6422528 | tf_op jit(solution)/shard_map/cond/branch_1_fun/pallas_call | solution.py:149
  487.1 6.9 %branch_1_fun.31 = f32[2,2,256,256]{3,2,1,0:T(8,128)} custom-call(s32[1]{0:T(128)} %bitcast.90.at_ref, bf16[8,2,16,256,256]{4,3,2,1,0:T(8,128)(2,1)} %get-tuple-element.79.maps_ref.refs_0_, bf16[8,16,512,256]{3,2,1,0:T(8,128)(2,1)} %branch_1_fun.17.refs_1_, bf16[4,2,4,256,256]{4,3,2,1,0:T(8,128)(2,1)} %bitcast.184, s32[256,256]{1,0:T(8,128)S(1)} %copy-done.5, ...), custom_call_target="tpu_custom_call" | custom-call | flops 2147483648 | bytes 8388608 | tf_op jit(solution)/shard_map/cond/branch_1_fun/pallas_call | solution.py:267
  510.6 10.1 %all-to-all-done.6 = bf16[16,2,2,16,256]{4,3,2,1,0:T(8,128)(2,1)S(1)} async-done(((bf16[16,2,2,16,256]{4,3,2,1,0:T(8,128)(2,1)}), bf16[16,2,2,16,256]{4,3,2,1,0:T(8,128)(2,1)S(1)}, u32[]{:S(2)}, u32[]{:S(2)}) %all-to-all-start.6) | async-done | bytes 524320 | tf_op jit(solution)/shard_map/cond/branch_1_fun/all_to_all | solution.py:277
  521.6 7.4 %collective-permute-done.6 = bf16[8,2,2,16,256]{4,3,2,0,1:T(8,128)(2,1)S(1)} collective-permute-done((bf16[8,2,2,16,256]{4,3,2,0,1:T(8,128)(2,1)S(1)}, bf16[8,2,2,16,256]{4,3,2,0,1:T(8,128)(2,1)S(1)}, u32[]{:S(2)}, u32[]{:S(2)}) %collective-permute-start.6) | collective-permute-done | bytes 262176 | tf_op jit(solution)/shard_map/cond/branch_1_fun/ppermute | solution.py:422
  (71 shorter events, 78.2 us)
Async XLA Ops:
  23.1 58.9 %all-to-all-start = ((bf16[16,1,32,2176]{3,2,1,0:T(8,128)(2,1)}), bf16[16,1,32,2176]{3,2,1,0:T(8,128)(2,1)S(1)}, u32[]{:S(2)}, u32[]{:S(2)}) async-start(bf16[16,1,32,2176]{3,2,1,0:T(8,128)(2,1)} %branch_1_fun.19), calls=%async_computation | async-start | bytes 4456448 | tf_op jit(solution)/shard_map/cond/branch_1_fun/all_to_all | solution.py:277
  30.5 48.3 %collective-permute-start = (bf16[2,16,128,256]{3,2,1,0:T(8,128)(2,1)}, bf16[2,16,128,256]{3,2,1,0:T(8,128)(2,1)}, u32[]{:S(2)}, u32[]{:S(2)}) collective-permute-start(bf16[2,16,128,256]{3,2,1,0:T(8,128)(2,1)} %get-tuple-element.84), channel_id=1, source_target_pairs={{0,1},{1,0},{2,3},{3,2},{4,5},{5,4},{6,7},{7,6},{8,9},{9,8},{10,11... | collective-permute-start | bytes 6291464 | tf_op jit(solution)/shard_map/cond/branch_1_fun/ppermute | solution.py:286
  32.1 2.6 copy-start.10
  32.1 4.1 copy-start.16
  83.5 126.8 %all-to-all-start.2 = ((bf16[16,3,32,2176]{3,2,1,0:T(8,128)(2,1)}), bf16[16,3,32,2176]{3,2,1,0:T(8,128)(2,1)}, u32[]{:S(2)}, u32[]{:S(2)}) async-start(bf16[16,3,32,2176]{3,2,1,0:T(8,128)(2,1)} %branch_1_fun.16), calls=%async_computation.2 | async-start | bytes 13369344 | tf_op jit(solution)/shard_map/cond/branch_1_fun/all_to_all | solution.py:277
  89.3 33.6 %copy-start.1 = (bf16[512,512]{1,0:T(8,128)(2,1)S(1)}, bf16[512,512]{1,0:T(8,128)(2,1)}, u32[]{:S(2)}) copy-start(bf16[512,512]{1,0:T(8,128)(2,1)} %get-tuple-element.87.left_ref.refs_5_) | copy-start | bytes 1572868 | tf_op jit(solution)/shard_map/cond
  89.3 33.6 %copy-start.3 = (bf16[512,512]{1,0:T(8,128)(2,1)S(1)}, bf16[512,512]{1,0:T(8,128)(2,1)}, u32[]{:S(2)}) copy-start(bf16[512,512]{1,0:T(8,128)(2,1)} %get-tuple-element.86.right_ref.refs_4_) | copy-start | bytes 1572868 | tf_op jit(solution)/shard_map/cond
  122.9 50.0 %copy-start.11 = (s32[256,256]{1,0:T(8,128)S(1)}, s32[256,256]{1,0:T(8,128)}, u32[]{:S(2)}) copy-start(s32[256,256]{1,0:T(8,128)} %get-tuple-element.81.place_ref) | copy-start | bytes 786436 | tf_op jit(solution)/shard_map/cond
  172.9 9.9 %copy-start.5 = (s32[256,256]{1,0:T(8,128)S(1)}, s32[256,256]{1,0:T(8,128)}, u32[]{:S(2)}) copy-start(s32[256,256]{1,0:T(8,128)} %get-tuple-element.91.refs_3_) | copy-start | bytes 786436 | tf_op jit(solution)/shard_map/cond
  210.3 150.7 %all-to-all-start.1 = ((bf16[16,4,24,2176]{3,2,1,0:T(8,128)(2,1)}), bf16[16,4,24,2176]{3,2,1,0:T(8,128)(2,1)}, u32[]{:S(2)}, u32[]{:S(2)}) async-start(bf16[16,4,24,2176]{3,2,1,0:T(8,128)(2,1)} %get-tuple-element.92), calls=%async_computation.1 | async-start | bytes 13369344 | tf_op jit(solution)/shard_map/cond/branch_1_fun/all_to_all | solution.py:277
  361.0 82.4 %all-to-all-start.3 = ((bf16[16,4,8,2176]{3,2,1,0:T(8,128)(2,1)}), bf16[16,4,8,2176]{3,2,1,0:T(8,128)(2,1)S(1)}, u32[]{:S(2)}, u32[]{:S(2)}) async-start(bf16[16,4,8,2176]{3,2,1,0:T(8,128)(2,1)} %get-tuple-element.98), calls=%async_computation.3 | async-start | bytes 4456448 | tf_op jit(solution)/shard_map/cond/branch_1_fun/all_to_all | solution.py:277
  414.0 25.8 %collective-permute-start.2 = (bf16[2,4,256,256]{3,2,1,0:T(8,128)(2,1)}, bf16[2,4,256,256]{3,2,1,0:T(8,128)(2,1)}, u32[]{:S(2)}, u32[]{:S(2)}) collective-permute-start(bf16[2,4,256,256]{3,2,1,0:T(8,128)(2,1)} %branch_1_fun.26), channel_id=1, source_target_pairs={{0,1},{1,0},{2,3},{3,2},{4,5},{5,4},{6,7},{7,6},{8,9},{9,8},{10,11... | collective-permute-start | bytes 3145736 | tf_op jit(solution)/shard_map/cond/branch_1_fun/ppermute | solution.py:397
  443.5 14.4 %copy-start.7 = (bf16[16,4,8,2176]{3,2,1,0:T(8,128)(2,1)}, bf16[16,4,8,2176]{3,2,1,0:T(8,128)(2,1)S(1)}, u32[]{:S(2)}) copy-start(bf16[16,4,8,2176]{3,2,1,0:T(8,128)(2,1)S(1)} %all-to-all-done.3.in_ref) | copy-start | bytes 6684676 | tf_op jit(solution)/shard_map/cond
  443.5 31.0 %all-to-all-start.4 = ((bf16[16,2,4,16,256]{4,3,2,1,0:T(8,128)(2,1)}), bf16[16,2,4,16,256]{4,3,2,1,0:T(8,128)(2,1)}, u32[]{:S(2)}, u32[]{:S(2)}) async-start(bf16[16,2,4,16,256]{4,3,2,1,0:T(8,128)(2,1)} %bitcast.194), calls=%async_computation.4 | async-start | bytes 2097152 | tf_op jit(solution)/shard_map/cond/branch_1_fun/all_to_all | solution.py:277
  449.5 24.9 %collective-permute-start.1 = (bf16[2,2,256,256]{3,2,1,0:T(8,128)(2,1)}, bf16[2,2,256,256]{3,2,1,0:T(8,128)(2,1)}, u32[]{:S(2)}, u32[]{:S(2)}) collective-permute-start(bf16[2,2,256,256]{3,2,1,0:T(8,128)(2,1)} %branch_1_fun.25), channel_id=1, source_target_pairs={{0,1},{1,0},{2,3},{3,2},{4,5},{5,4},{6,7},{7,6},{8,9},{9,8},{10,11... | collective-permute-start | bytes 1572872 | tf_op jit(solution)/shard_map/cond/branch_1_fun/ppermute | solution.py:397
  450.9 6.9 %copy-start.12 = (s32[256,256]{1,0:T(8,128)S(1)}, s32[256,256]{1,0:T(8,128)}, u32[]{:S(2)}) copy-start(s32[256,256]{1,0:T(8,128)} %get-tuple-element.81.place_ref) | copy-start | bytes 786436 | tf_op jit(solution)/shard_map/cond
  467.7 6.8 %copy-start.14 = (f32[2,2,256,256]{3,2,1,0:T(8,128)S(1)}, f32[2,2,256,256]{3,2,1,0:T(8,128)}, u32[]{:S(2)}) copy-start(f32[2,2,256,256]{3,2,1,0:T(8,128)} %branch_1_fun.28) | copy-start | bytes 3145732 | tf_op jit(solution)/shard_map/cond
  474.5 8.5 %copy-start.20 = (bf16[2,2,256,256]{3,2,1,0:T(8,128)(2,1)S(1)}, bf16[2,2,256,256]{3,2,1,0:T(8,128)(2,1)}, u32[]{:S(2)}) copy-start(bf16[2,2,256,256]{3,2,1,0:T(8,128)(2,1)} %branch_1_fun.30) | copy-start | bytes 1572868 | tf_op jit(solution)/shard_map/cond
  476.8 20.9 %all-to-all-start.5 = ((bf16[16,2,2,16,256]{4,3,2,1,0:T(8,128)(2,1)}), bf16[16,2,2,16,256]{4,3,2,1,0:T(8,128)(2,1)S(1)}, u32[]{:S(2)}, u32[]{:S(2)}) async-start(bf16[16,2,2,16,256]{4,3,2,1,0:T(8,128)(2,1)} %bitcast.165), calls=%async_computation.5 | async-start | bytes 1048576 | tf_op jit(solution)/shard_map/cond/branch_1_fun/all_to_all | solution.py:277
  482.9 14.8 %collective-permute-start.4 = (bf16[2,2,256,256]{3,2,1,0:T(8,128)(2,1)S(1)}, bf16[2,2,256,256]{3,2,1,0:T(8,128)(2,1)S(1)}, u32[]{:S(2)}, u32[]{:S(2)}) collective-permute-start(bf16[2,2,256,256]{3,2,1,0:T(8,128)(2,1)S(1)} %copy-done.20), channel_id=1, source_target_pairs={{0,1},{1,0},{2,3},{3,2},{4,5},{5,4},{6,7},{7,6},{8,9},{9,8},{10,11... | collective-permute-start | bytes 1572872 | tf_op jit(solution)/shard_map/cond/branch_1_fun/ppermute | solution.py:397
  485.8 22.8 %collective-permute-start.3 = (bf16[8,2,4,16,256]{4,3,2,1,0:T(8,128)(2,1)}, bf16[8,2,4,16,256]{4,3,2,1,0:T(8,128)(2,1)}, u32[]{:S(2)}, u32[]{:S(2)}) collective-permute-start(bf16[8,2,4,16,256]{4,3,2,1,0:T(8,128)(2,1)} %get-tuple-element.159), channel_id=1, source_target_pairs={{0,1},{1,0},{2,3},{3,2},{4,5},{5,4},{6,7},{7,6},{8,9},{9,8},{10,11... | collective-permute-start | bytes 1572872 | tf_op jit(solution)/shard_map/cond/branch_1_fun/ppermute | solution.py:422
  500.1 20.5 %all-to-all-start.6 = ((bf16[16,2,2,16,256]{4,3,2,1,0:T(8,128)(2,1)}), bf16[16,2,2,16,256]{4,3,2,1,0:T(8,128)(2,1)S(1)}, u32[]{:S(2)}, u32[]{:S(2)}) async-start(bf16[16,2,2,16,256]{4,3,2,1,0:T(8,128)(2,1)} %bitcast.164), calls=%async_computation.6 | async-start | bytes 1048576 | tf_op jit(solution)/shard_map/cond/branch_1_fun/all_to_all | solution.py:277
  509.7 11.8 %collective-permute-start.5 = (bf16[8,2,2,16,256]{4,3,2,1,0:T(8,128)(2,1)S(1)}, bf16[8,2,2,16,256]{4,3,2,1,0:T(8,128)(2,1)S(1)}, u32[]{:S(2)}, u32[]{:S(2)}) collective-permute-start(bf16[8,2,2,16,256]{4,3,2,1,0:T(8,128)(2,1)S(1)} %get-tuple-element.161), channel_id=1, source_target_pairs={{0,1},{1,0},{2,3},{3,2},{4,5},{5,4},{6,7},{7,6},{8,9},{9,8},{10,11... | collective-permute-start | bytes 786440 | tf_op jit(solution)/shard_map/cond/branch_1_fun/ppermute | solution.py:422
  520.7 8.3 %collective-permute-start.6 = (bf16[8,2,2,16,256]{4,3,2,0,1:T(8,128)(2,1)S(1)}, bf16[8,2,2,16,256]{4,3,2,0,1:T(8,128)(2,1)S(1)}, u32[]{:S(2)}, u32[]{:S(2)}) collective-permute-start(bf16[8,2,2,16,256]{4,3,2,0,1:T(8,128)(2,1)S(1)} %copy.79), channel_id=1, source_target_pairs={{0,1},{1,0},{2,3},{3,2},{4,5},{5,4},{6,7},{7,6},{8,9},{9,8},{10,11... | collective-permute-start | bytes 786440 | tf_op jit(solution)/shard_map/cond/branch_1_fun/ppermute | solution.py:422
  (2 other events, 2.7 us)
